TPU v7x, 32 devices: a whole 2x2x4 slice. The times are simulated.
32 devices in a mesh: ctx: 8 (over y, x, core), tp: 4 (over z).
Axes of the slice: x: 2, y: 2, z: 4, core: 2. Of those that a mesh axis runs over, the one named last changes fastest.
Arguments:
- query_gate: bfloat16 [16, 524288], P('tp', 'ctx'), may hold values from -6 to 6
- key_branch: bfloat16 [16, 524288], P('tp', 'ctx'), may hold values from -6 to 6
- value_branch: bfloat16 [16, 524288], P('tp', 'ctx'), may hold values from -6 to 6
- long_filter: float32 [16, 524288], P('tp', 'ctx'), may hold values from -0.0078125 to 0.0078125
- skip_gain: float32 [16], P('tp'), may hold values from 0.5 to 1.5
- out_weight: bfloat16 [16, 16], replicated, may hold values from -1.5 to 1.5
Outputs:
- mixed: bfloat16 [16, 524288], P('tp', 'ctx')
All inputs are finite; a program needn't handle non-finite values.
Results may differ from a plain program's by a relative error of at most 0.02.
Values may be sent and summed in bfloat16 or wider, within the bound.
No kernel may reach another device: no remote copies, remote signals or barrier semaphores. Data moves between devices by JAX's collectives and lax.ppermute only.
A program may use at most 256 MiB of HBM per device.

v0:
```python
import math

import jax
import jax.numpy as jnp
from jax import lax
from jax.sharding import PartitionSpec as P

FACTOR = 128


def turn_table(left_idx, right_idx, length, sign):
    phase = left_idx[:, None] * right_idx[None, :] % length
    angle = sign * 2.0 * math.pi / length * phase.astype(jnp.float32)
    return (jnp.cos(angle), jnp.sin(angle))


def apply_form(form, table, values):
    return jnp.einsum(form, table, values, precision=lax.Precision.HIGHEST)


def apply_complex(form, tab_re, tab_im, val_re, val_im, table_first):
    if table_first:
        out_re = apply_form(form, tab_re, val_re) - apply_form(form, tab_im, val_im)
        out_im = apply_form(form, tab_re, val_im) + apply_form(form, tab_im, val_re)
    else:
        out_re = apply_form(form, val_re, tab_re) - apply_form(form, val_im, tab_im)
        out_im = apply_form(form, val_im, tab_re) + apply_form(form, val_re, tab_im)
    return (out_re, out_im)


def times_table(val_re, val_im, tab_re, tab_im):
    return (val_re * tab_re - val_im * tab_im, val_re * tab_im + val_im * tab_re)


def local_forward(val_re, val_im, width_a, width_b):
    iota_a = jnp.arange(width_a, dtype=jnp.int32)
    iota_b = jnp.arange(width_b, dtype=jnp.int32)
    fb_re, fb_im = turn_table(iota_b, iota_b, width_b, -1.0)
    step_re, step_im = apply_complex("cb,...ba->...ca", fb_re, fb_im, val_re, val_im, True)
    tw_re, tw_im = turn_table(iota_b, iota_a, width_a * width_b, -1.0)
    step_re, step_im = times_table(step_re, step_im, tw_re, tw_im)
    fa_re, fa_im = turn_table(iota_a, iota_a, width_a, -1.0)
    return apply_complex("...ca,ad->...cd", fa_re, fa_im, step_re, step_im, False)


def local_inverse(val_re, val_im, width_a, width_b):
    iota_a = jnp.arange(width_a, dtype=jnp.int32)
    iota_b = jnp.arange(width_b, dtype=jnp.int32)
    fa_re, fa_im = turn_table(iota_a, iota_a, width_a, 1.0)
    step_re, step_im = apply_complex("...cd,da->...ca", fa_re, fa_im, val_re, val_im, False)
    tw_re, tw_im = turn_table(iota_b, iota_a, width_a * width_b, 1.0)
    step_re, step_im = times_table(step_re, step_im, tw_re, tw_im)
    fb_re, fb_im = turn_table(iota_b, iota_b, width_b, 1.0)
    return apply_complex("bc,...ca->...ba", fb_re, fb_im, step_re, step_im, True)


def local(query_gate, key_branch, value_branch, long_filter, skip_gain, out_weight):
    ctx_count = lax.axis_size("ctx")
    ctx_index = lax.axis_index("ctx")
    chans, tok_count = query_gate.shape
    width_a = FACTOR
    width_b = tok_count // FACTOR
    residues = 2 * ctx_count
    fft_length = residues * tok_count
    signal = key_branch.astype(jnp.float32) * value_branch.astype(jnp.float32)
    stacked = jnp.concatenate([signal, long_filter], 0)[:, None, :]
    blocks = lax.all_to_all(
        stacked.astype(jnp.bfloat16), "ctx", split_axis=2, concat_axis=1, tiled=True
    ).astype(stacked.dtype)
    dev_idx = jnp.arange(ctx_count, dtype=jnp.int32)
    second_res = jnp.where(dev_idx == 0, ctx_count, residues - dev_idx)
    res_order = jnp.stack([dev_idx, second_res], 1).reshape(residues)
    blk_idx = jnp.arange(ctx_count, dtype=jnp.int32)
    cross_re, cross_im = turn_table(res_order, blk_idx, residues, -1.0)
    spec_re = apply_form("kn,snm->skm", cross_re, blocks)
    spec_im = apply_form("kn,snm->skm", cross_im, blocks)
    spec_re, spec_im = (
        lax.all_to_all(
            spec_re.astype(jnp.bfloat16), "ctx", split_axis=1, concat_axis=2, tiled=True
        ).astype(spec_re.dtype),
        lax.all_to_all(
            spec_im.astype(jnp.bfloat16), "ctx", split_axis=1, concat_axis=2, tiled=True
        ).astype(spec_im.dtype),
    )
    own_res = jnp.stack([ctx_index, jnp.where(ctx_index == 0, ctx_count, residues - ctx_index)])
    offsets = jnp.arange(tok_count, dtype=jnp.int32)
    tw_re, tw_im = turn_table(own_res, offsets, fft_length, -1.0)
    spec_re, spec_im = times_table(spec_re, spec_im, tw_re, tw_im)
    series = spec_re.shape[0]
    spec_re = spec_re.reshape(series, 2, width_b, width_a)
    spec_im = spec_im.reshape(series, 2, width_b, width_a)
    spec_re, spec_im = local_forward(spec_re, spec_im, width_a, width_b)
    sig_re, sig_im = (spec_re[:chans], spec_im[:chans])
    fil_re, fil_im = (spec_re[chans:], spec_im[chans:])
    prod_re, prod_im = times_table(sig_re, sig_im, fil_re, fil_im)
    back_re, back_im = local_inverse(prod_re, prod_im, width_a, width_b)
    back_re = back_re.reshape(chans, 2, tok_count)
    back_im = back_im.reshape(chans, 2, tok_count)
    inv_re, inv_im = turn_table(own_res, offsets, fft_length, 1.0)
    back_re, back_im = times_table(back_re, back_im, inv_re, inv_im)
    back_re = back_re * (1.0 / fft_length)
    back_im = back_im * (1.0 / fft_length)
    block_rows = jnp.arange(1 * lax.axis_size("ctx"), dtype=jnp.int32)
    row_re, row_im = turn_table(block_rows, own_res, residues, 1.0)
    conv = lax.psum_scatter(
        (
            apply_form("nj,cjm->ncm", row_re, back_re) - apply_form("nj,cjm->ncm", row_im, back_im)
        ).astype(jnp.bfloat16),
        "ctx",
        scatter_dimension=0,
        tiled=True,
    ).astype(jnp.float32)[0]
    gated = (query_gate.astype(jnp.float32) * (conv + skip_gain[:, None] * signal)).astype(
        jnp.bfloat16
    )
    tp_index = lax.axis_index("tp")
    out_dev = out_weight.shape[1] // lax.axis_size("tp")
    own_cols = lax.dynamic_slice_in_dim(out_weight, tp_index * out_dev, out_dev, 1)
    mixed = jnp.dot(
        own_cols.T,
        lax.all_gather(gated, "tp", axis=0, tiled=True),
        preferred_element_type=jnp.float32,
    )
    return mixed.astype(jnp.bfloat16)


def solution(mesh):
    placed = (P("tp", "ctx"), P("tp", "ctx"), P("tp", "ctx"), P("tp", "ctx"), P("tp"), P())
    return jax.shard_map(
        local, mesh=mesh, in_specs=placed, out_specs=P("tp", "ctx"), check_vma=False
    )
```

profile of v0, /device:TPU:0, one launch (start us, length us, event | category | flops | bytes accessed | tf_op | source)
XLA Modules:
  0.0 979.5 jit_solution(13282593383783644077)
XLA Ops:
  9.1 49.7 %copy.64 = bf16[8,1,65536]{0,1,2:T(2,128)(2,1)} copy(bf16[8,1,65536]{2,0,1:T(8,128)(2,1)S(1)} %pad_maximum_fusion) | data formatting | bytes 2097152 | tf_op jit(solution)/shard_map/concatenate | solution.py:66
  59.3 355.8 %reduce = bf16[65536,8]{1,0:T(8,128)(2,1)} reduce(bf16[65536,1,8]{2,1,0:T(2,128)(2,1)} %bitcast.149, bf16[]{:T(256)} %broadcast.423), dimensions={1}, to_apply=%bitcast.134.reduce_sub_computation | reduce | bytes 2097154
  415.2 20.5 %reshape.239 = bf16[8,2,32768]{2,1,0:T(2,128)(2,1)} reshape(bf16[65536,8]{1,0:T(8,128)(2,1)} %reduce) | data formatting | bytes 2097152
  441.5 15.2 %all-to-all-done = bf16[8,2,32768]{2,1,0:T(2,128)(2,1)S(1)} async-done(((bf16[8,2,32768]{2,1,0:T(2,128)(2,1)}), bf16[8,2,32768]{2,1,0:T(2,128)(2,1)S(1)}, u32[]{:S(2)}, u32[]{:S(2)}) %all-to-all-start) | async-done | bytes 1048608 | tf_op jit(solution)/shard_map/all_to_all | solution.py:67
  456.7 39.9 %reshape.240 = bf16[65536,1,8]{2,1,0:T(2,128)(2,1)} reshape(bf16[8,2,32768]{2,1,0:T(2,128)(2,1)S(1)} %all-to-all-done) | data formatting | bytes 2097152
  496.5 58.6 %copy.65 = bf16[8,1,65536]{2,0,1:T(8,128)(2,1)S(1)} copy(bf16[8,1,65536]{0,1,2:T(2,128)(2,1)} %bitcast.150) | data formatting | bytes 2097152 | tf_op jit(solution)/shard_map/all_to_all | solution.py:67
  568.0 21.9 %all-to-all-done.2 = bf16[8,16,8192]{2,0,1:T(8,128)(2,1)S(1)} async-done(((bf16[8,16,8192]{2,0,1:T(8,128)(2,1)}), bf16[8,16,8192]{2,0,1:T(8,128)(2,1)S(1)}, u32[]{:S(2)}, u32[]{:S(2)}) %all-to-all-start.2) | async-done | bytes 2097184 | tf_op jit(solution)/shard_map/all_to_all | solution.py:81
  595.6 9.0 fusion.77
  632.2 21.9 %fusion.34 = f32[8,2,128,512]{3,2,1,0:T(8,128)S(1)} fusion(f32[8,2,512,128]{3,2,1,0:T(8,128)} %reshape.220, f32[8,2,512,128]{3,2,1,0:T(8,128)} %reshape.219, f32[2,512,128]{2,1,0:T(8,128)S(1)} %get-tuple-element.8, f32[2,512,128]{2,1,0:T(8,128)S(1)} %get-tuple-element.7), kind=kOutput, calls=%fused_computation.61 | convolution fusion | flops 6449266688 | bytes 13631488 | tf_op jit(solution)/shard_map/cb,...ba->...ca/dot_general | solution.py:18
  654.1 18.0 %fusion.36 = f32[8,2,128,512]{3,2,1,0:T(8,128)S(1)} fusion(f32[8,2,512,128]{3,2,1,0:T(8,128)S(1)} %copy-done.1, f32[8,2,512,128]{3,2,1,0:T(8,128)S(1)} %copy-done.2, f32[2,512,128]{2,1,0:T(8,128)S(1)} %get-tuple-element.8, f32[2,512,128]{2,1,0:T(8,128)S(1)} %get-tuple-element.7), kind=kOutput, calls=%fused_computation.63 | convolution fusion | flops 6449266688 | bytes 13631488 | tf_op jit(solution)/shard_map/cb,...ba->...ca/dot_general | solution.py:18
  672.1 18.6 %convolution_add_fusion.1 = f32[8,2,128,512]{3,2,1,0:T(8,128)S(1)} fusion(f32[8,2,128,512]{3,2,1,0:T(8,128)S(1)} %fusion.34, f32[8,2,512,128]{3,2,1,0:T(8,128)S(1)} %copy-done.1, f32[8,2,512,128]{3,2,1,0:T(8,128)S(1)} %copy-done.2, f32[2,512,128]{2,1,0:T(8,128)S(1)} %get-tuple-element.8, f32[2,512,128]{2,1,0:T(8,128)S(1)} %get-tuple-element.7), kind=kOutput, calls=%fused_computation.19 | convolution fusion | flops 6450315264 | bytes 17825792 | tf_op jit(solution)/shard_map/cb,...ba->...ca/dot_general | solution.py:18
  690.6 18.1 %convolution_subtract_fusion.2 = f32[8,2,128,512]{3,2,1,0:T(8,128)S(1)} fusion(f32[8,2,128,512]{3,2,1,0:T(8,128)S(1)} %fusion.36, f32[8,2,512,128]{3,2,1,0:T(8,128)S(1)} %copy-done.1, f32[8,2,512,128]{3,2,1,0:T(8,128)S(1)} %copy-done.2, f32[2,512,128]{2,1,0:T(8,128)S(1)} %get-tuple-element.8, f32[2,512,128]{2,1,0:T(8,128)S(1)} %get-tuple-element.7), kind=kOutput, calls=%fused_computation.20 | convolution fusion | flops 6450315264 | bytes 17825792 | tf_op jit(solution)/shard_map/cb,...ba->...ca/dot_general | solution.py:18
  708.8 7.7 fusion.14
  716.5 7.9 fusion.18
  724.4 7.7 convolution_add_fusion
  732.1 7.9 convolution_subtract_fusion.1
  749.0 10.9 %fusion.28 = f32[4,2,128,512]{3,2,1,0:T(8,128)S(1)} fusion(f32[4,2,512,128]{3,2,1,0:T(8,128)S(1)} %convolution_add_fusion.2, f32[4,2,512,128]{3,2,1,0:T(8,128)S(1)} %convolution_subtract_fusion.3, f32[512,128]{1,0:T(8,128)S(1)} %copy.80, f32[512,128]{1,0:T(8,128)S(1)} %copy.79), kind=kOutput, calls=%fused_computation.55 | convolution fusion | flops 3226468352 | bytes 6815744 | tf_op jit(solution)/shard_map/bc,...ca->...ba/dot_general | solution.py:18
  759.9 11.8 %fusion.30 = f32[4,2,128,512]{3,2,1,0:T(8,128)} fusion(f32[4,2,512,128]{3,2,1,0:T(8,128)S(1)} %convolution_add_fusion.2, f32[4,2,512,128]{3,2,1,0:T(8,128)S(1)} %convolution_subtract_fusion.3, f32[512,128]{1,0:T(8,128)S(1)} %copy.80, f32[512,128]{1,0:T(8,128)S(1)} %copy.79), kind=kOutput, calls=%fused_computation.57 | convolution fusion | flops 3226468352 | bytes 6815744 | tf_op jit(solution)/shard_map/bc,...ca->...ba/dot_general | solution.py:18
  771.7 11.7 %add_bitcast_fusion = f32[4,2,512,128]{2,3,1,0:T(8,128)S(1)} fusion(f32[4,2,128,512]{3,2,1,0:T(8,128)S(1)} %fusion.28, f32[4,2,512,128]{3,2,1,0:T(8,128)S(1)} %convolution_add_fusion.2, f32[4,2,512,128]{3,2,1,0:T(8,128)S(1)} %convolution_subtract_fusion.3, f32[512,128]{1,0:T(8,128)S(1)} %copy.80, f32[512,128]{1,0:T(8,128)} %copy-done.7), kind=kOutput, calls=%fused_computation.29 | convolution fusion | flops 3226992640 | bytes 8912896 | tf_op jit(solution)/shard_map/bc,...ca->...ba/dot_general | solution.py:18
  788.4 14.7 %subtract_bitcast_fusion = f32[4,2,512,128]{2,3,1,0:T(8,128)} fusion(f32[4,2,128,512]{3,2,1,0:T(8,128)} %fusion.30, f32[4,2,512,128]{3,2,1,0:T(8,128)} %copy-done.4, f32[4,2,512,128]{3,2,1,0:T(8,128)} %copy-done.5, f32[512,128]{1,0:T(8,128)S(1)} %copy.80, f32[512,128]{1,0:T(8,128)} %copy-done.7), kind=kOutput, calls=%fused_computation.31 | convolution fusion | flops 3226992640 | bytes 8912896 | tf_op jit(solution)/shard_map/bc,...ca->...ba/dot_general | solution.py:18
  810.4 12.3 %fusion.9 = f32[8,4,65536]{2,0,1:T(8,128)S(1)} fusion(f32[4,2,65536]{2,1,0:T(2,128)S(1)} %reshape.218, f32[4,2,65536]{2,1,0:T(2,128)} %reshape.217, f32[2,65536]{1,0:T(2,128)S(1)} %get-tuple-element.10, f32[2,65536]{1,0:T(2,128)S(1)} %get-tuple-element.9, s32[2]{0:T(128)S(1)} %pad_add_fusion.1), kind=kOutput, calls=%fused_computation.25 | convolution fusion | flops 52429024 | bytes 13631496 | tf_op jit(solution)/shard_map/nj,cjm->ncm/dot_general | solution.py:18
  822.7 11.1 %fusion = bf16[8,4,65536]{2,0,1:T(8,128)(2,1)S(1)} fusion(f32[8,4,65536]{2,0,1:T(8,128)S(1)} %fusion.9, f32[4,2,65536]{2,1,0:T(2,128)S(1)} %reshape.218, f32[4,2,65536]{2,1,0:T(2,128)S(1)} %copy-done.3, f32[2,65536]{1,0:T(2,128)S(1)} %get-tuple-element.10, f32[2,65536]{1,0:T(2,128)S(1)} %get-tuple-element.9, s32[2]{0:T(128)S(1)} %pad_add_fusion.1), kind=kOutput, calls=%fused_computation.1 | convolution fusion | flops 56623328 | bytes 17825800 | tf_op jit(solution)/shard_map/nj,cjm->ncm/dot_general | solution.py:18
  840.2 79.4 %all-reduce.3.cloned.1.call-done = bf16[8,4,65536]{2,1,0:T(4,128)(2,1)} async-done(((bf16[8,4,65536]{2,1,0:T(4,128)(2,1)}), bf16[8,4,65536]{2,1,0:T(4,128)(2,1)}) %all-reduce.3.cloned.1.call-update) | async-done | bytes 4194320
  922.8 46.2 %all-gather.3.cloned.1.call-done = bf16[4,4,65536]{2,1,0:T(4,128)(2,1)} async-done(((bf16[1,4,65536]{2,1,0:T(4,128)(2,1)}), bf16[4,4,65536]{2,1,0:T(4,128)(2,1)}) %all-gather.3.cloned.1.call-update) | async-done | bytes 2097168 | tf_op jit(solution)/shard_map/all_gather | solution.py:121
  (72 shorter events, 89.0 us)
Async XLA Ops:
  6.5 964.3 %copy-start = (bf16[16,16]{1,0:T(8,128)(2,1)S(1)}, bf16[16,16]{1,0:T(8,128)(2,1)}, u32[]{:S(2)}) copy-start(bf16[16,16]{1,0:T(8,128)(2,1)} %param.11) | copy-start | bytes 1540
  435.6 21.0 %all-to-all-start = ((bf16[8,2,32768]{2,1,0:T(2,128)(2,1)}), bf16[8,2,32768]{2,1,0:T(2,128)(2,1)S(1)}, u32[]{:S(2)}, u32[]{:S(2)}) async-start(bf16[8,2,32768]{2,1,0:T(2,128)(2,1)} %reshape.239), calls=%async_computation | async-start | bytes 2097152 | tf_op jit(solution)/shard_map/all_to_all | solution.py:67
  559.7 30.2 %all-to-all-start.2 = ((bf16[8,16,8192]{2,0,1:T(8,128)(2,1)}), bf16[8,16,8192]{2,0,1:T(8,128)(2,1)S(1)}, u32[]{:S(2)}, u32[]{:S(2)}) async-start(bf16[8,16,8192]{2,0,1:T(8,128)(2,1)} %copy.69), calls=%async_computation.2 | async-start | bytes 4194304 | tf_op jit(solution)/shard_map/all_to_all | solution.py:81
  589.9 1.3 copy-start.6
  591.2 31.0 %all-to-all-start.1 = ((bf16[8,16,8192]{2,0,1:T(8,128)(2,1)}), bf16[8,16,8192]{2,0,1:T(8,128)(2,1)}, u32[]{:S(2)}, u32[]{:S(2)}) async-start(bf16[8,16,8192]{2,0,1:T(8,128)(2,1)} %copy.67), calls=%async_computation.1 | async-start | bytes 4194304 | tf_op jit(solution)/shard_map/all_to_all | solution.py:78
  595.6 324.0 %all-reduce.3.cloned.1.call-start = ((), (), s32[]{:S(2)}) async-start(), calls=%async_computation.4 | async-start | bytes 8388608
  606.9 153.0 %copy-start.7 = (f32[512,128]{1,0:T(8,128)}, f32[512,128]{1,0:T(8,128)S(1)}, u32[]{:S(2)}) copy-start(f32[512,128]{1,0:T(8,128)S(1)} %copy.79) | copy-start | bytes 786436
  632.2 21.9 %copy-start.1 = (f32[8,2,512,128]{3,2,1,0:T(8,128)S(1)}, f32[8,2,512,128]{3,2,1,0:T(8,128)}, u32[]{:S(2)}) copy-start(f32[8,2,512,128]{3,2,1,0:T(8,128)} %reshape.220) | copy-start | bytes 12582916
  632.2 21.9 %copy-start.2 = (f32[8,2,512,128]{3,2,1,0:T(8,128)S(1)}, f32[8,2,512,128]{3,2,1,0:T(8,128)}, u32[]{:S(2)}) copy-start(f32[8,2,512,128]{3,2,1,0:T(8,128)} %reshape.219) | copy-start | bytes 12582916
  746.9 24.8 %copy-start.4 = (f32[4,2,512,128]{3,2,1,0:T(8,128)}, f32[4,2,512,128]{3,2,1,0:T(8,128)S(1)}, u32[]{:S(2)}) copy-start(f32[4,2,512,128]{3,2,1,0:T(8,128)S(1)} %convolution_add_fusion.2) | copy-start | bytes 6291460
  749.0 22.7 %copy-start.5 = (f32[4,2,512,128]{3,2,1,0:T(8,128)}, f32[4,2,512,128]{3,2,1,0:T(8,128)S(1)}, u32[]{:S(2)}) copy-start(f32[4,2,512,128]{3,2,1,0:T(8,128)S(1)} %convolution_subtract_fusion.3) | copy-start | bytes 6291460
  810.4 12.3 %copy-start.3 = (f32[4,2,65536]{2,1,0:T(2,128)S(1)}, f32[4,2,65536]{2,1,0:T(2,128)}, u32[]{:S(2)}) copy-start(f32[4,2,65536]{2,1,0:T(2,128)} %reshape.217) | copy-start | bytes 6291460
  839.0 0.7 copy-start.12
  839.0 80.6 %copy-start.8 = (bf16[4,65536]{1,0:T(4,128)(2,1)S(1)}, bf16[4,65536]{1,0:T(4,128)(2,1)}, u32[]{:S(2)}) copy-start(bf16[4,65536]{1,0:T(4,128)(2,1)} %param.8) | copy-start | bytes 1572868
  839.0 80.6 %copy-start.9 = (bf16[4,65536]{1,0:T(4,128)(2,1)S(1)}, bf16[4,65536]{1,0:T(4,128)(2,1)}, u32[]{:S(2)}) copy-start(bf16[4,65536]{1,0:T(4,128)(2,1)} %param.7) | copy-start | bytes 1572868
  839.0 80.6 %copy-start.10 = (bf16[4,65536]{1,0:T(4,128)(2,1)S(1)}, bf16[4,65536]{1,0:T(4,128)(2,1)}, u32[]{:S(2)}) copy-start(bf16[4,65536]{1,0:T(4,128)(2,1)} %param.6) | copy-start | bytes 1572868
  839.0 80.6 %copy-start.11 = (f32[4]{0:T(128)S(1)}, f32[4]{0:T(128)}, u32[]{:S(2)}) copy-start(f32[4]{0:T(128)} %param.10) | copy-start | bytes 52
  839.0 130.0 %all-gather.3.cloned.1.call-start = ((), (), s32[]{:S(2)}) async-start(), calls=%async_computation.3 | async-start | bytes 2621440 | tf_op jit(solution)/shard_map/all_gather | solution.py:121
Sparse Core Ops, SparseCore 0:
  839.1 80.4 all-reduce.2
  922.9 45.9 all-gather.2
where the time goes:
time: 990 us; the launch traced here: 979 us
  other arithmetic  376 us (38%)
  local copies, waits for them, and re-layouts  216 us (22%)
  matrix products  194 us (20%)
  waiting for transfers between devices  165 us (17%)
  between operations  14.3 us (1%)
  starting transfers between devices  13.7 us (1%)
    unnamed x2, other arithmetic  359 us
    dot_general x20, matrix products, apply_form(): return jnp.einsum(form, table, values, precision=lax.Precision.HIGHEST)  193 us
    unnamed x3, waiting for transfers between devices  79.4 us
    unnamed x31, local copies, waits for them, and re-layouts  65.2 us
    all_to_all x1, local copies, waits for them, and re-layouts, local(): lax.all_to_all(stacked.astype(jnp.bfloat16), 'ctx', split_axis=2, concat_...  58.6 us
    concatenate x1, local copies, waits for them, and re-layouts, local(): stacked = jnp.concatenate([signal, long_filter], 0)[:, None, :]  49.7 us
    all_gather x1, waiting for transfers between devices, local(): lax.all_gather(gated, 'tp', axis=0, tiled=True)  46.2 us
    all_to_all x1, waiting for transfers between devices, local(): lax.all_to_all(spec_im.astype(jnp.bfloat16), 'ctx', split_axis=1, concat_...  21.9 us
  transfers between devices with their start and end apart: 5, of which 5 were waited for; matrix products, arithmetic and copies ran while one was open for 3% of the time, Pallas kernels for 0%

commit v1 on v0

v1 whole, which is shorter than its diff:
```python
import functools

import jax
import jax.numpy as jnp
import numpy as np
from jax import lax
from jax.experimental import pallas as pl
from jax.experimental.pallas import tpu as pltpu
from jax.sharding import PartitionSpec as P

COLS = 512
CHUNKS = 2
BF = jnp.bfloat16
F32 = jnp.float32
VMEM = pl.BlockSpec(memory_space=pltpu.VMEM)
SMEM = pl.BlockSpec(memory_space=pltpu.SMEM)


def make_tables(ctx_count, group, chans, rows):
    big = ctx_count * rows
    own = big // group
    length = big * COLS
    k_one = np.arange(big, dtype=np.int64)
    n_one = np.arange(big, dtype=np.int64)
    angle = 2 * np.pi / (4 * big) * ((4 * k_one[:, None] + 1) * n_one[None, :] % (4 * big))
    both = np.stack([np.cos(angle), -np.sin(angle)], 0)
    both = both.reshape(2, group, own, chans, group, rows)
    left = np.empty((group, group, 2 * own, chans * rows))
    for sub in range(group):
        for step in range(group):
            left[sub, step] = both[:, sub, :, :, (sub + step) % group].reshape(2 * own, -1)
    n_two = np.arange(COLS, dtype=np.int64)
    angle = 2 * np.pi / (4 * length) * ((4 * k_one[:, None] + 1) * n_two[None, :] % (4 * length))
    turn = np.stack([np.cos(angle), -np.sin(angle)], 0).reshape(2, group, own, COLS)
    turn = turn.transpose(1, 0, 2, 3)
    angle = 2 * np.pi / COLS * (n_two[:, None] * n_two[None, :] % COLS)
    cos, sin = np.cos(angle), np.sin(angle)
    right = np.block([[cos, -sin], [sin, cos]])
    bf = jnp.bfloat16
    return (
        left.astype(bf),
        np.ascontiguousarray(left.transpose(0, 1, 3, 2)).astype(bf),
        np.ascontiguousarray(turn).astype(np.float32),
        right.astype(bf),
        np.ascontiguousarray(right.T).astype(bf),
    )


def dot(left, right):
    return jnp.dot(left, right, preferred_element_type=F32)


def forward(parts, left_ref, turn_ref, right_ref, mid_ref):
    own = mid_ref.shape[0]
    total = dot(left_ref[0], parts[0][...])
    for step in range(1, len(parts)):
        total += dot(left_ref[step], parts[step][...])
    val_re, val_im = total[:own], total[own:]
    tab_re, tab_im = turn_ref[0], turn_ref[1]
    mid_ref[:, :COLS] = (val_re * tab_re - val_im * tab_im).astype(BF)
    mid_ref[:, COLS:] = (val_re * tab_im + val_im * tab_re).astype(BF)
    return dot(mid_ref[...], right_ref[...])


def filter_kernel(group, scale, sub_ref, *refs):
    parts, (left_ref, turn_ref, right_ref, out_ref, mid_ref) = refs[:group], refs[group:]
    out_ref[...] = forward(parts, left_ref, turn_ref, right_ref, mid_ref) * scale


def signal_kernel(group, sub_ref, *refs):
    parts = refs[:group]
    spec_ref, left_ref, turn_ref, right_ref, back_right_ref, back_left_ref = refs[group : group + 6]
    own_ref, send_ref, mid_ref, last_ref = refs[group + 6 :]
    own = mid_ref.shape[0]
    spec = forward(parts, left_ref, turn_ref, right_ref, mid_ref)
    sig_re, sig_im = spec[:, :COLS], spec[:, COLS:]
    fil_re, fil_im = spec_ref[:, :COLS], spec_ref[:, COLS:]
    mid_ref[:, :COLS] = (sig_re * fil_re - sig_im * fil_im).astype(BF)
    mid_ref[:, COLS:] = (sig_re * fil_im + sig_im * fil_re).astype(BF)
    back = dot(mid_ref[...], back_right_ref[...])
    val_re, val_im = back[:, :COLS], back[:, COLS:]
    tab_re, tab_im = turn_ref[0], turn_ref[1]
    last_ref[:own] = (val_re * tab_re + val_im * tab_im).astype(BF)
    last_ref[own:] = (val_im * tab_re - val_re * tab_im).astype(BF)
    own_ref[...] = dot(back_left_ref[0], last_ref[...])
    for step in range(1, group):
        send_ref[step - 1] = dot(back_left_ref[step], last_ref[...]).astype(BF)


def by_sub(shape):
    rank = len(shape)
    return pl.BlockSpec((None,) + shape, lambda i, sub: (sub[0],) + (0,) * rank)


def whole(shape):
    rank = len(shape)
    return pl.BlockSpec(shape, lambda i, sub: (0,) * rank)


def run_filter(sub, parts, left, turn, right, scale):
    group = len(parts)
    own = left.shape[2] // 2
    return pl.pallas_call(
        functools.partial(filter_kernel, group, scale),
        out_shape=jax.ShapeDtypeStruct((own, 2 * COLS), F32),
        grid_spec=pltpu.PrefetchScalarGridSpec(
            num_scalar_prefetch=1,
            grid=(1,),
            in_specs=[whole(part.shape) for part in parts]
            + [by_sub(left.shape[1:]), by_sub(turn.shape[1:]), whole(right.shape)],
            out_specs=whole((own, 2 * COLS)),
            scratch_shapes=[pltpu.VMEM((own, 2 * COLS), BF)],
        ),
        compiler_params=pltpu.CompilerParams(vmem_limit_bytes=50 * 2**20),
        name="filter_spectrum",
    )(sub, *parts, left, turn, right)


def run_signal(sub, parts, spec, left, turn, right, back_right, back_left):
    group = len(parts)
    own = left.shape[2] // 2
    half = left.shape[3]
    return pl.pallas_call(
        functools.partial(signal_kernel, group),
        out_shape=(
            jax.ShapeDtypeStruct((half, COLS), F32),
            jax.ShapeDtypeStruct((group - 1, half, COLS), BF),
        ),
        grid_spec=pltpu.PrefetchScalarGridSpec(
            num_scalar_prefetch=1,
            grid=(1,),
            in_specs=[whole(part.shape) for part in parts]
            + [whole(spec.shape), by_sub(left.shape[1:]), by_sub(turn.shape[1:])]
            + [whole(right.shape), whole(back_right.shape), by_sub(back_left.shape[1:])],
            out_specs=(whole((half, COLS)), whole((group - 1, half, COLS))),
            scratch_shapes=[
                pltpu.VMEM((own, 2 * COLS), BF),
                pltpu.VMEM((2 * own, COLS), BF),
            ],
        ),
        compiler_params=pltpu.CompilerParams(vmem_limit_bytes=56 * 2**20),
        name="signal_convolution",
    )(sub, *parts, spec, left, turn, right, back_right, back_left)


def mix_kernel(chans, plane_ref, weight_ref, own_ref, mid_ref, far_ref, edge_ref, acc_ref, out_ref):
    slots = (own_ref, mid_ref, far_ref, edge_ref)
    outs = acc_ref.shape[0]
    final_col = plane_ref[0] * outs
    part_col = plane_ref[3] * outs

    @pl.loop(0, own_ref.shape[1] // 16)
    def _(index):
        rows = pl.ds(pl.multiple_of(index * 16, 16), 16)
        acc = [None] * outs
        part = [None] * outs
        for slot, ref in enumerate(slots):
            for chan in range(chans):
                value = ref[chan, rows].astype(F32)
                row = plane_ref[slot] * chans + chan
                for feat in range(outs):
                    term = value * weight_ref[row, final_col + feat]
                    acc[feat] = term if acc[feat] is None else acc[feat] + term
                    if slot < 3:
                        term = value * weight_ref[row, part_col + feat]
                        part[feat] = term if part[feat] is None else part[feat] + term
        for feat in range(outs):
            acc_ref[feat, rows] = acc[feat]
            out_ref[feat, rows] = part[feat].astype(BF)


def run_mix(planes, weight, own, mid, far, edge):
    chans, rows, cols = own.shape
    outs = weight.shape[1] // 4
    return pl.pallas_call(
        functools.partial(mix_kernel, chans),
        out_shape=(
            jax.ShapeDtypeStruct((outs, rows, cols), F32),
            jax.ShapeDtypeStruct((outs, rows, cols), BF),
        ),
        in_specs=[SMEM, SMEM] + [VMEM] * 4,
        out_specs=(VMEM, VMEM),
        compiler_params=pltpu.CompilerParams(vmem_limit_bytes=32 * 2**20),
        name="mix_features",
    )(planes, weight, own, mid, far, edge)


def line_mix(gated, out_weight):
    plane = lax.axis_index("tp")
    near = plane < 2
    mid_of, far_of, edge_of = jnp.where(near, 2, 1), jnp.where(near, 3, 0), jnp.where(near, 0, 3)
    planes = jnp.stack([plane, mid_of, far_of, edge_of]).astype(jnp.int32)
    weight = out_weight.astype(F32)
    received = []
    for own in gated:
        mid = lax.ppermute(own, "tp", [(1, 2), (2, 1)])
        far = lax.ppermute(own, "tp", [(0, 2), (3, 1)])
        edge = lax.ppermute(own, "tp", [(0, 1), (3, 2)])
        received.append((own, mid, far, edge))
    sums = [run_mix(planes, weight, *slots) for slots in received]
    mixed = []
    for acc, send in sums:
        got = lax.ppermute(send, "tp", [(2, 3), (1, 0)])
        mixed.append((acc + got.astype(F32)).astype(BF))
    return mixed


def gather_mix(gated, out_weight):
    plane = lax.axis_index("tp")
    outs = out_weight.shape[1] // lax.axis_size("tp")
    own_cols = lax.dynamic_slice_in_dim(out_weight, plane * outs, outs, 1)
    return [
        jnp.einsum(
            "co,crl->orl",
            own_cols,
            lax.all_gather(own, "tp", axis=0, tiled=True),
            preferred_element_type=F32,
        ).astype(BF)
        for own in gated
    ]


def local(query_gate, key_branch, value_branch, long_filter, skip_gain, out_weight):
    ctx_count = lax.axis_size("ctx")
    ctx_index = lax.axis_index("ctx")
    chans, tok_count = query_gate.shape
    rows = tok_count // COLS
    group = ctx_count // chans
    length = ctx_count * tok_count
    sub = (ctx_index % group).astype(jnp.int32).reshape(1)
    shape = (chans, rows, COLS)
    left, back_left, turn, right, back_right = make_tables(ctx_count, group, chans, rows)
    swaps = [[sub_i + group * p for p in range(chans)] for sub_i in range(group)]

    def swap(value):
        return lax.all_to_all(value, "ctx", 0, 0, axis_index_groups=swaps, tiled=True)

    def shift(value, step):
        pairs = [
            (group * p + i, group * p + (i + step) % group)
            for p in range(chans)
            for i in range(group)
        ]
        return lax.ppermute(value, "ctx", pairs)

    def gather_parts(value):
        got = swap(value)
        parts = [got] + [shift(got, -step) for step in range(1, group)]
        return [part.reshape(chans * rows, COLS) for part in parts]

    filter_parts = gather_parts(long_filter.astype(BF).reshape(shape))
    product = key_branch.astype(F32) * value_branch.astype(F32)
    signal_parts = gather_parts(product.astype(BF).reshape(shape))
    spec = run_filter(sub, filter_parts, left, turn, right, 1.0 / length)
    conv, send = run_signal(sub, signal_parts, spec, left, turn, right, back_right, back_left)
    for step in range(1, group):
        conv += shift(send[step - 1], step).astype(F32)
    conv = conv.astype(BF).reshape(shape)
    query = query_gate.reshape(shape)
    key = key_branch.reshape(shape).astype(F32)
    value = value_branch.reshape(shape).astype(F32)
    size = rows // CHUNKS
    gated = []
    for chunk in range(CHUNKS):
        cut = slice(chunk * size, (chunk + 1) * size)
        got = swap(conv[:, cut]).astype(F32)
        skip = skip_gain[:, None, None] * (key[:, cut] * value[:, cut])
        gated.append((query[:, cut].astype(F32) * (got + skip)).astype(BF))
    mixed = (line_mix if lax.axis_size("tp") == 4 else gather_mix)(gated, out_weight)
    return jnp.concatenate(mixed, 1).reshape(-1, tok_count)


def solution(mesh):
    placed = (P("tp", "ctx"), P("tp", "ctx"), P("tp", "ctx"), P("tp", "ctx"), P("tp"), P())
    return jax.shard_map(
        local, mesh=mesh, in_specs=placed, out_specs=P("tp", "ctx"), check_vma=False
    )
```

time: 990 us -> 109 us (0.11); the launches traced: 979 us -> 109 us
  other arithmetic: 376 us -> 6.7 us
  local copies, waits for them, and re-layouts: 216 us -> 8.52 us
  matrix products: 194 us -> 0 us
  waiting for transfers between devices: 165 us -> 33.1 us
  starting transfers between devices: 13.7 us -> 40.3 us
  Pallas kernels: 0 us -> 19.9 us
  between operations: 14.3 us -> 0.27 us
    unnamed x2 -> x3, other arithmetic: 359 us -> 0.32 us
    dot_general x21 -> x0, matrix products: 194 us -> none  [the longest x20 193 us: apply_form(): return jnp.einsum(form, table, values, precision=lax.Precision.HIGHEST)]
    unnamed x3 -> x0, waiting for transfers between devices: 79.4 us -> none
    unnamed x31 -> x20, local copies, waits for them, and re-layouts: 65.2 us -> 6.06 us
    all_to_all x1 -> x0, local copies, waits for them, and re-layouts: 58.6 us -> none  [local(): lax.all_to_all(stacked.astype(jnp.bfloat16), 'ctx', split_axis=2, concat_...]
    concatenate x1 -> x0, local copies, waits for them, and re-layouts: 49.7 us -> none  [local(): stacked = jnp.concatenate([signal, long_filter], 0)[:, None, :]]
    all_gather x1 -> x0, waiting for transfers between devices: 46.2 us -> none  [local(): lax.all_gather(gated, 'tp', axis=0, tiled=True)]
    convert_element_type x7 -> x1, local copies, waits for them, and re-layouts: 29.9 us -> 1.6 us  [local(): value = value_branch.reshape(shape).astype(F32)]
  transfers between devices with their start and end apart: 5 -> 15, of which waited for: 5 -> 9; matrix products, arithmetic and copies ran while one was open for 3% -> 5% of each run, Pallas kernels for 0% -> 8%
where the time goes in v1:
time: 109 us
  starting transfers between devices  40.3 us (37%)
  waiting for transfers between devices  33.1 us (30%)
  Pallas kernels  19.9 us (18%)
  local copies, waits for them, and re-layouts  8.52 us (8%)
  other arithmetic  6.7 us (6%)
    all_to_all x4, waiting for transfers between devices, swap(): lax.all_to_all(value, 'ctx', 0, 0, axis_index_groups=swaps, tiled=True)  21.3 us
    all_to_all x4, starting transfers between devices, swap(): lax.all_to_all(value, 'ctx', 0, 0, axis_index_groups=swaps, tiled=True)  16.2 us
    pallas_call x1, Pallas kernels, run_signal(): pl.pallas_call(functools.partial(signal_kernel, group), out_shape=(jax.Sh...  10.8 us
    ppermute x2, starting transfers between devices, line_mix(): far = lax.ppermute(own, 'tp', [(0, 2), (3, 1)])  10.2 us
    ppermute x2, starting transfers between devices, line_mix(): edge = lax.ppermute(own, 'tp', [(0, 1), (3, 2)])  9.55 us
    ppermute x2, waiting for transfers between devices, line_mix(): got = lax.ppermute(send, 'tp', [(2, 3), (1, 0)])  6.88 us
    unnamed x20, local copies, waits for them, and re-layouts  6.06 us
    pallas_call x1, Pallas kernels, run_filter(): pl.pallas_call(functools.partial(filter_kernel, group, scale), out_shape=...  5.55 us
  transfers between devices with their start and end apart: 15, of which 9 were waited for; matrix products, arithmetic and copies ran while one was open for 5% of the time, Pallas kernels for 8%

profile of v1, /device:TPU:0, one launch (start us, length us, event | category | flops | bytes accessed | tf_op | source)
XLA Modules:
  0.0 108.7 jit_solution(10002925109671093378)
XLA Ops:
  0.0 1.4 %convert_element_type.68 = bf16[4,65536]{1,0:T(4,128)(2,1)S(1)} convert(f32[4,65536]{1,0:T(4,128)} %param.14) | non-fusion elementwise | flops 262144 | bytes 1572864 | tf_op jit(solution)/shard_map/convert_element_type | solution.py:251
  2.3 5.2 %all-to-all-start.1 = ((bf16[4,128,512]{2,1,0:T(8,128)(2,1)}), bf16[4,128,512]{2,1,0:T(8,128)(2,1)S(1)}, u32[]{:S(2)}, u32[]{:S(2)}) async-start(bf16[4,128,512]{2,1,0:T(8,128)(2,1)} %bitcast.31), calls=%async_computation.1 | async-start | bytes 1048576 | tf_op jit(solution)/shard_map/all_to_all | solution.py:236
  7.5 1.5 %multiply_convert_fusion = bf16[4,65536]{1,0:T(4,128)(2,1)S(1)} fusion(bf16[4,65536]{1,0:T(4,128)(2,1)} %param.13, bf16[4,65536]{1,0:T(4,128)(2,1)} %param.12), kind=kLoop, calls=%fused_computation.3 | loop fusion | flops 1048576 | bytes 1572864 | tf_op jit(solution)/shard_map/convert_element_type | solution.py:253
  9.8 5.7 %all-to-all-done.1 = bf16[4,128,512]{2,1,0:T(8,128)(2,1)S(1)} async-done(((bf16[4,128,512]{2,1,0:T(8,128)(2,1)}), bf16[4,128,512]{2,1,0:T(8,128)(2,1)S(1)}, u32[]{:S(2)}, u32[]{:S(2)}) %all-to-all-start.1) | async-done | bytes 524320 | tf_op jit(solution)/shard_map/all_to_all | solution.py:236
  15.5 3.5 %all-to-all-start = ((bf16[4,128,512]{2,1,0:T(8,128)(2,1)}), bf16[4,128,512]{2,1,0:T(8,128)(2,1)S(1)}, u32[]{:S(2)}, u32[]{:S(2)}) async-start(bf16[4,128,512]{2,1,0:T(8,128)(2,1)} %bitcast.32), calls=%async_computation | async-start | bytes 1048576 | tf_op jit(solution)/shard_map/all_to_all | solution.py:236
  19.1 7.0 %all-to-all-done = bf16[4,128,512]{2,1,0:T(8,128)(2,1)S(1)} async-done(((bf16[4,128,512]{2,1,0:T(8,128)(2,1)}), bf16[4,128,512]{2,1,0:T(8,128)(2,1)S(1)}, u32[]{:S(2)}, u32[]{:S(2)}) %all-to-all-start) | async-done | bytes 524320 | tf_op jit(solution)/shard_map/all_to_all | solution.py:236
  26.1 5.5 %filter_spectrum.1.refs_2_ = f32[512,1024]{1,0:T(8,128)S(1)} custom-call(s32[1]{0:T(128)} %bitcast.4.sub_ref, bf16[512,512]{1,0:T(8,128)(2,1)S(1)} %bitcast.34, bf16[512,512]{1,0:T(8,128)(2,1)S(1)} %bitcast.35, bf16[2,2,1024,512]{3,2,1,0:T(8,128)(2,1)} %constant.36.clone.refs_2_.refs_3_, f32[2,2,512,512]{3,2,1,0:T(8,128)} %constant.37.clone.refs_3_.refs_4_, ...), custom_call_target="tpu_custom_call" | custom-call | tf_op jit(solution)/shard_map/filter_spectrum/pallas_call | solution.py:103
  33.8 10.8 %signal_convolution.1 = (f32[512,512]{1,0:T(8,128)}, bf16[1,512,512]{2,1,0:T(8,128)(2,1)}) custom-call(s32[1]{0:T(128)} %bitcast.4.sub_ref, bf16[512,512]{1,0:T(8,128)(2,1)} %bitcast.38, bf16[512,512]{1,0:T(8,128)(2,1)} %bitcast.43, f32[512,1024]{1,0:T(8,128)} %copy-done, bf16[2,2,1024,512]{3,2,1,0:T(8,128)(2,1)} %constant.36.clone.refs_2_.refs_3_, ...), custom_call_target="tpu_custom_call" | custom-call | tf_op jit(solution)/shard_map/signal_convolution/pallas_call | solution.py:123
  44.9 1.8 %collective-permute-done.2 = bf16[512,512]{1,0:T(8,128)(2,1)S(1)} collective-permute-done((bf16[512,512]{1,0:T(8,128)(2,1)}, bf16[512,512]{1,0:T(8,128)(2,1)S(1)}, u32[]{:S(2)}, u32[]{:S(2)}) %collective-permute-start.2) | collective-permute-done | bytes 524320 | tf_op jit(solution)/shard_map/ppermute | solution.py:244
  46.7 1.4 %add_convert_fusion = bf16[512,512]{1,0:T(8,128)(2,1)S(1)} fusion(f32[512,512]{1,0:T(8,128)} %get-tuple-element.11, bf16[512,512]{1,0:T(8,128)(2,1)S(1)} %collective-permute-done.2), kind=kLoop, calls=%fused_computation.2 | loop fusion | flops 786432 | bytes 2097152 | tf_op jit(solution)/shard_map/convert_element_type | solution.py:258
  49.0 3.4 %all-to-all-start.2 = ((bf16[4,64,512]{2,1,0:T(8,128)(2,1)}), bf16[4,64,512]{2,1,0:T(8,128)(2,1)S(1)}, u32[]{:S(2)}, u32[]{:S(2)}) async-start(bf16[4,64,512]{2,1,0:T(8,128)(2,1)} %get-tuple-element.19), calls=%async_computation.2 | async-start | bytes 524288 | tf_op jit(solution)/shard_map/all_to_all | solution.py:236
  53.6 4.8 %all-to-all-done.2 = bf16[4,64,512]{2,1,0:T(8,128)(2,1)S(1)} async-done(((bf16[4,64,512]{2,1,0:T(8,128)(2,1)}), bf16[4,64,512]{2,1,0:T(8,128)(2,1)S(1)}, u32[]{:S(2)}, u32[]{:S(2)}) %all-to-all-start.2) | async-done | bytes 262176 | tf_op jit(solution)/shard_map/all_to_all | solution.py:236
  58.4 4.2 %all-to-all-start.3 = ((bf16[4,64,512]{2,1,0:T(8,128)(2,1)}), bf16[4,64,512]{2,1,0:T(8,128)(2,1)}, u32[]{:S(2)}, u32[]{:S(2)}) async-start(bf16[4,64,512]{2,1,0:T(8,128)(2,1)} %get-tuple-element.20), calls=%async_computation.3 | async-start | bytes 524288 | tf_op jit(solution)/shard_map/all_to_all | solution.py:236
  62.5 1.6 %copy_bitcast_fusion = (f32[4,128,512]{2,1,0:T(8,128)S(1)}, f32[4,128,512]{2,1,0:T(8,128)}) fusion(f32[1,4,128,512]{3,1,2,0:T(4,128)S(1)} %convert.2, f32[1,4,128,512]{3,1,2,0:T(4,128)S(1)} %convert.3), kind=kLoop, calls=%fused_computation | loop fusion | bytes 4194304 | tf_op jit(solution)/shard_map/convert_element_type | solution.py:261
  64.2 3.8 %all-to-all-done.3 = bf16[4,64,512]{2,1,0:T(8,128)(2,1)} async-done(((bf16[4,64,512]{2,1,0:T(8,128)(2,1)}), bf16[4,64,512]{2,1,0:T(8,128)(2,1)}, u32[]{:S(2)}, u32[]{:S(2)}) %all-to-all-start.3) | async-done | bytes 262176 | tf_op jit(solution)/shard_map/all_to_all | solution.py:236
  68.0 1.9 %fusion.7 = (bf16[4,64,512]{2,1,0:T(8,128)(2,1)S(1)}, bf16[4,64,512]{2,1,0:T(8,128)(2,1)S(1)}) fusion(f32[4,128,512]{2,1,0:T(8,128)S(1)} %get-tuple-element.21, f32[4,128,512]{2,1,0:T(8,128)} %get-tuple-element.22, bf16[4,64,512]{2,1,0:T(8,128)(2,1)S(1)} %all-to-all-done.2, bf16[4,128,512]{2,1,0:T(8,128)(2,1)} %bitcast.41, f32[4]{0:T(128)S(1)} %copy-done.7, ...), kind=kLoop, calls=%fused_computation.16 | loop fusion | flops 1835008 | bytes 3670032 | tf_op jit(solution)/shard_map/convert_element_type | solution.py:268
  70.5 6.2 %collective-permute-start.4 = (bf16[4,64,512]{2,1,0:T(8,128)(2,1)S(1)}, bf16[4,64,512]{2,1,0:T(8,128)(2,1)S(1)}, u32[]{:S(2)}, u32[]{:S(2)}) collective-permute-start(bf16[4,64,512]{2,1,0:T(8,128)(2,1)S(1)} %get-tuple-element.17.own_ref), channel_id=1, source_target_pairs={{0,2},{3,1},{4,6},{7,5},{8,10},{11,9},{12,14},{15,13},{16,18},{19,... | collective-permute-start | bytes 786440 | tf_op jit(solution)/shard_map/ppermute | solution.py:197
  76.8 1.4 %collective-permute-start.5 = (bf16[4,64,512]{2,1,0:T(8,128)(2,1)S(1)}, bf16[4,64,512]{2,1,0:T(8,128)(2,1)S(1)}, u32[]{:S(2)}, u32[]{:S(2)}) collective-permute-start(bf16[4,64,512]{2,1,0:T(8,128)(2,1)S(1)} %get-tuple-element.17.own_ref), channel_id=1, source_target_pairs={{0,1},{3,2},{4,5},{7,6},{8,9},{11,10},{12,13},{15,14},{16,17},{19,... | collective-permute-start | bytes 786440 | tf_op jit(solution)/shard_map/ppermute | solution.py:198
  78.9 4.0 %collective-permute-start.8 = (bf16[4,64,512]{2,1,0:T(8,128)(2,1)S(1)}, bf16[4,64,512]{2,1,0:T(8,128)(2,1)S(1)}, u32[]{:S(2)}, u32[]{:S(2)}) collective-permute-start(bf16[4,64,512]{2,1,0:T(8,128)(2,1)S(1)} %get-tuple-element.18.own_ref), channel_id=1, source_target_pairs={{0,2},{3,1},{4,6},{7,5},{8,10},{11,9},{12,14},{15,13},{16,18},{19,... | collective-permute-start | bytes 786440 | tf_op jit(solution)/shard_map/ppermute | solution.py:197
  82.9 8.2 %collective-permute-start.9 = (bf16[4,64,512]{2,1,0:T(8,128)(2,1)S(1)}, bf16[4,64,512]{2,1,0:T(8,128)(2,1)S(1)}, u32[]{:S(2)}, u32[]{:S(2)}) collective-permute-start(bf16[4,64,512]{2,1,0:T(8,128)(2,1)S(1)} %get-tuple-element.18.own_ref), channel_id=1, source_target_pairs={{0,1},{3,2},{4,5},{7,6},{8,9},{11,10},{12,13},{15,14},{16,17},{19,... | collective-permute-start | bytes 786440 | tf_op jit(solution)/shard_map/ppermute | solution.py:198
  91.1 1.8 %mix_features.2 = (f32[4,64,512]{2,1,0:T(8,128)S(1)}, bf16[4,64,512]{2,1,0:T(8,128)(2,1)S(1)}) custom-call(s32[4]{0:T(128)S(1)} %pad_add_fusion.plane_ref, f32[16,16]{1,0:T(8,128)S(1)} %convert_element_type.63.weight_ref, bf16[4,64,512]{2,1,0:T(8,128)(2,1)S(1)} %get-tuple-element.17.own_ref, bf16[4,64,512]{2,1,0:T(8,128)(2,1)S(1)} %collective-permute-done.3.mid_ref, ...), custom_call_target="tpu_custom_call" | custom-call | tf_op jit(solution)/shard_map/mix_features/pallas_call | solution.py:175
  94.5 2.8 %collective-permute-done.9.edge_ref = bf16[4,64,512]{2,1,0:T(8,128)(2,1)S(1)} collective-permute-done((bf16[4,64,512]{2,1,0:T(8,128)(2,1)S(1)}, bf16[4,64,512]{2,1,0:T(8,128)(2,1)S(1)}, u32[]{:S(2)}, u32[]{:S(2)}) %collective-permute-start.9) | collective-permute-done | bytes 262176 | tf_op jit(solution)/shard_map/ppermute | solution.py:198
  97.3 1.8 %mix_features.3 = (f32[4,64,512]{2,1,0:T(8,128)S(1)}, bf16[4,64,512]{2,1,0:T(8,128)(2,1)S(1)}) custom-call(s32[4]{0:T(128)S(1)} %pad_add_fusion.plane_ref, f32[16,16]{1,0:T(8,128)S(1)} %convert_element_type.63.weight_ref, bf16[4,64,512]{2,1,0:T(8,128)(2,1)S(1)} %get-tuple-element.18.own_ref, bf16[4,64,512]{2,1,0:T(8,128)(2,1)S(1)} %collective-permute-done.7.mid_ref, ...), custom_call_target="tpu_custom_call" | custom-call | tf_op jit(solution)/shard_map/mix_features/pallas_call | solution.py:175
  101.6 5.8 %collective-permute-done.10 = bf16[4,64,512]{2,1,0:T(8,128)(2,1)S(1)} collective-permute-done((bf16[4,64,512]{2,1,0:T(8,128)(2,1)S(1)}, bf16[4,64,512]{2,1,0:T(8,128)(2,1)S(1)}, u32[]{:S(2)}, u32[]{:S(2)}) %collective-permute-start.10) | collective-permute-done | bytes 262176 | tf_op jit(solution)/shard_map/ppermute | solution.py:203
  (43 shorter events, 13.2 us)
Async XLA Ops:
  2.3 13.2 %all-to-all-start.1 = ((bf16[4,128,512]{2,1,0:T(8,128)(2,1)}), bf16[4,128,512]{2,1,0:T(8,128)(2,1)S(1)}, u32[]{:S(2)}, u32[]{:S(2)}) async-start(bf16[4,128,512]{2,1,0:T(8,128)(2,1)} %bitcast.31), calls=%async_computation.1 | async-start | bytes 1048576 | tf_op jit(solution)/shard_map/all_to_all | solution.py:236
  15.5 10.6 %all-to-all-start = ((bf16[4,128,512]{2,1,0:T(8,128)(2,1)}), bf16[4,128,512]{2,1,0:T(8,128)(2,1)S(1)}, u32[]{:S(2)}, u32[]{:S(2)}) async-start(bf16[4,128,512]{2,1,0:T(8,128)(2,1)} %bitcast.32), calls=%async_computation | async-start | bytes 1048576 | tf_op jit(solution)/shard_map/all_to_all | solution.py:236
  19.0 7.1 %collective-permute-start.1 = (bf16[4,128,512]{2,1,0:T(8,128)(2,1)S(1)}, bf16[4,128,512]{2,1,0:T(8,128)(2,1)S(1)}, u32[]{:S(2)}, u32[]{:S(2)}) collective-permute-start(bf16[4,128,512]{2,1,0:T(8,128)(2,1)S(1)} %all-to-all-done.1), channel_id=1, source_target_pairs={{0,4},{4,0},{8,12},{12,8},{16,20},{20,16},{24,28},{28,24},{1,5},{5... | collective-permute-start | bytes 1572872 | tf_op jit(solution)/shard_map/ppermute | solution.py:244
  26.1 5.6 %copy-start.3 = (bf16[4,128,512]{2,1,0:T(8,128)(2,1)}, bf16[4,128,512]{2,1,0:T(8,128)(2,1)S(1)}, u32[]{:S(2)}) copy-start(bf16[4,128,512]{2,1,0:T(8,128)(2,1)S(1)} %all-to-all-done) | copy-start | bytes 1572868
  26.1 6.9 %collective-permute-start = (bf16[4,128,512]{2,1,0:T(8,128)(2,1)S(1)}, bf16[4,128,512]{2,1,0:T(8,128)(2,1)S(1)}, u32[]{:S(2)}, u32[]{:S(2)}) collective-permute-start(bf16[4,128,512]{2,1,0:T(8,128)(2,1)S(1)} %all-to-all-done), channel_id=1, source_target_pairs={{0,4},{4,0},{8,12},{12,8},{16,20},{20,16},{24,28},{28,24},{1,5},{5... | collective-permute-start | bytes 1572872 | tf_op jit(solution)/shard_map/ppermute | solution.py:244
  31.7 1.4 %copy-start = (f32[512,1024]{1,0:T(8,128)}, f32[512,1024]{1,0:T(8,128)S(1)}, u32[]{:S(2)}) copy-start(f32[512,1024]{1,0:T(8,128)S(1)} %filter_spectrum.1.refs_2_) | copy-start | bytes 6291460
  33.0 0.8 copy-start.4
  33.8 18.5 %copy-start.1 = (bf16[4,65536]{1,0:T(4,128)(2,1)S(1)}, bf16[4,65536]{1,0:T(4,128)(2,1)}, u32[]{:S(2)}) copy-start(bf16[4,65536]{1,0:T(4,128)(2,1)} %param.13) | copy-start | bytes 1572868
  44.6 8.0 %copy-start.2 = (bf16[4,65536]{1,0:T(4,128)(2,1)S(1)}, bf16[4,65536]{1,0:T(4,128)(2,1)}, u32[]{:S(2)}) copy-start(bf16[4,65536]{1,0:T(4,128)(2,1)} %param.12) | copy-start | bytes 1572868
  44.6 8.1 %copy-start.5 = (bf16[4,65536]{1,0:T(4,128)(2,1)S(1)}, bf16[4,65536]{1,0:T(4,128)(2,1)}, u32[]{:S(2)}) copy-start(bf16[4,65536]{1,0:T(4,128)(2,1)} %param.11) | copy-start | bytes 1572868
  44.6 2.1 %collective-permute-start.2 = (bf16[512,512]{1,0:T(8,128)(2,1)}, bf16[512,512]{1,0:T(8,128)(2,1)S(1)}, u32[]{:S(2)}, u32[]{:S(2)}) collective-permute-start(bf16[512,512]{1,0:T(8,128)(2,1)} %bitcast.45), channel_id=1, source_target_pairs={{0,4},{4,0},{8,12},{12,8},{16,20},{20,16},{24,28},{28,24},{1,5},{5... | collective-permute-start | bytes 1572872 | tf_op jit(solution)/shard_map/ppermute | solution.py:244
  49.0 9.4 %all-to-all-start.2 = ((bf16[4,64,512]{2,1,0:T(8,128)(2,1)}), bf16[4,64,512]{2,1,0:T(8,128)(2,1)S(1)}, u32[]{:S(2)}, u32[]{:S(2)}) async-start(bf16[4,64,512]{2,1,0:T(8,128)(2,1)} %get-tuple-element.19), calls=%async_computation.2 | async-start | bytes 524288 | tf_op jit(solution)/shard_map/all_to_all | solution.py:236
  52.4 15.6 %copy-start.7 = (f32[4]{0:T(128)S(1)}, f32[4]{0:T(128)}, u32[]{:S(2)}) copy-start(f32[4]{0:T(128)} %param.15) | copy-start | bytes 52
  58.4 32.7 %copy-start.6 = (bf16[16,16]{1,0:T(8,128)(2,1)S(1)}, bf16[16,16]{1,0:T(8,128)(2,1)}, u32[]{:S(2)}) copy-start(bf16[16,16]{1,0:T(8,128)(2,1)} %param.16) | copy-start | bytes 1540
  58.4 9.6 %all-to-all-start.3 = ((bf16[4,64,512]{2,1,0:T(8,128)(2,1)}), bf16[4,64,512]{2,1,0:T(8,128)(2,1)}, u32[]{:S(2)}, u32[]{:S(2)}) async-start(bf16[4,64,512]{2,1,0:T(8,128)(2,1)} %get-tuple-element.20), calls=%async_computation.3 | async-start | bytes 524288 | tf_op jit(solution)/shard_map/all_to_all | solution.py:236
  69.9 13.0 %collective-permute-start.3 = (bf16[4,64,512]{2,1,0:T(8,128)(2,1)S(1)}, bf16[4,64,512]{2,1,0:T(8,128)(2,1)S(1)}, u32[]{:S(2)}, u32[]{:S(2)}) collective-permute-start(bf16[4,64,512]{2,1,0:T(8,128)(2,1)S(1)} %get-tuple-element.17.own_ref), channel_id=1, source_target_pairs={{1,2},{2,1},{5,6},{6,5},{9,10},{10,9},{13,14},{14,13},{17,18},{18,... | collective-permute-start | bytes 786440 | tf_op jit(solution)/shard_map/ppermute | solution.py:196
  70.5 20.6 %collective-permute-start.4 = (bf16[4,64,512]{2,1,0:T(8,128)(2,1)S(1)}, bf16[4,64,512]{2,1,0:T(8,128)(2,1)S(1)}, u32[]{:S(2)}, u32[]{:S(2)}) collective-permute-start(bf16[4,64,512]{2,1,0:T(8,128)(2,1)S(1)} %get-tuple-element.17.own_ref), channel_id=1, source_target_pairs={{0,2},{3,1},{4,6},{7,5},{8,10},{11,9},{12,14},{15,13},{16,18},{19,... | collective-permute-start | bytes 786440 | tf_op jit(solution)/shard_map/ppermute | solution.py:197
  76.8 14.4 %collective-permute-start.5 = (bf16[4,64,512]{2,1,0:T(8,128)(2,1)S(1)}, bf16[4,64,512]{2,1,0:T(8,128)(2,1)S(1)}, u32[]{:S(2)}, u32[]{:S(2)}) collective-permute-start(bf16[4,64,512]{2,1,0:T(8,128)(2,1)S(1)} %get-tuple-element.17.own_ref), channel_id=1, source_target_pairs={{0,1},{3,2},{4,5},{7,6},{8,9},{11,10},{12,13},{15,14},{16,17},{19,... | collective-permute-start | bytes 786440 | tf_op jit(solution)/shard_map/ppermute | solution.py:198
  78.2 16.0 %collective-permute-start.7 = (bf16[4,64,512]{2,1,0:T(8,128)(2,1)S(1)}, bf16[4,64,512]{2,1,0:T(8,128)(2,1)S(1)}, u32[]{:S(2)}, u32[]{:S(2)}) collective-permute-start(bf16[4,64,512]{2,1,0:T(8,128)(2,1)S(1)} %get-tuple-element.18.own_ref), channel_id=1, source_target_pairs={{1,2},{2,1},{5,6},{6,5},{9,10},{10,9},{13,14},{14,13},{17,18},{18,... | collective-permute-start | bytes 786440 | tf_op jit(solution)/shard_map/ppermute | solution.py:196
  78.9 15.7 %collective-permute-start.8 = (bf16[4,64,512]{2,1,0:T(8,128)(2,1)S(1)}, bf16[4,64,512]{2,1,0:T(8,128)(2,1)S(1)}, u32[]{:S(2)}, u32[]{:S(2)}) collective-permute-start(bf16[4,64,512]{2,1,0:T(8,128)(2,1)S(1)} %get-tuple-element.18.own_ref), channel_id=1, source_target_pairs={{0,2},{3,1},{4,6},{7,5},{8,10},{11,9},{12,14},{15,13},{16,18},{19,... | collective-permute-start | bytes 786440 | tf_op jit(solution)/shard_map/ppermute | solution.py:197
  82.9 14.5 %collective-permute-start.9 = (bf16[4,64,512]{2,1,0:T(8,128)(2,1)S(1)}, bf16[4,64,512]{2,1,0:T(8,128)(2,1)S(1)}, u32[]{:S(2)}, u32[]{:S(2)}) collective-permute-start(bf16[4,64,512]{2,1,0:T(8,128)(2,1)S(1)} %get-tuple-element.18.own_ref), channel_id=1, source_target_pairs={{0,1},{3,2},{4,5},{7,6},{8,9},{11,10},{12,13},{15,14},{16,17},{19,... | collective-permute-start | bytes 786440 | tf_op jit(solution)/shard_map/ppermute | solution.py:198
  92.9 8.6 %collective-permute-start.6 = (bf16[4,64,512]{2,1,0:T(8,128)(2,1)S(1)}, bf16[4,64,512]{2,1,0:T(8,128)(2,1)S(1)}, u32[]{:S(2)}, u32[]{:S(2)}) collective-permute-start(bf16[4,64,512]{2,1,0:T(8,128)(2,1)S(1)} %get-tuple-element.14), channel_id=1, source_target_pairs={{2,3},{1,0},{6,7},{5,4},{10,11},{9,8},{14,15},{13,12},{18,19},{17,... | collective-permute-start | bytes 786440 | tf_op jit(solution)/shard_map/ppermute | solution.py:203
  99.1 8.3 %collective-permute-start.10 = (bf16[4,64,512]{2,1,0:T(8,128)(2,1)S(1)}, bf16[4,64,512]{2,1,0:T(8,128)(2,1)S(1)}, u32[]{:S(2)}, u32[]{:S(2)}) collective-permute-start(bf16[4,64,512]{2,1,0:T(8,128)(2,1)S(1)} %get-tuple-element.16), channel_id=1, source_target_pairs={{2,3},{1,0},{6,7},{5,4},{10,11},{9,8},{14,15},{13,12},{18,19},{17,... | collective-permute-start | bytes 786440 | tf_op jit(solution)/shard_map/ppermute | solution.py:203

commit v2 on v1

v2 whole, which is shorter than its diff:
```python
import functools

import jax
import jax.numpy as jnp
import numpy as np
from jax import lax
from jax.experimental import pallas as pl
from jax.experimental.pallas import tpu as pltpu
from jax.sharding import PartitionSpec as P

COLS = 512
CUTS = (0, 256, 512)
BF = jnp.bfloat16
F32 = jnp.float32
VMEM = pl.BlockSpec(memory_space=pltpu.VMEM)
SMEM = pl.BlockSpec(memory_space=pltpu.SMEM)
ANY = pl.BlockSpec(memory_space=pl.ANY)


def make_tables(ctx_count, group, chans, rows):
    big = ctx_count * rows
    own = big // group
    length = big * COLS
    k_one = np.arange(big, dtype=np.int64)
    n_one = np.arange(big, dtype=np.int64)
    angle = 2 * np.pi / (4 * big) * ((4 * k_one[:, None] + 1) * n_one[None, :] % (4 * big))
    both = np.stack([np.cos(angle), -np.sin(angle)], 0)
    both = both.reshape(2, group, own, chans, group, rows)
    left = np.empty((group, 2 * own, group, chans * rows))
    back_left = np.empty((group, chans * rows, group, 2 * own))
    for sub in range(group):
        for step in range(group):
            other = (sub + step) % group
            left[sub, :, step] = both[:, sub, :, :, other].reshape(2 * own, -1)
            back_left[sub, :, step] = both[:, other, :, :, sub].reshape(2 * own, -1).T
    n_two = np.arange(COLS, dtype=np.int64)
    angle = 2 * np.pi / (4 * length) * ((4 * k_one[:, None] + 1) * n_two[None, :] % (4 * length))
    turn = np.stack([np.cos(angle), -np.sin(angle)], 0).reshape(2, group, own, COLS)
    turn = np.ascontiguousarray(turn.transpose(1, 0, 2, 3))
    angle = 2 * np.pi / COLS * (n_two[:, None] * n_two[None, :] % COLS)
    cos, sin = np.cos(angle), np.sin(angle)
    right = np.block([[cos, -sin], [sin, cos]])
    return (
        left.reshape(group, 2 * own, big).astype(BF),
        back_left.reshape(group, chans * rows, 2 * big).astype(BF),
        turn.astype(np.float32),
        right.astype(BF),
        np.ascontiguousarray(right.T).astype(BF),
    )


def dot(left, right):
    return jnp.dot(left, right, preferred_element_type=F32)


def load(copies):
    started = [pltpu.make_async_copy(*copy) for copy in copies]
    for copy in started:
        copy.start()
    return started


def cost(flops, moved):
    return pl.CostEstimate(flops=flops, bytes_accessed=moved, transcendentals=0)


def params(mib):
    return pltpu.CompilerParams(vmem_limit_bytes=mib * 2**20)


def place():
    index = lax.axis_index("ctx")
    return index


def forward_stage(blocks, chans, group, x_ref, left_ref, turn_ref, mid_ref, waits):
    rows = blocks[0].shape[0]
    own = mid_ref.shape[0]
    home = lax.axis_index("ctx") // group
    for step in range(group):
        for rel in range(chans):
            first = pl.multiple_of((step * chans + (home ^ rel)) * rows, rows)
            x_ref[pl.ds(first, rows)] = blocks[step * chans + rel][...]
    waits[0].wait()
    for tile in range(0, COLS, 256):
        cut = slice(tile, tile + 256)
        val = dot(left_ref[...], x_ref[:, cut])
        if tile == 0:
            waits[1].wait()
        val_re, val_im = val[:own], val[own:]
        tab_re, tab_im = turn_ref[0, :, cut], turn_ref[1, :, cut]
        mid_ref[:, cut] = (val_re * tab_re - val_im * tab_im).astype(BF)
        cut_im = slice(COLS + tile, COLS + tile + 256)
        mid_ref[:, cut_im] = (val_re * tab_im + val_im * tab_re).astype(BF)


def back_stage(cols, prod, table_ref, turn_ref, out_ref):
    own = turn_ref.shape[1]
    for tile in range(cols[0], cols[1], 128):
        cut = slice(tile, tile + 128)
        dst = slice(tile - cols[0], tile - cols[0] + 128)
        val_re = dot(prod, table_ref[:, cut])
        val_im = dot(prod, table_ref[:, COLS + tile : COLS + tile + 128])
        tab_re, tab_im = turn_ref[0, :, cut], turn_ref[1, :, cut]
        out_ref[:own, dst] = (val_re * tab_re + val_im * tab_im).astype(BF)
        out_ref[own:, dst] = (val_im * tab_re - val_re * tab_im).astype(BF)


def filter_kernel(chans, group, scale, *refs):
    count = chans * group
    blocks, (left_hbm, turn_hbm, right_hbm, out_ref) = refs[:count], refs[count : count + 4]
    x_ref, left_ref, turn_ref, right_ref, mid_ref, sems = refs[count + 4 :]
    sub = lax.rem(lax.axis_index("ctx"), group)
    waits = load(
        [
            (left_hbm.at[sub], left_ref, sems.at[0]),
            (turn_hbm.at[sub], turn_ref, sems.at[1]),
            (right_hbm, right_ref, sems.at[2]),
        ]
    )
    forward_stage(blocks, chans, group, x_ref, left_ref, turn_ref, mid_ref, waits)
    waits[2].wait()
    for tile in range(0, 2 * COLS, 256):
        cut = slice(tile, tile + 256)
        out_ref[:, cut] = dot(mid_ref[...], right_ref[:, cut]) * scale


def signal_kernel(chans, group, cols, *refs):
    count = chans * group
    blocks = refs[:count]
    spec_ref, left_hbm, turn_hbm, right_hbm, back_hbm, prod_ref, out_ref = refs[count : count + 7]
    x_ref, left_ref, turn_ref, right_ref, back_ref, mid_ref, sems = refs[count + 7 :]
    sub = lax.rem(lax.axis_index("ctx"), group)
    waits = load(
        [
            (left_hbm.at[sub], left_ref, sems.at[0]),
            (turn_hbm.at[sub], turn_ref, sems.at[1]),
            (right_hbm, right_ref, sems.at[2]),
            (back_hbm, back_ref, sems.at[3]),
        ]
    )
    forward_stage(blocks, chans, group, x_ref, left_ref, turn_ref, mid_ref, waits)
    waits[2].wait()
    for tile in range(0, COLS, 256):
        cut, cut_im = slice(tile, tile + 256), slice(COLS + tile, COLS + tile + 256)
        sig_re = dot(mid_ref[...], right_ref[:, cut])
        sig_im = dot(mid_ref[...], right_ref[:, cut_im])
        fil_re, fil_im = spec_ref[:, cut], spec_ref[:, cut_im]
        prod_ref[:, cut] = (sig_re * fil_re - sig_im * fil_im).astype(BF)
        prod_ref[:, cut_im] = (sig_re * fil_im + sig_im * fil_re).astype(BF)
    waits[3].wait()
    back_stage(cols, prod_ref[...], back_ref, turn_ref, out_ref)


def later_kernel(group, cols, prod_ref, turn_hbm, back_hbm, out_ref, turn_ref, back_ref, sems):
    sub = lax.rem(lax.axis_index("ctx"), group)
    waits = load(
        [(back_hbm, back_ref, sems.at[0]), (turn_hbm.at[sub], turn_ref, sems.at[1])]
    )
    for wait in waits:
        wait.wait()
    back_stage(cols, prod_ref[...], back_ref, turn_ref, out_ref)


def position_kernel(chans, group, *refs):
    parts, table_hbm = refs[:group], refs[group]
    outs = refs[group + 1 : group + 1 + chans]
    table_ref, sum_ref, sems = refs[group + 1 + chans :]
    home = lax.axis_index("ctx") // group
    sub = lax.rem(lax.axis_index("ctx"), group)
    (wait,) = load([(table_hbm.at[sub], table_ref, sems.at[0])])
    wait.wait()
    depth = parts[0].shape[0]
    total = dot(table_ref[:, :depth], parts[0][...])
    for step in range(1, group):
        total += dot(table_ref[:, step * depth : (step + 1) * depth], parts[step][...])
    sum_ref[...] = total.astype(BF)
    rows = outs[0].shape[0]
    for rel in range(chans):
        outs[rel][...] = sum_ref[pl.ds(pl.multiple_of((home ^ rel) * rows, rows), rows)]


def gate_kernel(group, cols, *refs):
    chans = len(refs) - 5
    parts = refs[:chans]
    query_ref, key_ref, value_ref, gain_ref, out_ref = refs[chans:]
    home = lax.axis_index("ctx") // group
    cut = slice(*cols)
    for rel in range(chans):
        chan = home ^ rel
        signal = key_ref[chan, :, cut].astype(F32) * value_ref[chan, :, cut].astype(F32)
        total = parts[rel][...].astype(F32) + gain_ref[chan] * signal
        out_ref[chan] = (query_ref[chan, :, cut].astype(F32) * total).astype(BF)


def mix_kernel(chans, plane_ref, weight_ref, own_ref, mid_ref, far_ref, edge_ref, acc_ref, out_ref):
    slots = (own_ref, mid_ref, far_ref, edge_ref)
    outs = acc_ref.shape[0]
    final_col = plane_ref[0] * outs
    part_col = plane_ref[3] * outs

    @pl.loop(0, own_ref.shape[1] // 16)
    def _(index):
        rows = pl.ds(pl.multiple_of(index * 16, 16), 16)
        acc = [None] * outs
        part = [None] * outs
        for slot, ref in enumerate(slots):
            for chan in range(chans):
                value = ref[chan, rows].astype(F32)
                row = plane_ref[slot] * chans + chan
                for feat in range(outs):
                    term = value * weight_ref[row, final_col + feat]
                    acc[feat] = term if acc[feat] is None else acc[feat] + term
                    if slot < 3:
                        term = value * weight_ref[row, part_col + feat]
                        part[feat] = term if part[feat] is None else part[feat] + term
        for feat in range(outs):
            acc_ref[feat, rows] = acc[feat]
            out_ref[feat, rows] = part[feat].astype(BF)


def run_filter(blocks, chans, group, tables, scale):
    left, _, turn, right, _ = tables
    own, big = left.shape[1] // 2, left.shape[2]
    return pl.pallas_call(
        functools.partial(filter_kernel, chans, group, scale),
        out_shape=jax.ShapeDtypeStruct((own, 2 * COLS), F32),
        in_specs=[VMEM] * len(blocks) + [ANY] * 3,
        out_specs=VMEM,
        scratch_shapes=[
            pltpu.VMEM((big, COLS), BF),
            pltpu.VMEM(left.shape[1:], BF),
            pltpu.VMEM(turn.shape[1:], F32),
            pltpu.VMEM(right.shape, BF),
            pltpu.VMEM((own, 2 * COLS), BF),
            pltpu.SemaphoreType.DMA((3,)),
        ],
        compiler_params=params(24),
        cost_estimate=cost(4 * own * COLS * (big + 2 * COLS), 8 * 2**20),
        name="filter_spectrum",
    )(*blocks, left, turn, right)


def run_signal(blocks, spec, chans, group, tables, cols):
    left, _, turn, right, back = tables
    own, big = left.shape[1] // 2, left.shape[2]
    return pl.pallas_call(
        functools.partial(signal_kernel, chans, group, cols),
        out_shape=(
            jax.ShapeDtypeStruct((own, 2 * COLS), BF),
            jax.ShapeDtypeStruct((2 * own, cols[1] - cols[0]), BF),
        ),
        in_specs=[VMEM] * (len(blocks) + 1) + [ANY] * 4,
        out_specs=(VMEM, VMEM),
        scratch_shapes=[
            pltpu.VMEM((big, COLS), BF),
            pltpu.VMEM(left.shape[1:], BF),
            pltpu.VMEM(turn.shape[1:], F32),
            pltpu.VMEM(right.shape, BF),
            pltpu.VMEM(back.shape, BF),
            pltpu.VMEM((own, 2 * COLS), BF),
            pltpu.SemaphoreType.DMA((4,)),
        ],
        compiler_params=params(28),
        cost_estimate=cost(4 * own * COLS * (big + 4 * COLS), 12 * 2**20),
        name="signal_product",
    )(*blocks, spec, left, turn, right, back)


def run_later(prod, group, tables, cols):
    _, _, turn, _, back = tables
    own = prod.shape[0]
    return pl.pallas_call(
        functools.partial(later_kernel, group, cols),
        out_shape=jax.ShapeDtypeStruct((2 * own, cols[1] - cols[0]), BF),
        in_specs=[VMEM, ANY, ANY],
        out_specs=VMEM,
        scratch_shapes=[
            pltpu.VMEM(turn.shape[1:], F32),
            pltpu.VMEM(back.shape, BF),
            pltpu.SemaphoreType.DMA((2,)),
        ],
        compiler_params=params(16),
        cost_estimate=cost(8 * own * COLS * (cols[1] - cols[0]), 6 * 2**20),
        name="back_columns",
    )(prod, turn, back)


def run_position(parts, chans, group, tables):
    table = tables[1]
    out_rows, depth = table.shape[1:]
    cols = parts[0].shape[1]
    rows = out_rows // chans
    return pl.pallas_call(
        functools.partial(position_kernel, chans, group),
        out_shape=(jax.ShapeDtypeStruct((rows, cols), BF),) * chans,
        in_specs=[VMEM] * group + [ANY],
        out_specs=(VMEM,) * chans,
        scratch_shapes=[
            pltpu.VMEM(table.shape[1:], BF),
            pltpu.VMEM((out_rows, cols), BF),
            pltpu.SemaphoreType.DMA((1,)),
        ],
        compiler_params=params(20),
        cost_estimate=cost(2 * out_rows * depth * cols, 4 * 2**20),
        name="back_positions",
    )(*parts, table)


def run_gate(parts, query, key, value, gain, group, cols):
    chans, rows, _ = query.shape
    return pl.pallas_call(
        functools.partial(gate_kernel, group, cols),
        out_shape=jax.ShapeDtypeStruct((chans, rows, cols[1] - cols[0]), BF),
        in_specs=[VMEM] * (chans + 3) + [SMEM],
        out_specs=VMEM,
        compiler_params=params(12),
        cost_estimate=cost(4 * chans * rows * (cols[1] - cols[0]), 2 * 2**20),
        name="gate",
    )(*parts, query, key, value, gain)


def run_mix(planes, weight, own, mid, far, edge):
    chans, rows, cols = own.shape
    outs = weight.shape[1] // 4
    return pl.pallas_call(
        functools.partial(mix_kernel, chans),
        out_shape=(
            jax.ShapeDtypeStruct((outs, rows, cols), F32),
            jax.ShapeDtypeStruct((outs, rows, cols), BF),
        ),
        in_specs=[SMEM, SMEM] + [VMEM] * 4,
        out_specs=(VMEM, VMEM),
        compiler_params=params(12),
        cost_estimate=cost(56 * outs * rows * cols, 3 * 2**20),
        name="mix_features",
    )(planes, weight, own, mid, far, edge)


def line_mix(gated, out_weight):
    plane = lax.axis_index("tp")
    near = plane < 2
    mid_of, far_of, edge_of = jnp.where(near, 2, 1), jnp.where(near, 3, 0), jnp.where(near, 0, 3)
    planes = jnp.stack([plane, mid_of, far_of, edge_of]).astype(jnp.int32)
    weight = out_weight.astype(F32)
    mixed = []
    for own in gated:
        mid = lax.ppermute(own, "tp", [(1, 2), (2, 1)])
        far = lax.ppermute(own, "tp", [(0, 2), (3, 1)])
        edge = lax.ppermute(own, "tp", [(0, 1), (3, 2)])
        acc, send = run_mix(planes, weight, own, mid, far, edge)
        got = lax.ppermute(send, "tp", [(2, 3), (1, 0)])
        mixed.append((acc + got.astype(F32)).astype(BF))
    return mixed


def gather_mix(gated, out_weight):
    plane = lax.axis_index("tp")
    outs = out_weight.shape[1] // lax.axis_size("tp")
    own_cols = lax.dynamic_slice_in_dim(out_weight, plane * outs, outs, 1)
    return [
        jnp.einsum(
            "co,crl->orl",
            own_cols,
            lax.all_gather(own, "tp", axis=0, tiled=True),
            preferred_element_type=F32,
        ).astype(BF)
        for own in gated
    ]


def local(query_gate, key_branch, value_branch, long_filter, skip_gain, out_weight):
    ctx_count = lax.axis_size("ctx")
    chans, tok_count = query_gate.shape
    rows = tok_count // COLS
    group = ctx_count // chans
    length = ctx_count * tok_count
    home = lax.axis_index("ctx") // group
    shape = (chans, rows, COLS)
    tables = make_tables(ctx_count, group, chans, rows)

    def swap(values):
        got = [values[0]]
        for rel in range(1, chans):
            pairs = [
                (group * chip + core, group * (chip ^ rel) + core)
                for chip in range(chans)
                for core in range(group)
            ]
            got.append(lax.ppermute(values[rel], "ctx", pairs))
        return got

    def shift(value, step):
        pairs = [
            (group * chip + core, group * chip + (core + step) % group)
            for chip in range(chans)
            for core in range(group)
        ]
        return lax.ppermute(value, "ctx", pairs)

    def gather_blocks(value):
        relative = [lax.dynamic_index_in_dim(value, home ^ rel, 0, False) for rel in range(chans)]
        got = swap(relative)
        blocks = list(got)
        for step in range(1, group):
            blocks += [shift(part, -step) for part in got]
        return blocks

    filter_blocks = gather_blocks(long_filter.astype(BF).reshape(shape))
    query = query_gate.reshape(shape)
    key = key_branch.reshape(shape)
    value = value_branch.reshape(shape)
    signal_blocks = gather_blocks((key.astype(F32) * value.astype(F32)).astype(BF))
    spec = run_filter(filter_blocks, chans, group, tables, 1.0 / length)
    spans = list(zip(CUTS[:-1], CUTS[1:]))
    prod, first = run_signal(signal_blocks, spec, chans, group, tables, spans[0])
    gated = []
    for span in spans:
        back = first if span == spans[0] else run_later(prod, group, tables, span)
        parts = [back] + [shift(back, -step) for step in range(1, group)]
        got = swap(run_position(parts, chans, group, tables))
        gated.append(run_gate(got, query, key, value, skip_gain, group, span))
    mixed = (line_mix if lax.axis_size("tp") == 4 else gather_mix)(gated, out_weight)
    return jnp.concatenate(mixed, 2).reshape(-1, tok_count)


def solution(mesh):
    placed = (P("tp", "ctx"), P("tp", "ctx"), P("tp", "ctx"), P("tp", "ctx"), P("tp"), P())
    return jax.shard_map(
        local, mesh=mesh, in_specs=placed, out_specs=P("tp", "ctx"), check_vma=False
    )
```

time: 109 us -> 88.8 us (0.81)
  waiting for transfers between devices: 33.1 us -> 24.5 us
  starting transfers between devices: 40.3 us -> 35.3 us
  other arithmetic: 6.7 us -> 3.17 us
  local copies, waits for them, and re-layouts: 8.52 us -> 6.11 us
    all_to_all x4 -> x0, waiting for transfers between devices: 21.3 us -> none  [swap(): lax.all_to_all(value, 'ctx', 0, 0, axis_index_groups=swaps, tiled=True)]
    ppermute x0 -> x12, starting transfers between devices: none -> 16.6 us  [swap(): got.append(lax.ppermute(values[rel], 'ctx', pairs))]
    all_to_all x4 -> x0, starting transfers between devices: 16.2 us -> none  [swap(): lax.all_to_all(value, 'ctx', 0, 0, axis_index_groups=swaps, tiled=True)]
    ppermute x0 -> x12, waiting for transfers between devices: none -> 14.5 us  [swap(): got.append(lax.ppermute(values[rel], 'ctx', pairs))]
    ppermute x2, starting transfers between devices: 9.55 us -> 2.7 us  [line_mix(): edge = lax.ppermute(own, 'tp', [(0, 1), (3, 2)])]
    convert_element_type x4 -> x2, other arithmetic: 6.14 us -> 2.92 us  [the longest x1 1.55 us: local(): filter_blocks = gather_blocks(long_filter.astype(BF).reshape(shape))]
    ppermute x3 -> x10, waiting for transfers between devices: 1.81 us -> 0.03 us  [shift(): return lax.ppermute(value, 'ctx', pairs)]
    convert_element_type x1 -> x0, local copies, waits for them, and re-layouts: 1.6 us -> none  [local(): value = value_branch.reshape(shape).astype(F32)]
  transfers between devices with their start and end apart: 15 -> 30, of which waited for: 9 -> 13; matrix products, arithmetic and copies ran while one was open for 5% -> 2% of each run, Pallas kernels for 8% -> 15%
where the time goes in v2:
time: 88.8 us; the launch traced here: 88.5 us
  starting transfers between devices  35.3 us (40%)
  waiting for transfers between devices  24.5 us (28%)
  Pallas kernels  19 us (21%)
  local copies, waits for them, and re-layouts  6.11 us (7%)
  other arithmetic  3.17 us (4%)
    ppermute x12, starting transfers between devices, swap(): got.append(lax.ppermute(values[rel], 'ctx', pairs))  16.6 us
    ppermute x12, waiting for transfers between devices, swap(): got.append(lax.ppermute(values[rel], 'ctx', pairs))  14.5 us
    ppermute x2, starting transfers between devices, line_mix(): far = lax.ppermute(own, 'tp', [(0, 2), (3, 1)])  10.2 us
    ppermute x2, waiting for transfers between devices, line_mix(): got = lax.ppermute(send, 'tp', [(2, 3), (1, 0)])  6.9 us
    pallas_call x1, Pallas kernels, run_signal(): pl.pallas_call(functools.partial(signal_kernel, chans, group, cols), out_...  5.89 us
    unnamed x27, local copies, waits for them, and re-layouts  5.81 us
    pallas_call x1, Pallas kernels, run_filter(): pl.pallas_call(functools.partial(filter_kernel, chans, group, scale), out...  4.47 us
    pallas_call x2, Pallas kernels, run_mix(): pl.pallas_call(functools.partial(mix_kernel, chans), out_shape=(jax.Shape...  3.9 us
  transfers between devices with their start and end apart: 30, of which 13 were waited for; matrix products, arithmetic and copies ran while one was open for 2% of the time, Pallas kernels for 15%

profile of v2, /device:TPU:0, one launch (start us, length us, event | category | flops | bytes accessed | tf_op | source)
XLA Modules:
  0.0 88.5 jit_solution(18190272091508082917)
XLA Ops:
  0.0 1.6 %convert_element_type.31 = bf16[4,65536]{1,0:T(4,128)(2,1)S(1)} convert(f32[4,65536]{1,0:T(4,128)} %param.14) | non-fusion elementwise | flops 262144 | bytes 1572864 | tf_op jit(solution)/shard_map/convert_element_type | solution.py:409
  1.7 3.0 %collective-permute-start.7 = (bf16[128,512]{1,0:T(8,128)(2,1)S(1)}, bf16[128,512]{1,0:T(8,128)(2,1)S(1)}, u32[]{:S(2)}, u32[]{:S(2)}) collective-permute-start(bf16[128,512]{1,0:T(8,128)(2,1)S(1)} %get-tuple-element.35), channel_id=1, source_target_pairs={{0,8},{4,12},{8,0},{12,4},{16,24},{20,28},{24,16},{28,20},{1,9},{5... | collective-permute-start | bytes 393224 | tf_op jit(solution)/shard_map/ppermute | solution.py:390
  4.7 1.5 %collective-permute-start.8 = (bf16[128,512]{1,0:T(8,128)(2,1)S(1)}, bf16[128,512]{1,0:T(8,128)(2,1)S(1)}, u32[]{:S(2)}, u32[]{:S(2)}) collective-permute-start(bf16[128,512]{1,0:T(8,128)(2,1)S(1)} %get-tuple-element.34), channel_id=1, source_target_pairs={{0,16},{4,20},{8,24},{12,28},{16,0},{20,4},{24,8},{28,12},{1,17},{... | collective-permute-start | bytes 393224 | tf_op jit(solution)/shard_map/ppermute | solution.py:390
  7.7 2.0 %collective-permute-start = (bf16[128,512]{1,0:T(8,128)(2,1)S(1)}, bf16[128,512]{1,0:T(8,128)(2,1)S(1)}, u32[]{:S(2)}, u32[]{:S(2)}) collective-permute-start(bf16[128,512]{1,0:T(8,128)(2,1)S(1)} %get-tuple-element.39), channel_id=1, source_target_pairs={{0,8},{4,12},{8,0},{12,4},{16,24},{20,28},{24,16},{28,20},{1,9},{5... | collective-permute-start | bytes 393224 | tf_op jit(solution)/shard_map/ppermute | solution.py:390
  9.7 1.5 %collective-permute-start.1 = (bf16[128,512]{1,0:T(8,128)(2,1)S(1)}, bf16[128,512]{1,0:T(8,128)(2,1)S(1)}, u32[]{:S(2)}, u32[]{:S(2)}) collective-permute-start(bf16[128,512]{1,0:T(8,128)(2,1)S(1)} %get-tuple-element.38), channel_id=1, source_target_pairs={{0,16},{4,20},{8,24},{12,28},{16,0},{20,4},{24,8},{28,12},{1,17},{... | collective-permute-start | bytes 393224 | tf_op jit(solution)/shard_map/ppermute | solution.py:390
  12.5 1.5 %collective-permute-start.2 = (bf16[128,512]{1,0:T(8,128)(2,1)S(1)}, bf16[128,512]{1,0:T(8,128)(2,1)S(1)}, u32[]{:S(2)}, u32[]{:S(2)}) collective-permute-start(bf16[128,512]{1,0:T(8,128)(2,1)S(1)} %get-tuple-element.37), channel_id=1, source_target_pairs={{0,24},{4,28},{8,16},{12,20},{16,8},{20,12},{24,0},{28,4},{1,25},{... | collective-permute-start | bytes 393224 | tf_op jit(solution)/shard_map/ppermute | solution.py:390
  14.6 2.2 %collective-permute-done.1.refs_2_ = bf16[128,512]{1,0:T(8,128)(2,1)S(1)} collective-permute-done((bf16[128,512]{1,0:T(8,128)(2,1)S(1)}, bf16[128,512]{1,0:T(8,128)(2,1)S(1)}, u32[]{:S(2)}, u32[]{:S(2)}) %collective-permute-start.1) | collective-permute-done | bytes 131104 | tf_op jit(solution)/shard_map/ppermute | solution.py:390
  16.8 1.6 %collective-permute-done.2.refs_3_ = bf16[128,512]{1,0:T(8,128)(2,1)S(1)} collective-permute-done((bf16[128,512]{1,0:T(8,128)(2,1)S(1)}, bf16[128,512]{1,0:T(8,128)(2,1)S(1)}, u32[]{:S(2)}, u32[]{:S(2)}) %collective-permute-start.2) | collective-permute-done | bytes 131104 | tf_op jit(solution)/shard_map/ppermute | solution.py:390
  19.0 2.2 %copy-done = f32[2,2,512,512]{3,2,1,0:T(8,128)S(1)} copy-done((f32[2,2,512,512]{3,2,1,0:T(8,128)S(1)}, f32[2,2,512,512]{3,2,1,0:T(8,128)}, u32[]{:S(2)}) %copy-start) | copy-done | bytes 4194328
  21.2 2.2 %copy-done.3 = bf16[2,1024,1024]{2,1,0:T(8,128)(2,1)S(1)} copy-done((bf16[2,1024,1024]{2,1,0:T(8,128)(2,1)S(1)}, bf16[2,1024,1024]{2,1,0:T(8,128)(2,1)}, u32[]{:S(2)}) %copy-start.3) | copy-done | bytes 4194328
  23.4 4.5 %filter_spectrum.1.refs_8_ = f32[512,1024]{1,0:T(8,128)S(1)} custom-call(bf16[128,512]{1,0:T(8,128)(2,1)S(1)} %get-tuple-element.36.refs_0_, bf16[128,512]{1,0:T(8,128)(2,1)S(1)} %collective-permute-done.7.refs_1_, bf16[128,512]{1,0:T(8,128)(2,1)S(1)} %collective-permute-done.8.refs_2_, bf16[128,512]{1,0:T(8,128)(2,1)S(1)} %collective-permute-done.9.refs_3_, ...), custom_call_target="tpu_custom_call" | custom-call | flops 2147483648 | bytes 8388608 | tf_op jit(solution)/shard_map/filter_spectrum/pallas_call | solution.py:225
  27.9 5.9 %signal_product.1 = (bf16[512,1024]{1,0:T(8,128)(2,1)S(1)}, bf16[1024,256]{1,0:T(8,128)(2,1)S(1)}) custom-call(bf16[128,512]{1,0:T(8,128)(2,1)S(1)} %get-tuple-element.40.refs_0_, bf16[128,512]{1,0:T(8,128)(2,1)S(1)} %collective-permute-done.refs_1_, bf16[128,512]{1,0:T(8,128)(2,1)S(1)} %collective-permute-done.1.refs_2_, ...), custom_call_target="tpu_custom_call" | custom-call | flops 3221225472 | bytes 12582912 | tf_op jit(solution)/shard_map/signal_product/pallas_call | solution.py:247
  34.3 1.6 %back_columns.1.refs_0_ = bf16[1024,256]{1,0:T(8,128)(2,1)S(1)} custom-call(bf16[512,1024]{1,0:T(8,128)(2,1)S(1)} %get-tuple-element.26.prod_ref, f32[2,2,512,512]{3,2,1,0:T(8,128)S(1)} %copy-done.1, bf16[1024,1024]{1,0:T(8,128)(2,1)S(1)} %copy-done.5), custom_call_target="tpu_custom_call" | custom-call | flops 536870912 | bytes 6291456 | tf_op jit(solution)/shard_map/back_columns/pallas_call | solution.py:273
  42.3 1.9 %collective-permute-done.17.refs_3_ = bf16[128,256]{1,0:T(8,128)(2,1)S(1)} collective-permute-done((bf16[128,256]{1,0:T(8,128)(2,1)S(1)}, bf16[128,256]{1,0:T(8,128)(2,1)S(1)}, u32[]{:S(2)}, u32[]{:S(2)}) %collective-permute-start.17) | collective-permute-done | bytes 65568 | tf_op jit(solution)/shard_map/ppermute | solution.py:390
  45.7 6.2 %collective-permute-start.19 = (bf16[4,128,256]{2,1,0:T(8,128)(2,1)S(1)}, bf16[4,128,256]{2,1,0:T(8,128)(2,1)S(1)}, u32[]{:S(2)}, u32[]{:S(2)}) collective-permute-start(bf16[4,128,256]{2,1,0:T(8,128)(2,1)S(1)} %gate.2.own_ref), channel_id=1, source_target_pairs={{0,2},{3,1},{4,6},{7,5},{8,10},{11,9},{12,14},{15,13},{16,18},{19,... | collective-permute-start | bytes 786440 | tf_op jit(solution)/shard_map/ppermute | solution.py:349
  54.2 1.6 %collective-permute-start.23 = (bf16[128,256]{1,0:T(8,128)(2,1)S(1)}, bf16[128,256]{1,0:T(8,128)(2,1)S(1)}, u32[]{:S(2)}, u32[]{:S(2)}) collective-permute-start(bf16[128,256]{1,0:T(8,128)(2,1)S(1)} %get-tuple-element.28), channel_id=1, source_target_pairs={{0,8},{4,12},{8,0},{12,4},{16,24},{20,28},{24,16},{28,20},{1,9},{5... | collective-permute-start | bytes 196616 | tf_op jit(solution)/shard_map/ppermute | solution.py:390
  56.3 2.3 %collective-permute-done.23.refs_1_ = bf16[128,256]{1,0:T(8,128)(2,1)S(1)} collective-permute-done((bf16[128,256]{1,0:T(8,128)(2,1)S(1)}, bf16[128,256]{1,0:T(8,128)(2,1)S(1)}, u32[]{:S(2)}, u32[]{:S(2)}) %collective-permute-start.23) | collective-permute-done | bytes 65568 | tf_op jit(solution)/shard_map/ppermute | solution.py:390
  60.5 3.2 %collective-permute-done.25.refs_3_ = bf16[128,256]{1,0:T(8,128)(2,1)S(1)} collective-permute-done((bf16[128,256]{1,0:T(8,128)(2,1)S(1)}, bf16[128,256]{1,0:T(8,128)(2,1)S(1)}, u32[]{:S(2)}, u32[]{:S(2)}) %collective-permute-start.25) | collective-permute-done | bytes 65568 | tf_op jit(solution)/shard_map/ppermute | solution.py:390
  65.1 4.0 %collective-permute-start.27 = (bf16[4,128,256]{2,1,0:T(8,128)(2,1)S(1)}, bf16[4,128,256]{2,1,0:T(8,128)(2,1)S(1)}, u32[]{:S(2)}, u32[]{:S(2)}) collective-permute-start(bf16[4,128,256]{2,1,0:T(8,128)(2,1)S(1)} %gate.3.own_ref), channel_id=1, source_target_pairs={{0,2},{3,1},{4,6},{7,5},{8,10},{11,9},{12,14},{15,13},{16,18},{19,... | collective-permute-start | bytes 786440 | tf_op jit(solution)/shard_map/ppermute | solution.py:349
  70.5 2.0 %mix_features.2 = (f32[4,128,256]{2,1,0:T(8,128)S(1)}, bf16[4,128,256]{2,1,0:T(8,128)(2,1)S(1)}) custom-call(s32[4]{0:T(128)S(1)} %pad_add_fusion.plane_ref, f32[16,16]{1,0:T(8,128)S(1)} %convert_element_type.27.weight_ref, bf16[4,128,256]{2,1,0:T(8,128)(2,1)S(1)} %gate.2.own_ref, bf16[4,128,256]{2,1,0:T(8,128)(2,1)S(1)} %collective-permute-done.18.mid_ref, ...), custom_call_target="tpu_custom_call" | custom-call | flops 7340032 | bytes 3145728 | tf_op jit(solution)/shard_map/mix_features/pallas_call | solution.py:326
  74.1 2.8 %collective-permute-done.28.edge_ref = bf16[4,128,256]{2,1,0:T(8,128)(2,1)S(1)} collective-permute-done((bf16[4,128,256]{2,1,0:T(8,128)(2,1)S(1)}, bf16[4,128,256]{2,1,0:T(8,128)(2,1)S(1)}, u32[]{:S(2)}, u32[]{:S(2)}) %collective-permute-start.28) | collective-permute-done | bytes 262176 | tf_op jit(solution)/shard_map/ppermute | solution.py:350
  76.9 1.9 %mix_features.3 = (f32[4,128,256]{2,1,0:T(8,128)S(1)}, bf16[4,128,256]{2,1,0:T(8,128)(2,1)S(1)}) custom-call(s32[4]{0:T(128)S(1)} %pad_add_fusion.plane_ref, f32[16,16]{1,0:T(8,128)S(1)} %convert_element_type.27.weight_ref, bf16[4,128,256]{2,1,0:T(8,128)(2,1)S(1)} %gate.3.own_ref, bf16[4,128,256]{2,1,0:T(8,128)(2,1)S(1)} %collective-permute-done.26.mid_ref, ...), custom_call_target="tpu_custom_call" | custom-call | flops 7340032 | bytes 3145728 | tf_op jit(solution)/shard_map/mix_features/pallas_call | solution.py:326
  80.2 2.2 %collective-permute-done.21 = bf16[4,128,256]{2,1,0:T(8,128)(2,1)S(1)} collective-permute-done((bf16[4,128,256]{2,1,0:T(8,128)(2,1)S(1)}, bf16[4,128,256]{2,1,0:T(8,128)(2,1)S(1)}, u32[]{:S(2)}, u32[]{:S(2)}) %collective-permute-start.21) | collective-permute-done | bytes 262176 | tf_op jit(solution)/shard_map/ppermute | solution.py:352
  82.5 4.7 %collective-permute-done.29 = bf16[4,128,256]{2,1,0:T(8,128)(2,1)S(1)} collective-permute-done((bf16[4,128,256]{2,1,0:T(8,128)(2,1)S(1)}, bf16[4,128,256]{2,1,0:T(8,128)(2,1)S(1)}, u32[]{:S(2)}, u32[]{:S(2)}) %collective-permute-start.29) | collective-permute-done | bytes 262176 | tf_op jit(solution)/shard_map/ppermute | solution.py:352
  (82 shorter events, 24.1 us)
Async XLA Ops:
  1.7 8.0 %collective-permute-start.7 = (bf16[128,512]{1,0:T(8,128)(2,1)S(1)}, bf16[128,512]{1,0:T(8,128)(2,1)S(1)}, u32[]{:S(2)}, u32[]{:S(2)}) collective-permute-start(bf16[128,512]{1,0:T(8,128)(2,1)S(1)} %get-tuple-element.35), channel_id=1, source_target_pairs={{0,8},{4,12},{8,0},{12,4},{16,24},{20,28},{24,16},{28,20},{1,9},{5... | collective-permute-start | bytes 393224 | tf_op jit(solution)/shard_map/ppermute | solution.py:390
  4.7 7.8 %collective-permute-start.8 = (bf16[128,512]{1,0:T(8,128)(2,1)S(1)}, bf16[128,512]{1,0:T(8,128)(2,1)S(1)}, u32[]{:S(2)}, u32[]{:S(2)}) collective-permute-start(bf16[128,512]{1,0:T(8,128)(2,1)S(1)} %get-tuple-element.34), channel_id=1, source_target_pairs={{0,16},{4,20},{8,24},{12,28},{16,0},{20,4},{24,8},{28,12},{1,17},{... | collective-permute-start | bytes 393224 | tf_op jit(solution)/shard_map/ppermute | solution.py:390
  6.3 7.7 %collective-permute-start.9 = (bf16[128,512]{1,0:T(8,128)(2,1)S(1)}, bf16[128,512]{1,0:T(8,128)(2,1)S(1)}, u32[]{:S(2)}, u32[]{:S(2)}) collective-permute-start(bf16[128,512]{1,0:T(8,128)(2,1)S(1)} %get-tuple-element.33), channel_id=1, source_target_pairs={{0,24},{4,28},{8,16},{12,20},{16,8},{20,12},{24,0},{28,4},{1,25},{... | collective-permute-start | bytes 393224 | tf_op jit(solution)/shard_map/ppermute | solution.py:390
  6.3 7.7 %collective-permute-start.10 = (bf16[128,512]{1,0:T(8,128)(2,1)S(1)}, bf16[128,512]{1,0:T(8,128)(2,1)S(1)}, u32[]{:S(2)}, u32[]{:S(2)}) collective-permute-start(bf16[128,512]{1,0:T(8,128)(2,1)S(1)} %get-tuple-element.36.refs_0_), channel_id=1, source_target_pairs={{0,4},{4,0},{8,12},{12,8},{16,20},{20,16},{24,28},{28,24},{1,5},{5... | collective-permute-start | bytes 393224 | tf_op jit(solution)/shard_map/ppermute | solution.py:399
  7.7 6.8 %collective-permute-start = (bf16[128,512]{1,0:T(8,128)(2,1)S(1)}, bf16[128,512]{1,0:T(8,128)(2,1)S(1)}, u32[]{:S(2)}, u32[]{:S(2)}) collective-permute-start(bf16[128,512]{1,0:T(8,128)(2,1)S(1)} %get-tuple-element.39), channel_id=1, source_target_pairs={{0,8},{4,12},{8,0},{12,4},{16,24},{20,28},{24,16},{28,20},{1,9},{5... | collective-permute-start | bytes 393224 | tf_op jit(solution)/shard_map/ppermute | solution.py:390
  9.7 7.0 %collective-permute-start.1 = (bf16[128,512]{1,0:T(8,128)(2,1)S(1)}, bf16[128,512]{1,0:T(8,128)(2,1)S(1)}, u32[]{:S(2)}, u32[]{:S(2)}) collective-permute-start(bf16[128,512]{1,0:T(8,128)(2,1)S(1)} %get-tuple-element.38), channel_id=1, source_target_pairs={{0,16},{4,20},{8,24},{12,28},{16,0},{20,4},{24,8},{28,12},{1,17},{... | collective-permute-start | bytes 393224 | tf_op jit(solution)/shard_map/ppermute | solution.py:390
  12.5 5.9 %collective-permute-start.2 = (bf16[128,512]{1,0:T(8,128)(2,1)S(1)}, bf16[128,512]{1,0:T(8,128)(2,1)S(1)}, u32[]{:S(2)}, u32[]{:S(2)}) collective-permute-start(bf16[128,512]{1,0:T(8,128)(2,1)S(1)} %get-tuple-element.37), channel_id=1, source_target_pairs={{0,24},{4,28},{8,16},{12,20},{16,8},{20,12},{24,0},{28,4},{1,25},{... | collective-permute-start | bytes 393224 | tf_op jit(solution)/shard_map/ppermute | solution.py:390
  14.0 4.9 %collective-permute-start.12 = (bf16[128,512]{1,0:T(8,128)(2,1)S(1)}, bf16[128,512]{1,0:T(8,128)(2,1)S(1)}, u32[]{:S(2)}, u32[]{:S(2)}) collective-permute-start(bf16[128,512]{1,0:T(8,128)(2,1)S(1)} %collective-permute-done.8.refs_2_), channel_id=1, source_target_pairs={{0,4},{4,0},{8,12},{12,8},{16,20},{20,16},{24,28},{28,24},{1,5},{5... | collective-permute-start | bytes 393224 | tf_op jit(solution)/shard_map/ppermute | solution.py:399
  16.8 11.1 %collective-permute-start.3 = (bf16[128,512]{1,0:T(8,128)(2,1)S(1)}, bf16[128,512]{1,0:T(8,128)(2,1)S(1)}, u32[]{:S(2)}, u32[]{:S(2)}) collective-permute-start(bf16[128,512]{1,0:T(8,128)(2,1)S(1)} %get-tuple-element.40.refs_0_), channel_id=1, source_target_pairs={{0,4},{4,0},{8,12},{12,8},{16,20},{20,16},{24,28},{28,24},{1,5},{5... | collective-permute-start | bytes 393224 | tf_op jit(solution)/shard_map/ppermute | solution.py:399
  18.4 9.5 %collective-permute-start.4 = (bf16[128,512]{1,0:T(8,128)(2,1)S(1)}, bf16[128,512]{1,0:T(8,128)(2,1)S(1)}, u32[]{:S(2)}, u32[]{:S(2)}) collective-permute-start(bf16[128,512]{1,0:T(8,128)(2,1)S(1)} %collective-permute-done.refs_1_), channel_id=1, source_target_pairs={{0,4},{4,0},{8,12},{12,8},{16,20},{20,16},{24,28},{28,24},{1,5},{5... | collective-permute-start | bytes 393224 | tf_op jit(solution)/shard_map/ppermute | solution.py:399
  18.4 9.5 %collective-permute-start.5 = (bf16[128,512]{1,0:T(8,128)(2,1)S(1)}, bf16[128,512]{1,0:T(8,128)(2,1)S(1)}, u32[]{:S(2)}, u32[]{:S(2)}) collective-permute-start(bf16[128,512]{1,0:T(8,128)(2,1)S(1)} %collective-permute-done.1.refs_2_), channel_id=1, source_target_pairs={{0,4},{4,0},{8,12},{12,8},{16,20},{20,16},{24,28},{28,24},{1,5},{5... | collective-permute-start | bytes 393224 | tf_op jit(solution)/shard_map/ppermute | solution.py:399
  18.9 9.0 %collective-permute-start.6 = (bf16[128,512]{1,0:T(8,128)(2,1)S(1)}, bf16[128,512]{1,0:T(8,128)(2,1)S(1)}, u32[]{:S(2)}, u32[]{:S(2)}) collective-permute-start(bf16[128,512]{1,0:T(8,128)(2,1)S(1)} %collective-permute-done.2.refs_3_), channel_id=1, source_target_pairs={{0,4},{4,0},{8,12},{12,8},{16,20},{20,16},{24,28},{28,24},{1,5},{5... | collective-permute-start | bytes 393224 | tf_op jit(solution)/shard_map/ppermute | solution.py:399
  35.9 17.4 %collective-permute-start.22 = (bf16[1024,256]{1,0:T(8,128)(2,1)S(1)}, bf16[1024,256]{1,0:T(8,128)(2,1)S(1)}, u32[]{:S(2)}, u32[]{:S(2)}) collective-permute-start(bf16[1024,256]{1,0:T(8,128)(2,1)S(1)} %back_columns.1.refs_0_), channel_id=1, source_target_pairs={{0,4},{4,0},{8,12},{12,8},{16,20},{20,16},{24,28},{28,24},{1,5},{5... | collective-permute-start | bytes 1572872 | tf_op jit(solution)/shard_map/ppermute | solution.py:399
  39.1 5.2 %collective-permute-start.17 = (bf16[128,256]{1,0:T(8,128)(2,1)S(1)}, bf16[128,256]{1,0:T(8,128)(2,1)S(1)}, u32[]{:S(2)}, u32[]{:S(2)}) collective-permute-start(bf16[128,256]{1,0:T(8,128)(2,1)S(1)} %get-tuple-element.23), channel_id=1, source_target_pairs={{0,24},{4,28},{8,16},{12,20},{16,8},{20,12},{24,0},{28,4},{1,25},{... | collective-permute-start | bytes 196616 | tf_op jit(solution)/shard_map/ppermute | solution.py:390
  45.0 24.1 %collective-permute-start.18 = (bf16[4,128,256]{2,1,0:T(8,128)(2,1)S(1)}, bf16[4,128,256]{2,1,0:T(8,128)(2,1)S(1)}, u32[]{:S(2)}, u32[]{:S(2)}) collective-permute-start(bf16[4,128,256]{2,1,0:T(8,128)(2,1)S(1)} %gate.2.own_ref), channel_id=1, source_target_pairs={{1,2},{2,1},{5,6},{6,5},{9,10},{10,9},{13,14},{14,13},{17,18},{18,... | collective-permute-start | bytes 786440 | tf_op jit(solution)/shard_map/ppermute | solution.py:348
  45.7 24.8 %collective-permute-start.19 = (bf16[4,128,256]{2,1,0:T(8,128)(2,1)S(1)}, bf16[4,128,256]{2,1,0:T(8,128)(2,1)S(1)}, u32[]{:S(2)}, u32[]{:S(2)}) collective-permute-start(bf16[4,128,256]{2,1,0:T(8,128)(2,1)S(1)} %gate.2.own_ref), channel_id=1, source_target_pairs={{0,2},{3,1},{4,6},{7,5},{8,10},{11,9},{12,14},{15,13},{16,18},{19,... | collective-permute-start | bytes 786440 | tf_op jit(solution)/shard_map/ppermute | solution.py:349
  51.9 18.6 %collective-permute-start.20 = (bf16[4,128,256]{2,1,0:T(8,128)(2,1)S(1)}, bf16[4,128,256]{2,1,0:T(8,128)(2,1)S(1)}, u32[]{:S(2)}, u32[]{:S(2)}) collective-permute-start(bf16[4,128,256]{2,1,0:T(8,128)(2,1)S(1)} %gate.2.own_ref), channel_id=1, source_target_pairs={{0,1},{3,2},{4,5},{7,6},{8,9},{11,10},{12,13},{15,14},{16,17},{19,... | collective-permute-start | bytes 786440 | tf_op jit(solution)/shard_map/ppermute | solution.py:350
  55.8 4.7 %collective-permute-start.24 = (bf16[128,256]{1,0:T(8,128)(2,1)S(1)}, bf16[128,256]{1,0:T(8,128)(2,1)S(1)}, u32[]{:S(2)}, u32[]{:S(2)}) collective-permute-start(bf16[128,256]{1,0:T(8,128)(2,1)S(1)} %get-tuple-element.29), channel_id=1, source_target_pairs={{0,16},{4,20},{8,24},{12,28},{16,0},{20,4},{24,8},{28,12},{1,17},{... | collective-permute-start | bytes 196616 | tf_op jit(solution)/shard_map/ppermute | solution.py:390
  58.5 5.2 %collective-permute-start.25 = (bf16[128,256]{1,0:T(8,128)(2,1)S(1)}, bf16[128,256]{1,0:T(8,128)(2,1)S(1)}, u32[]{:S(2)}, u32[]{:S(2)}) collective-permute-start(bf16[128,256]{1,0:T(8,128)(2,1)S(1)} %get-tuple-element.30), channel_id=1, source_target_pairs={{0,24},{4,28},{8,16},{12,20},{16,8},{20,12},{24,0},{28,4},{1,25},{... | collective-permute-start | bytes 196616 | tf_op jit(solution)/shard_map/ppermute | solution.py:390
  64.4 9.4 %collective-permute-start.26 = (bf16[4,128,256]{2,1,0:T(8,128)(2,1)S(1)}, bf16[4,128,256]{2,1,0:T(8,128)(2,1)S(1)}, u32[]{:S(2)}, u32[]{:S(2)}) collective-permute-start(bf16[4,128,256]{2,1,0:T(8,128)(2,1)S(1)} %gate.3.own_ref), channel_id=1, source_target_pairs={{1,2},{2,1},{5,6},{6,5},{9,10},{10,9},{13,14},{14,13},{17,18},{18,... | collective-permute-start | bytes 786440 | tf_op jit(solution)/shard_map/ppermute | solution.py:348
  65.1 9.0 %collective-permute-start.27 = (bf16[4,128,256]{2,1,0:T(8,128)(2,1)S(1)}, bf16[4,128,256]{2,1,0:T(8,128)(2,1)S(1)}, u32[]{:S(2)}, u32[]{:S(2)}) collective-permute-start(bf16[4,128,256]{2,1,0:T(8,128)(2,1)S(1)} %gate.3.own_ref), channel_id=1, source_target_pairs={{0,2},{3,1},{4,6},{7,5},{8,10},{11,9},{12,14},{15,13},{16,18},{19,... | collective-permute-start | bytes 786440 | tf_op jit(solution)/shard_map/ppermute | solution.py:349
  69.1 7.8 %collective-permute-start.28 = (bf16[4,128,256]{2,1,0:T(8,128)(2,1)S(1)}, bf16[4,128,256]{2,1,0:T(8,128)(2,1)S(1)}, u32[]{:S(2)}, u32[]{:S(2)}) collective-permute-start(bf16[4,128,256]{2,1,0:T(8,128)(2,1)S(1)} %gate.3.own_ref), channel_id=1, source_target_pairs={{0,1},{3,2},{4,5},{7,6},{8,9},{11,10},{12,13},{15,14},{16,17},{19,... | collective-permute-start | bytes 786440 | tf_op jit(solution)/shard_map/ppermute | solution.py:350
  72.5 9.9 %collective-permute-start.21 = (bf16[4,128,256]{2,1,0:T(8,128)(2,1)S(1)}, bf16[4,128,256]{2,1,0:T(8,128)(2,1)S(1)}, u32[]{:S(2)}, u32[]{:S(2)}) collective-permute-start(bf16[4,128,256]{2,1,0:T(8,128)(2,1)S(1)} %get-tuple-element.25), channel_id=1, source_target_pairs={{2,3},{1,0},{6,7},{5,4},{10,11},{9,8},{14,15},{13,12},{18,19},{17,... | collective-permute-start | bytes 786440 | tf_op jit(solution)/shard_map/ppermute | solution.py:352
  78.9 8.3 %collective-permute-start.29 = (bf16[4,128,256]{2,1,0:T(8,128)(2,1)S(1)}, bf16[4,128,256]{2,1,0:T(8,128)(2,1)S(1)}, u32[]{:S(2)}, u32[]{:S(2)}) collective-permute-start(bf16[4,128,256]{2,1,0:T(8,128)(2,1)S(1)} %get-tuple-element.32), channel_id=1, source_target_pairs={{2,3},{1,0},{6,7},{5,4},{10,11},{9,8},{14,15},{13,12},{18,19},{17,... | collective-permute-start | bytes 786440 | tf_op jit(solution)/shard_map/ppermute | solution.py:352
  (18 other events, 111.4 us)

commit v3 on v0

v3 whole, which is shorter than its diff:
```python
import functools

import jax
import jax.numpy as jnp
import numpy as np
from jax import lax
from jax.experimental import pallas as pl
from jax.experimental.pallas import tpu as pltpu
from jax.sharding import PartitionSpec as P

COLS = 512
STEP = 32
CUTS = (0, 256, 512)
BF = jnp.bfloat16
F32 = jnp.float32
VMEM = pl.BlockSpec(memory_space=pltpu.VMEM)
SMEM = pl.BlockSpec(memory_space=pltpu.SMEM)
HBM = pl.BlockSpec(memory_space=pltpu.HBM)


def make_tables(ctx_count, group, chans, rows):
    big = ctx_count * rows
    own = big // group
    length = big * COLS
    k_one = np.arange(big, dtype=np.int64)
    n_one = np.arange(big, dtype=np.int64)
    angle = 2 * np.pi / (4 * big) * ((4 * k_one[:, None] + 1) * n_one[None, :] % (4 * big))
    both = np.stack([np.cos(angle), -np.sin(angle)], 0)
    both = both.reshape(2, group, own, chans, group, rows)
    left = np.empty((group, 2 * own, group, chans * rows))
    back_left = np.empty((group, chans * rows, group, 2 * own))
    for sub in range(group):
        for step in range(group):
            other = (sub + step) % group
            left[sub, :, step] = both[:, sub, :, :, other].reshape(2 * own, -1)
            back_left[sub, :, step] = both[:, other, :, :, sub].reshape(2 * own, -1).T
    n_two = np.arange(COLS, dtype=np.int64)
    coarse = STEP * np.arange(big // STEP, dtype=np.int64)
    fine = np.arange(STEP, dtype=np.int64)
    angle = 2 * np.pi / (4 * length) * (4 * coarse[:, None] * n_two[None, :] % (4 * length))
    coarse = np.stack([np.cos(angle), -np.sin(angle)], 0).reshape(2, group, own // STEP, COLS)
    coarse = np.ascontiguousarray(coarse.transpose(1, 0, 2, 3))
    angle = 2 * np.pi / (4 * length) * ((4 * fine[:, None] + 1) * n_two[None, :] % (4 * length))
    fine = np.stack([np.cos(angle), -np.sin(angle)], 0)
    angle = 2 * np.pi / COLS * (n_two[:, None] * n_two[None, :] % COLS)
    return (
        left.reshape(group, 2 * own, big).astype(BF),
        back_left.reshape(group, chans * rows, 2 * big).astype(BF),
        np.concatenate([np.cos(angle), np.sin(angle)], 0).astype(BF),
        coarse.astype(np.float32),
        fine.astype(np.float32),
    )


def dot(left, right):
    return jnp.dot(left, right, preferred_element_type=F32)


def cost(flops):
    return pl.CostEstimate(flops=int(flops), bytes_accessed=0, transcendentals=0)


def params(mib):
    return pltpu.CompilerParams(vmem_limit_bytes=mib * 2**20)


def tables_kernel(group, *refs):
    left_hbm, back_hbm, wave_hbm, coarse_hbm, fine_hbm = refs[:5]
    left_ref, back_ref, wave_ref, turn_ref, coarse_ref, fine_ref, sems = refs[5:]
    sub = lax.rem(lax.axis_index("ctx"), group)
    copies = [
        pltpu.make_async_copy(coarse_hbm.at[sub], coarse_ref, sems.at[0]),
        pltpu.make_async_copy(fine_hbm, fine_ref, sems.at[1]),
        pltpu.make_async_copy(left_hbm.at[sub], left_ref, sems.at[2]),
        pltpu.make_async_copy(wave_hbm, wave_ref, sems.at[3]),
        pltpu.make_async_copy(back_hbm.at[sub], back_ref, sems.at[4]),
    ]
    for copy in copies:
        copy.start()
    copies[0].wait()
    copies[1].wait()
    fine_re, fine_im = fine_ref[0], fine_ref[1]
    for number in range(coarse_ref.shape[1]):
        tab_re = coarse_ref[0, number : number + 1]
        tab_im = coarse_ref[1, number : number + 1]
        cut = slice(number * STEP, (number + 1) * STEP)
        turn_ref[0, cut] = fine_re * tab_re - fine_im * tab_im
        turn_ref[1, cut] = fine_re * tab_im + fine_im * tab_re
    for copy in copies[2:]:
        copy.wait()


def run_tables(group, tables):
    left, back, wave, coarse, fine = tables
    own = left.shape[1] // 2
    return pl.pallas_call(
        functools.partial(tables_kernel, group),
        out_shape=(
            jax.ShapeDtypeStruct(left.shape[1:], BF),
            jax.ShapeDtypeStruct(back.shape[1:], BF),
            jax.ShapeDtypeStruct(wave.shape, BF),
            jax.ShapeDtypeStruct((2, own, COLS), F32),
        ),
        in_specs=[HBM] * 5,
        out_specs=(VMEM,) * 4,
        scratch_shapes=[
            pltpu.VMEM(coarse.shape[1:], F32),
            pltpu.VMEM(fine.shape, F32),
            pltpu.SemaphoreType.DMA((5,)),
        ],
        compiler_params=params(40),
        cost_estimate=cost(3e9),
        name="load_tables",
    )(*tables)


def spectrum_kernel(chans, group, scale, *refs):
    count = chans * group
    blocks, (left_ref, wave_ref, turn_ref, out_ref) = refs[:count], refs[count : count + 4]
    x_ref, mid_ref, prod_ref, spec_ref = refs[count + 4 :]
    rows = blocks[0].shape[1]
    own = mid_ref.shape[0]
    home = lax.axis_index("ctx") // group
    for step in range(group):
        for rel in range(chans):
            first = pl.multiple_of((step * chans + (home ^ rel)) * rows, rows)
            for kind in range(2):
                x_ref[kind, pl.ds(first, rows)] = blocks[step * chans + rel][kind]
    for kind in range(2):
        for tile in range(0, COLS, 256):
            cut = slice(tile, tile + 256)
            val = dot(left_ref[...], x_ref[kind, :, cut])
            val_re, val_im = val[:own], val[own:]
            tab_re, tab_im = turn_ref[0, :, cut], turn_ref[1, :, cut]
            mid_re = (val_re * tab_re - val_im * tab_im).astype(BF)
            mid_ref[:, cut] = mid_re
            mid_ref[:, COLS + tile : COLS + tile + 256] = (
                val_re * tab_im + val_im * tab_re
            ).astype(BF)
            mid_ref[:, 2 * COLS + tile : 2 * COLS + tile + 256] = -mid_re
        for tile in range(0, COLS, 256):
            cut = slice(tile, tile + 256)
            out_re = dot(mid_ref[:, : 2 * COLS], wave_ref[:, cut])
            out_im = dot(mid_ref[:, COLS:], wave_ref[:, cut])
            if kind == 0:
                spec_ref[0, :, cut] = out_re * scale
                spec_ref[1, :, cut] = out_im * scale
            else:
                fil_re, fil_im = spec_ref[0, :, cut], spec_ref[1, :, cut]
                prod_im = (out_re * fil_im + out_im * fil_re).astype(BF)
                prod_ref[:, cut] = prod_im
                prod_ref[:, COLS + tile : COLS + tile + 256] = (
                    out_re * fil_re - out_im * fil_im
                ).astype(BF)
                prod_ref[:, 2 * COLS + tile : 2 * COLS + tile + 256] = -prod_im
    for tile in range(0, COLS, 256):
        cut = slice(tile, tile + 256)
        val_im = dot(prod_ref[:, : 2 * COLS], wave_ref[:, cut])
        val_re = dot(prod_ref[:, COLS:], wave_ref[:, cut])
        tab_re, tab_im = turn_ref[0, :, cut], turn_ref[1, :, cut]
        out_ref[:own, cut] = (val_re * tab_re + val_im * tab_im).astype(BF)
        out_ref[own:, cut] = (val_im * tab_re - val_re * tab_im).astype(BF)


def position_kernel(chans, group, *refs):
    parts, table_ref = refs[:group], refs[group]
    outs, sum_ref = refs[group + 1 : group + 1 + chans], refs[group + 1 + chans]
    home = lax.axis_index("ctx") // group
    depth = parts[0].shape[0]
    total = dot(table_ref[:, :depth], parts[0][...])
    for step in range(1, group):
        total += dot(table_ref[:, step * depth : (step + 1) * depth], parts[step][...])
    sum_ref[...] = total.astype(BF)
    rows = outs[0].shape[0]
    for rel in range(chans):
        outs[rel][...] = sum_ref[pl.ds(pl.multiple_of((home ^ rel) * rows, rows), rows)]


def gate_kernel(chans, group, *refs):
    parts = refs[:chans]
    query_ref, key_ref, value_ref, gain_ref = refs[chans : chans + 4]
    outs = refs[chans + 4 :]
    home = lax.axis_index("ctx") // group
    for rel in range(chans):
        chan = home ^ rel
        signal = key_ref[chan].astype(F32) * value_ref[chan].astype(F32)
        total = parts[rel][...].astype(F32) + gain_ref[chan] * signal
        gated = (query_ref[chan].astype(F32) * total).astype(BF)
        for out, low, high in zip(outs, CUTS[:-1], CUTS[1:]):
            out[chan] = gated[:, low:high]


def run_spectrum(blocks, chans, group, tables, scale):
    left, _, wave, turn = tables
    own, big = left.shape[0] // 2, left.shape[1]
    return pl.pallas_call(
        functools.partial(spectrum_kernel, chans, group, scale),
        out_shape=jax.ShapeDtypeStruct((2 * own, COLS), BF),
        in_specs=[VMEM] * (len(blocks) + 3),
        out_specs=VMEM,
        scratch_shapes=[
            pltpu.VMEM((2, big, COLS), BF),
            pltpu.VMEM((own, 3 * COLS), BF),
            pltpu.VMEM((own, 3 * COLS), BF),
            pltpu.VMEM((2, own, COLS), F32),
        ],
        compiler_params=params(20),
        cost_estimate=cost(8 * own * COLS * (big + 3 * COLS)),
        name="spectrum_product",
    )(*blocks, left, wave, turn)


def run_position(parts, chans, group, table):
    out_rows, depth = table.shape
    rows = out_rows // chans
    return pl.pallas_call(
        functools.partial(position_kernel, chans, group),
        out_shape=(jax.ShapeDtypeStruct((rows, COLS), BF),) * chans,
        in_specs=[VMEM] * (group + 1),
        out_specs=(VMEM,) * chans,
        scratch_shapes=[pltpu.VMEM((out_rows, COLS), BF)],
        compiler_params=params(12),
        cost_estimate=cost(2 * out_rows * depth * COLS),
        name="back_positions",
    )(*parts, table)


def run_gate(parts, query, key, value, gain, group):
    chans, rows, _ = query.shape
    return pl.pallas_call(
        functools.partial(gate_kernel, chans, group),
        out_shape=tuple(
            jax.ShapeDtypeStruct((chans, rows, high - low), BF)
            for low, high in zip(CUTS[:-1], CUTS[1:])
        ),
        in_specs=[VMEM] * (chans + 3) + [SMEM],
        out_specs=(VMEM,) * (len(CUTS) - 1),
        compiler_params=params(12),
        cost_estimate=cost(4 * chans * rows * COLS),
        name="gate",
    )(*parts, query, key, value, gain)


def mix_kernel(chans, slots, outputs, plane_ref, weight_ref, *refs):
    count = len(slots)
    feats = refs[count].shape[0]

    @pl.loop(0, refs[0].shape[1] // 16)
    def _(index):
        rows = pl.ds(pl.multiple_of(index * 16, 16), 16)
        sums = [[None] * feats for _ in outputs]
        for slot, ref in zip(slots, refs[:count]):
            for chan in range(chans):
                value = ref[chan, rows].astype(F32)
                row = plane_ref[slot] * chans + chan
                for out, total in zip(outputs, sums):
                    for feat in range(feats):
                        term = value * weight_ref[row, plane_ref[out[0]] * feats + feat]
                        total[feat] = term if total[feat] is None else total[feat] + term
        for ref, total in zip(refs[count:], sums):
            for feat in range(feats):
                ref[feat, rows] = total[feat].astype(ref.dtype)


def run_mix(planes, weight, slots, outputs, values):
    chans, rows, cols = values[0].shape
    feats = weight.shape[1] // 4
    size = feats * rows * cols
    return pl.pallas_call(
        functools.partial(mix_kernel, chans, slots, outputs),
        out_shape=tuple(jax.ShapeDtypeStruct((feats, rows, cols), out[1]) for out in outputs),
        in_specs=[SMEM, SMEM] + [VMEM] * len(slots),
        out_specs=(VMEM,) * len(outputs),
        compiler_params=params(12),
        cost_estimate=cost(2 * chans * len(slots) * len(outputs) * size),
        name="mix_features",
    )(planes, weight, *values)


def line_mix(gated, out_weight):
    plane = lax.axis_index("tp")
    near = plane < 2
    planes = jnp.stack(
        [plane, jnp.where(near, 2, 1), jnp.where(near, 3, 0), jnp.where(near, 0, 3), plane ^ 1]
    ).astype(jnp.int32)
    own_at, mid_at, far_at, edge_at, pair_at = range(5)
    weight = out_weight.astype(F32)
    mix = functools.partial(run_mix, planes, weight)
    swapped, gathered = gated
    pair = lax.ppermute(swapped, "tp", [(0, 1), (1, 0), (2, 3), (3, 2)])
    far = lax.ppermute(gathered, "tp", [(0, 2), (3, 1)])
    mid = lax.ppermute(gathered, "tp", [(1, 2), (2, 1)])
    edge = lax.ppermute(gathered, "tp", [(0, 1), (3, 2)])
    to_mid, to_far = mix((own_at, pair_at), ((mid_at, BF), (far_at, BF)), (swapped, pair))
    from_far = lax.ppermute(to_far, "tp", [(1, 3), (2, 0)])
    from_mid = lax.ppermute(to_mid, "tp", [(1, 2), (2, 1)])
    far, mid, to_mid, to_far = lax.optimization_barrier((far, mid, to_mid, to_far))
    (to_edge,) = mix((own_at, far_at, mid_at), ((edge_at, BF),), (gathered, far, mid))
    from_edge = lax.ppermute(to_edge, "tp", [(2, 3), (1, 0)])
    (acc_swapped,) = mix((own_at, pair_at), ((own_at, F32),), (swapped, pair))
    (acc_gathered,) = mix(
        (own_at, far_at, mid_at, edge_at), ((own_at, F32),), (gathered, far, mid, edge)
    )
    done = (acc_swapped + from_far.astype(F32) + from_mid.astype(F32)).astype(BF)
    done, acc_gathered = lax.optimization_barrier((done, acc_gathered))
    return [done, (acc_gathered + from_edge.astype(F32)).astype(BF)]


def gather_mix(gated, out_weight):
    plane = lax.axis_index("tp")
    outs = out_weight.shape[1] // lax.axis_size("tp")
    own_cols = lax.dynamic_slice_in_dim(out_weight, plane * outs, outs, 1)
    return [
        jnp.einsum(
            "co,crl->orl",
            own_cols,
            lax.all_gather(own, "tp", axis=0, tiled=True),
            preferred_element_type=F32,
        ).astype(BF)
        for own in gated
    ]


def local(query_gate, key_branch, value_branch, long_filter, skip_gain, out_weight):
    ctx_count = lax.axis_size("ctx")
    chans, tok_count = query_gate.shape
    rows = tok_count // COLS
    group = ctx_count // chans
    length = ctx_count * tok_count
    home = lax.axis_index("ctx") // group
    shape = (chans, rows, COLS)
    tables = run_tables(group, make_tables(ctx_count, group, chans, rows))

    def swap(values):
        got = [values[0]]
        for rel in range(1, chans):
            pairs = [
                (group * chip + core, group * (chip ^ rel) + core)
                for chip in range(chans)
                for core in range(group)
            ]
            got.append(lax.ppermute(values[rel], "ctx", pairs))
        return got

    def shift(value, step):
        pairs = [
            (group * chip + core, group * chip + (core + step) % group)
            for chip in range(chans)
            for core in range(group)
        ]
        return lax.ppermute(value, "ctx", pairs)

    query = query_gate.reshape(shape)
    key = key_branch.reshape(shape)
    value = value_branch.reshape(shape)
    signal = (key.astype(F32) * value.astype(F32)).astype(BF)
    pairs = jnp.stack([long_filter.astype(BF).reshape(shape), signal], 1)
    blocks = [lax.dynamic_index_in_dim(pairs, home ^ rel, 0, False) for rel in range(chans)]
    blocks = swap(blocks)
    blocks, tables = lax.optimization_barrier((blocks, tables))
    blocks += [shift(part, -step) for step in range(1, group) for part in blocks]
    back = run_spectrum(blocks, chans, group, tables, 1.0 / length)
    parts = [back] + [shift(back, -step) for step in range(1, group)]
    parts = swap(list(run_position(parts, chans, group, tables[1])))
    gated = run_gate(parts, query, key, value, skip_gain, group)
    mixed = (line_mix if lax.axis_size("tp") == 4 else gather_mix)(gated, out_weight)
    return jnp.concatenate(mixed, 2).reshape(-1, tok_count)


def solution(mesh):
    placed = (P("tp", "ctx"), P("tp", "ctx"), P("tp", "ctx"), P("tp", "ctx"), P("tp"), P())
    return jax.shard_map(
        local, mesh=mesh, in_specs=placed, out_specs=P("tp", "ctx"), check_vma=False
    )
```

time: 990 us -> 74.4 us (0.08); the launches traced: 979 us -> 74.1 us
  other arithmetic: 376 us -> 3.3 us
  local copies, waits for them, and re-layouts: 216 us -> 1.84 us
  matrix products: 194 us -> 0 us
  waiting for transfers between devices: 165 us -> 30.7 us
  Pallas kernels: 0 us -> 15.5 us
  between operations: 14.3 us -> 0.32 us
    unnamed x2 -> x1, other arithmetic: 359 us -> 0.04 us
    dot_general x21 -> x0, matrix products: 194 us -> none  [the longest x20 193 us: apply_form(): return jnp.einsum(form, table, values, precision=lax.Precision.HIGHEST)]
    unnamed x3 -> x0, waiting for transfers between devices: 79.4 us -> none
    unnamed x31 -> x20, local copies, waits for them, and re-layouts: 65.2 us -> 1.35 us
    all_to_all x1 -> x0, local copies, waits for them, and re-layouts: 58.6 us -> none  [local(): lax.all_to_all(stacked.astype(jnp.bfloat16), 'ctx', split_axis=2, concat_...]
    concatenate x1 -> x0, local copies, waits for them, and re-layouts: 49.7 us -> none  [local(): stacked = jnp.concatenate([signal, long_filter], 0)[:, None, :]]
    all_gather x1 -> x0, waiting for transfers between devices: 46.2 us -> none  [local(): lax.all_gather(gated, 'tp', axis=0, tiled=True)]
    all_to_all x3 -> x0, waiting for transfers between devices: 39.5 us -> none  [the longest x1 21.9 us: local(): lax.all_to_all(spec_im.astype(jnp.bfloat16), 'ctx', split_axis=1, concat_...]
  transfers between devices with their start and end apart: 5 -> 18, of which waited for: 5 -> 13; matrix products, arithmetic and copies ran while one was open for 3% -> 1% of each run, Pallas kernels for 0% -> 10%
where the time goes in v3:
time: 74.4 us; the launch traced here: 74.1 us
  waiting for transfers between devices  30.7 us (41%)
  starting transfers between devices  22.5 us (30%)
  Pallas kernels  15.5 us (21%)
  other arithmetic  3.3 us (4%)
  local copies, waits for them, and re-layouts  1.84 us (2%)
    ppermute x6, waiting for transfers between devices, swap(): got.append(lax.ppermute(values[rel], 'ctx', pairs))  15.2 us
    ppermute x6, starting transfers between devices, swap(): got.append(lax.ppermute(values[rel], 'ctx', pairs))  8.1 us
    pallas_call x1, Pallas kernels, run_spectrum(): pl.pallas_call(functools.partial(spectrum_kernel, chans, group, scale), o...  6.04 us
    ppermute x1, waiting for transfers between devices, line_mix(): from_far = lax.ppermute(to_far, 'tp', [(1, 3), (2, 0)])  5.91 us
    pallas_call x4, Pallas kernels, run_mix(): pl.pallas_call(functools.partial(mix_kernel, chans, slots, outputs), out_...  5.2 us
    ppermute x1, starting transfers between devices, line_mix(): far = lax.ppermute(gathered, 'tp', [(0, 2), (3, 1)])  4.5 us
    ppermute x1, waiting for transfers between devices, line_mix(): from_edge = lax.ppermute(to_edge, 'tp', [(2, 3), (1, 0)])  4.32 us
    ppermute x5, waiting for transfers between devices, shift(): return lax.ppermute(value, 'ctx', pairs)  4.16 us
  transfers between devices with their start and end apart: 18, of which 13 were waited for; matrix products, arithmetic and copies ran while one was open for 1% of the time, Pallas kernels for 10%

profile of v3, /device:TPU:0, one launch (start us, length us, event | category | flops | bytes accessed | tf_op | source)
XLA Modules:
  0.0 74.1 jit_solution(4735225680733853825)
XLA Ops:
  0.0 1.4 %convert_element_type.57 = bf16[4,65536]{1,0:T(4,128)(2,1)S(1)} convert(f32[4,65536]{1,0:T(4,128)} %param.14) | non-fusion elementwise | flops 262144 | bytes 1572864 | tf_op jit(solution)/shard_map/convert_element_type | solution.py:357
  1.5 1.6 %multiply_convert_fusion = bf16[4,65536]{1,0:T(4,128)(2,1)S(1)} fusion(bf16[4,65536]{1,0:T(4,128)(2,1)} %param.13, bf16[4,65536]{1,0:T(4,128)(2,1)} %param.12), kind=kLoop, calls=%fused_computation.8 | loop fusion | flops 1048576 | bytes 1572864 | tf_op jit(solution)/shard_map/convert_element_type | solution.py:356
  3.4 3.0 %collective-permute-start = (bf16[2,128,512]{2,1,0:T(8,128)(2,1)S(1)}, bf16[2,128,512]{2,1,0:T(8,128)(2,1)S(1)}, u32[]{:S(2)}, u32[]{:S(2)}) collective-permute-start(bf16[2,128,512]{2,1,0:T(8,128)(2,1)S(1)} %get-tuple-element.55), channel_id=1, source_target_pairs={{0,8},{4,12},{8,0},{12,4},{16,24},{20,28},{24,16},{28,20},{1,9},{5... | collective-permute-start | bytes 786440 | tf_op jit(solution)/shard_map/ppermute | solution.py:342
  6.4 1.5 %collective-permute-start.1 = (bf16[2,128,512]{2,1,0:T(8,128)(2,1)S(1)}, bf16[2,128,512]{2,1,0:T(8,128)(2,1)S(1)}, u32[]{:S(2)}, u32[]{:S(2)}) collective-permute-start(bf16[2,128,512]{2,1,0:T(8,128)(2,1)S(1)} %get-tuple-element.56), channel_id=1, source_target_pairs={{0,16},{4,20},{8,24},{12,28},{16,0},{20,4},{24,8},{28,12},{1,17},{... | collective-permute-start | bytes 786440 | tf_op jit(solution)/shard_map/ppermute | solution.py:342
  7.9 2.1 %load_tables.1 = (bf16[1024,1024]{1,0:T(8,128)(2,1)S(1)}, bf16[512,2048]{1,0:T(8,128)(2,1)S(1)}, bf16[1024,512]{1,0:T(8,128)(2,1)S(1)}, f32[2,512,512]{2,1,0:T(8,128)S(1)}) custom-call(bf16[2,1024,1024]{2,1,0:T(8,128)(2,1)S(1)} %copy-done.1, bf16[2,512,2048]{2,1,0:T(8,128)(2,1)} %constant.50.clone.refs_1_, bf16[1024,512]{1,0:T(8,128)(2,1)S(1)} %copy-done.2, ...), custom_call_target="tpu_custom_call" | custom-call | flops 3000000000 | tf_op jit(solution)/shard_map/load_tables/pallas_call | solution.py:96
  10.1 3.5 %collective-permute-done.refs_1_ = bf16[2,128,512]{2,1,0:T(8,128)(2,1)S(1)} collective-permute-done((bf16[2,128,512]{2,1,0:T(8,128)(2,1)S(1)}, bf16[2,128,512]{2,1,0:T(8,128)(2,1)S(1)}, u32[]{:S(2)}, u32[]{:S(2)}) %collective-permute-start) | collective-permute-done | bytes 262176 | tf_op jit(solution)/shard_map/ppermute | solution.py:342
  13.5 6.2 %collective-permute-done.1.refs_2_ = bf16[2,128,512]{2,1,0:T(8,128)(2,1)S(1)} collective-permute-done((bf16[2,128,512]{2,1,0:T(8,128)(2,1)S(1)}, bf16[2,128,512]{2,1,0:T(8,128)(2,1)S(1)}, u32[]{:S(2)}, u32[]{:S(2)}) %collective-permute-start.1) | collective-permute-done | bytes 262176 | tf_op jit(solution)/shard_map/ppermute | solution.py:342
  22.4 6.0 %spectrum_product.1.refs_0_ = bf16[1024,512]{1,0:T(8,128)(2,1)S(1)} custom-call(bf16[2,128,512]{2,1,0:T(8,128)(2,1)S(1)} %get-tuple-element.33.refs_0_, bf16[2,128,512]{2,1,0:T(8,128)(2,1)S(1)} %collective-permute-done.refs_1_, bf16[2,128,512]{2,1,0:T(8,128)(2,1)S(1)} %collective-permute-done.1.refs_2_, ...), custom_call_target="tpu_custom_call" | custom-call | flops 5368709120 | tf_op jit(solution)/shard_map/spectrum_product/pallas_call | solution.py:196
  28.7 2.5 %collective-permute-done.7.refs_1_ = bf16[1024,512]{1,0:T(8,128)(2,1)S(1)} collective-permute-done((bf16[1024,512]{1,0:T(8,128)(2,1)S(1)}, bf16[1024,512]{1,0:T(8,128)(2,1)S(1)}, u32[]{:S(2)}, u32[]{:S(2)}) %collective-permute-start.7) | collective-permute-done | bytes 1048608 | tf_op jit(solution)/shard_map/ppermute | solution.py:351
  31.2 1.3 %back_positions.1 = (bf16[128,512]{1,0:T(8,128)(2,1)S(1)}, bf16[128,512]{1,0:T(8,128)(2,1)S(1)}, bf16[128,512]{1,0:T(8,128)(2,1)S(1)}, bf16[128,512]{1,0:T(8,128)(2,1)S(1)}) custom-call(bf16[1024,512]{1,0:T(8,128)(2,1)S(1)} %spectrum_product.1.refs_0_, bf16[1024,512]{1,0:T(8,128)(2,1)S(1)} %collective-permute-done.7.refs_1_, ...), custom_call_target="tpu_custom_call" | custom-call | flops 1073741824 | tf_op jit(solution)/shard_map/back_positions/pallas_call | solution.py:216
  32.5 1.6 %collective-permute-start.10 = (bf16[128,512]{1,0:T(8,128)(2,1)S(1)}, bf16[128,512]{1,0:T(8,128)(2,1)S(1)}, u32[]{:S(2)}, u32[]{:S(2)}) collective-permute-start(bf16[128,512]{1,0:T(8,128)(2,1)S(1)} %get-tuple-element.44), channel_id=1, source_target_pairs={{0,24},{4,28},{8,16},{12,20},{16,8},{20,12},{24,0},{28,4},{1,25},{... | collective-permute-start | bytes 393224 | tf_op jit(solution)/shard_map/ppermute | solution.py:342
  34.1 1.5 %collective-permute-start.8 = (bf16[128,512]{1,0:T(8,128)(2,1)S(1)}, bf16[128,512]{1,0:T(8,128)(2,1)S(1)}, u32[]{:S(2)}, u32[]{:S(2)}) collective-permute-start(bf16[128,512]{1,0:T(8,128)(2,1)S(1)} %get-tuple-element.42), channel_id=1, source_target_pairs={{0,8},{4,12},{8,0},{12,4},{16,24},{20,28},{24,16},{28,20},{1,9},{5... | collective-permute-start | bytes 393224 | tf_op jit(solution)/shard_map/ppermute | solution.py:342
  36.4 3.4 %collective-permute-done.10.refs_3_ = bf16[128,512]{1,0:T(8,128)(2,1)S(1)} collective-permute-done((bf16[128,512]{1,0:T(8,128)(2,1)S(1)}, bf16[128,512]{1,0:T(8,128)(2,1)S(1)}, u32[]{:S(2)}, u32[]{:S(2)}) %collective-permute-start.10) | collective-permute-done | bytes 131104 | tf_op jit(solution)/shard_map/ppermute | solution.py:342
  39.8 2.1 %collective-permute-done.8.refs_1_ = bf16[128,512]{1,0:T(8,128)(2,1)S(1)} collective-permute-done((bf16[128,512]{1,0:T(8,128)(2,1)S(1)}, bf16[128,512]{1,0:T(8,128)(2,1)S(1)}, u32[]{:S(2)}, u32[]{:S(2)}) %collective-permute-start.8) | collective-permute-done | bytes 131104 | tf_op jit(solution)/shard_map/ppermute | solution.py:342
  42.8 1.6 %collective-permute-start.11 = (bf16[4,128,256]{2,1,0:T(8,128)(2,1)S(1)}, bf16[4,128,256]{2,1,0:T(8,128)(2,1)S(1)}, u32[]{:S(2)}, u32[]{:S(2)}) collective-permute-start(bf16[4,128,256]{2,1,0:T(8,128)(2,1)S(1)} %get-tuple-element.45.refs_0_), channel_id=1, source_target_pairs={{0,1},{1,0},{2,3},{3,2},{4,5},{5,4},{6,7},{7,6},{8,9},{9,8},{10,11... | collective-permute-start | bytes 786440 | tf_op jit(solution)/shard_map/ppermute | solution.py:290
  44.4 4.5 %collective-permute-start.14 = (bf16[4,128,256]{2,1,0:T(8,128)(2,1)S(1)}, bf16[4,128,256]{2,1,0:T(8,128)(2,1)S(1)}, u32[]{:S(2)}, u32[]{:S(2)}) collective-permute-start(bf16[4,128,256]{2,1,0:T(8,128)(2,1)S(1)} %get-tuple-element.48.refs_0_), channel_id=1, source_target_pairs={{0,2},{3,1},{4,6},{7,5},{8,10},{11,9},{12,14},{15,13},{16,18},{19,... | collective-permute-start | bytes 786440 | tf_op jit(solution)/shard_map/ppermute | solution.py:291
  49.7 3.1 %collective-permute-start.16 = (bf16[4,128,256]{2,1,0:T(8,128)(2,1)S(1)}, bf16[4,128,256]{2,1,0:T(8,128)(2,1)S(1)}, u32[]{:S(2)}, u32[]{:S(2)}) collective-permute-start(bf16[4,128,256]{2,1,0:T(8,128)(2,1)S(1)} %get-tuple-element.48.refs_0_), channel_id=1, source_target_pairs={{0,1},{3,2},{4,5},{7,6},{8,9},{11,10},{12,13},{15,14},{16,17},{19,... | collective-permute-start | bytes 786440 | tf_op jit(solution)/shard_map/ppermute | solution.py:293
  52.8 1.4 %mix_features.5 = (bf16[4,128,256]{2,1,0:T(8,128)(2,1)S(1)}, bf16[4,128,256]{2,1,0:T(8,128)(2,1)S(1)}) custom-call(s32[5]{0:T(128)S(1)} %stack.27.plane_ref, f32[16,16]{1,0:T(8,128)S(1)} %convert_element_type.56.weight_ref, bf16[4,128,256]{2,1,0:T(8,128)(2,1)S(1)} %get-tuple-element.45.refs_0_, bf16[4,128,256]{2,1,0:T(8,128)(2,1)S(1)} %collective-permute-done.11.refs_1_), custom_call_target="tpu_custom_call" | custom-call | flops 4194304 | tf_op jit(solution)/shard_map/mix_features/pallas_call | solution.py:269
  54.2 1.3 %collective-permute-start.12 = (bf16[4,128,256]{2,1,0:T(8,128)(2,1)S(1)}, bf16[4,128,256]{2,1,0:T(8,128)(2,1)S(1)}, u32[]{:S(2)}, u32[]{:S(2)}) collective-permute-start(bf16[4,128,256]{2,1,0:T(8,128)(2,1)S(1)} %get-tuple-element.46), channel_id=1, source_target_pairs={{1,3},{2,0},{5,7},{6,4},{9,11},{10,8},{13,15},{14,12},{17,19},{18,... | collective-permute-start | bytes 786440 | tf_op jit(solution)/shard_map/ppermute | solution.py:295
  56.7 1.3 %mix_features.7 = bf16[4,128,256]{2,1,0:T(8,128)(2,1)S(1)} custom-call(s32[5]{0:T(128)S(1)} %stack.27.plane_ref, f32[16,16]{1,0:T(8,128)S(1)} %convert_element_type.56.weight_ref, bf16[4,128,256]{2,1,0:T(8,128)(2,1)S(1)} %get-tuple-element.48.refs_0_, bf16[4,128,256]{2,1,0:T(8,128)(2,1)S(1)} %collective-permute-done.14.refs_1_, ...), custom_call_target="tpu_custom_call" | custom-call | flops 3145728 | tf_op jit(solution)/shard_map/mix_features/pallas_call | solution.py:269
  58.0 1.3 %collective-permute-start.17 = (bf16[4,128,256]{2,1,0:T(8,128)(2,1)S(1)}, bf16[4,128,256]{2,1,0:T(8,128)(2,1)S(1)}, u32[]{:S(2)}, u32[]{:S(2)}) collective-permute-start(bf16[4,128,256]{2,1,0:T(8,128)(2,1)S(1)} %mix_features.7), channel_id=1, source_target_pairs={{2,3},{1,0},{6,7},{5,4},{10,11},{9,8},{14,15},{13,12},{18,19},{17,... | collective-permute-start | bytes 786440 | tf_op jit(solution)/shard_map/ppermute | solution.py:299
  61.0 1.5 %mix_features.6 = f32[4,128,256]{2,1,0:T(8,128)S(1)} custom-call(s32[5]{0:T(128)S(1)} %stack.27.plane_ref, f32[16,16]{1,0:T(8,128)S(1)} %convert_element_type.56.weight_ref, bf16[4,128,256]{2,1,0:T(8,128)(2,1)S(1)} %get-tuple-element.48.refs_0_, bf16[4,128,256]{2,1,0:T(8,128)(2,1)S(1)} %collective-permute-done.14.refs_1_, ...), custom_call_target="tpu_custom_call" | custom-call | flops 4194304 | tf_op jit(solution)/shard_map/mix_features/pallas_call | solution.py:269
  62.4 5.9 %collective-permute-done.12 = bf16[4,128,256]{2,1,0:T(8,128)(2,1)S(1)} collective-permute-done((bf16[4,128,256]{2,1,0:T(8,128)(2,1)S(1)}, bf16[4,128,256]{2,1,0:T(8,128)(2,1)S(1)}, u32[]{:S(2)}, u32[]{:S(2)}) %collective-permute-start.12) | collective-permute-done | bytes 262176 | tf_op jit(solution)/shard_map/ppermute | solution.py:295
  68.5 4.3 %collective-permute-done.17 = bf16[4,128,256]{2,1,0:T(8,128)(2,1)S(1)} collective-permute-done((bf16[4,128,256]{2,1,0:T(8,128)(2,1)S(1)}, bf16[4,128,256]{2,1,0:T(8,128)(2,1)S(1)}, u32[]{:S(2)}, u32[]{:S(2)}) %collective-permute-start.17) | collective-permute-done | bytes 262176 | tf_op jit(solution)/shard_map/ppermute | solution.py:299
  (50 shorter events, 9.9 us)
Async XLA Ops:
  1.4 6.5 %copy-start.2 = (bf16[1024,512]{1,0:T(8,128)(2,1)S(1)}, bf16[1024,512]{1,0:T(8,128)(2,1)}, u32[]{:S(2)}) copy-start(bf16[1024,512]{1,0:T(8,128)(2,1)} %constant.51.clone.refs_2_) | copy-start | bytes 3145732
  1.4 6.5 %copy-start.3 = (f32[2,2,16,512]{3,2,1,0:T(8,128)S(1)}, f32[2,2,16,512]{3,2,1,0:T(8,128)}, u32[]{:S(2)}) copy-start(f32[2,2,16,512]{3,2,1,0:T(8,128)} %constant.52.clone.refs_3_) | copy-start | bytes 393220
  3.4 10.1 %collective-permute-start = (bf16[2,128,512]{2,1,0:T(8,128)(2,1)S(1)}, bf16[2,128,512]{2,1,0:T(8,128)(2,1)S(1)}, u32[]{:S(2)}, u32[]{:S(2)}) collective-permute-start(bf16[2,128,512]{2,1,0:T(8,128)(2,1)S(1)} %get-tuple-element.55), channel_id=1, source_target_pairs={{0,8},{4,12},{8,0},{12,4},{16,24},{20,28},{24,16},{28,20},{1,9},{5... | collective-permute-start | bytes 786440 | tf_op jit(solution)/shard_map/ppermute | solution.py:342
  6.4 13.4 %collective-permute-start.1 = (bf16[2,128,512]{2,1,0:T(8,128)(2,1)S(1)}, bf16[2,128,512]{2,1,0:T(8,128)(2,1)S(1)}, u32[]{:S(2)}, u32[]{:S(2)}) collective-permute-start(bf16[2,128,512]{2,1,0:T(8,128)(2,1)S(1)} %get-tuple-element.56), channel_id=1, source_target_pairs={{0,16},{4,20},{8,24},{12,28},{16,0},{20,4},{24,8},{28,12},{1,17},{... | collective-permute-start | bytes 786440 | tf_op jit(solution)/shard_map/ppermute | solution.py:342
  7.9 11.9 %collective-permute-start.2 = (bf16[2,128,512]{2,1,0:T(8,128)(2,1)S(1)}, bf16[2,128,512]{2,1,0:T(8,128)(2,1)S(1)}, u32[]{:S(2)}, u32[]{:S(2)}) collective-permute-start(bf16[2,128,512]{2,1,0:T(8,128)(2,1)S(1)} %get-tuple-element.53), channel_id=1, source_target_pairs={{0,24},{4,28},{8,16},{12,20},{16,8},{20,12},{24,0},{28,4},{1,25},{... | collective-permute-start | bytes 786440 | tf_op jit(solution)/shard_map/ppermute | solution.py:342
  19.8 1.5 %collective-permute-start.3 = (bf16[2,128,512]{2,1,0:T(8,128)(2,1)S(1)}, bf16[2,128,512]{2,1,0:T(8,128)(2,1)S(1)}, u32[]{:S(2)}, u32[]{:S(2)}) collective-permute-start(bf16[2,128,512]{2,1,0:T(8,128)(2,1)S(1)} %get-tuple-element.33.refs_0_), channel_id=1, source_target_pairs={{0,4},{4,0},{8,12},{12,8},{16,20},{20,16},{24,28},{28,24},{1,5},{5... | collective-permute-start | bytes 786440 | tf_op jit(solution)/shard_map/ppermute | solution.py:351
  19.8 1.9 %collective-permute-start.4 = (bf16[2,128,512]{2,1,0:T(8,128)(2,1)S(1)}, bf16[2,128,512]{2,1,0:T(8,128)(2,1)S(1)}, u32[]{:S(2)}, u32[]{:S(2)}) collective-permute-start(bf16[2,128,512]{2,1,0:T(8,128)(2,1)S(1)} %collective-permute-done.refs_1_), channel_id=1, source_target_pairs={{0,4},{4,0},{8,12},{12,8},{16,20},{20,16},{24,28},{28,24},{1,5},{5... | collective-permute-start | bytes 786440 | tf_op jit(solution)/shard_map/ppermute | solution.py:351
  20.3 1.8 %collective-permute-start.5 = (bf16[2,128,512]{2,1,0:T(8,128)(2,1)S(1)}, bf16[2,128,512]{2,1,0:T(8,128)(2,1)S(1)}, u32[]{:S(2)}, u32[]{:S(2)}) collective-permute-start(bf16[2,128,512]{2,1,0:T(8,128)(2,1)S(1)} %collective-permute-done.1.refs_2_), channel_id=1, source_target_pairs={{0,4},{4,0},{8,12},{12,8},{16,20},{20,16},{24,28},{28,24},{1,5},{5... | collective-permute-start | bytes 786440 | tf_op jit(solution)/shard_map/ppermute | solution.py:351
  20.3 2.1 %collective-permute-start.6 = (bf16[2,128,512]{2,1,0:T(8,128)(2,1)S(1)}, bf16[2,128,512]{2,1,0:T(8,128)(2,1)S(1)}, u32[]{:S(2)}, u32[]{:S(2)}) collective-permute-start(bf16[2,128,512]{2,1,0:T(8,128)(2,1)S(1)} %collective-permute-done.2.refs_3_), channel_id=1, source_target_pairs={{0,4},{4,0},{8,12},{12,8},{16,20},{20,16},{24,28},{28,24},{1,5},{5... | collective-permute-start | bytes 786440 | tf_op jit(solution)/shard_map/ppermute | solution.py:351
  28.5 7.6 %copy-start.5 = (bf16[4,65536]{1,0:T(4,128)(2,1)S(1)}, bf16[4,65536]{1,0:T(4,128)(2,1)}, u32[]{:S(2)}) copy-start(bf16[4,65536]{1,0:T(4,128)(2,1)} %param.13) | copy-start | bytes 1572868
  28.5 7.6 %copy-start.6 = (bf16[4,65536]{1,0:T(4,128)(2,1)S(1)}, bf16[4,65536]{1,0:T(4,128)(2,1)}, u32[]{:S(2)}) copy-start(bf16[4,65536]{1,0:T(4,128)(2,1)} %param.12) | copy-start | bytes 1572868
  28.5 2.7 %collective-permute-start.7 = (bf16[1024,512]{1,0:T(8,128)(2,1)S(1)}, bf16[1024,512]{1,0:T(8,128)(2,1)S(1)}, u32[]{:S(2)}, u32[]{:S(2)}) collective-permute-start(bf16[1024,512]{1,0:T(8,128)(2,1)S(1)} %spectrum_product.1.refs_0_), channel_id=1, source_target_pairs={{0,4},{4,0},{8,12},{12,8},{16,20},{20,16},{24,28},{28,24},{1,5},{5... | collective-permute-start | bytes 3145736 | tf_op jit(solution)/shard_map/ppermute | solution.py:351
  32.5 9.4 %copy-start = (f32[4]{0:T(128)S(1)}, f32[4]{0:T(128)}, u32[]{:S(2)}) copy-start(f32[4]{0:T(128)} %refs_7_.1) | copy-start | bytes 52
  32.5 7.3 %collective-permute-start.10 = (bf16[128,512]{1,0:T(8,128)(2,1)S(1)}, bf16[128,512]{1,0:T(8,128)(2,1)S(1)}, u32[]{:S(2)}, u32[]{:S(2)}) collective-permute-start(bf16[128,512]{1,0:T(8,128)(2,1)S(1)} %get-tuple-element.44), channel_id=1, source_target_pairs={{0,24},{4,28},{8,16},{12,20},{16,8},{20,12},{24,0},{28,4},{1,25},{... | collective-permute-start | bytes 393224 | tf_op jit(solution)/shard_map/ppermute | solution.py:342
  34.1 7.8 %collective-permute-start.8 = (bf16[128,512]{1,0:T(8,128)(2,1)S(1)}, bf16[128,512]{1,0:T(8,128)(2,1)S(1)}, u32[]{:S(2)}, u32[]{:S(2)}) collective-permute-start(bf16[128,512]{1,0:T(8,128)(2,1)S(1)} %get-tuple-element.42), channel_id=1, source_target_pairs={{0,8},{4,12},{8,0},{12,4},{16,24},{20,28},{24,16},{28,20},{1,9},{5... | collective-permute-start | bytes 393224 | tf_op jit(solution)/shard_map/ppermute | solution.py:342
  35.6 6.3 %collective-permute-start.9 = (bf16[128,512]{1,0:T(8,128)(2,1)S(1)}, bf16[128,512]{1,0:T(8,128)(2,1)S(1)}, u32[]{:S(2)}, u32[]{:S(2)}) collective-permute-start(bf16[128,512]{1,0:T(8,128)(2,1)S(1)} %get-tuple-element.43), channel_id=1, source_target_pairs={{0,16},{4,20},{8,24},{12,28},{16,0},{20,4},{24,8},{28,12},{1,17},{... | collective-permute-start | bytes 393224 | tf_op jit(solution)/shard_map/ppermute | solution.py:342
  36.3 13.3 %copy-start.8 = (bf16[16,16]{1,0:T(8,128)(2,1)S(1)}, bf16[16,16]{1,0:T(8,128)(2,1)}, u32[]{:S(2)}) copy-start(bf16[16,16]{1,0:T(8,128)(2,1)} %param.16) | copy-start | bytes 1540
  42.8 10.0 %collective-permute-start.11 = (bf16[4,128,256]{2,1,0:T(8,128)(2,1)S(1)}, bf16[4,128,256]{2,1,0:T(8,128)(2,1)S(1)}, u32[]{:S(2)}, u32[]{:S(2)}) collective-permute-start(bf16[4,128,256]{2,1,0:T(8,128)(2,1)S(1)} %get-tuple-element.45.refs_0_), channel_id=1, source_target_pairs={{0,1},{1,0},{2,3},{3,2},{4,5},{5,4},{6,7},{7,6},{8,9},{9,8},{10,11... | collective-permute-start | bytes 786440 | tf_op jit(solution)/shard_map/ppermute | solution.py:290
  44.4 12.3 %collective-permute-start.14 = (bf16[4,128,256]{2,1,0:T(8,128)(2,1)S(1)}, bf16[4,128,256]{2,1,0:T(8,128)(2,1)S(1)}, u32[]{:S(2)}, u32[]{:S(2)}) collective-permute-start(bf16[4,128,256]{2,1,0:T(8,128)(2,1)S(1)} %get-tuple-element.48.refs_0_), channel_id=1, source_target_pairs={{0,2},{3,1},{4,6},{7,5},{8,10},{11,9},{12,14},{15,13},{16,18},{19,... | collective-permute-start | bytes 786440 | tf_op jit(solution)/shard_map/ppermute | solution.py:291
  48.9 7.8 %collective-permute-start.15 = (bf16[4,128,256]{2,1,0:T(8,128)(2,1)S(1)}, bf16[4,128,256]{2,1,0:T(8,128)(2,1)S(1)}, u32[]{:S(2)}, u32[]{:S(2)}) collective-permute-start(bf16[4,128,256]{2,1,0:T(8,128)(2,1)S(1)} %get-tuple-element.48.refs_0_), channel_id=1, source_target_pairs={{1,2},{2,1},{5,6},{6,5},{9,10},{10,9},{13,14},{14,13},{17,18},{18,... | collective-permute-start | bytes 786440 | tf_op jit(solution)/shard_map/ppermute | solution.py:292
  49.7 11.2 %collective-permute-start.16 = (bf16[4,128,256]{2,1,0:T(8,128)(2,1)S(1)}, bf16[4,128,256]{2,1,0:T(8,128)(2,1)S(1)}, u32[]{:S(2)}, u32[]{:S(2)}) collective-permute-start(bf16[4,128,256]{2,1,0:T(8,128)(2,1)S(1)} %get-tuple-element.48.refs_0_), channel_id=1, source_target_pairs={{0,1},{3,2},{4,5},{7,6},{8,9},{11,10},{12,13},{15,14},{16,17},{19,... | collective-permute-start | bytes 786440 | tf_op jit(solution)/shard_map/ppermute | solution.py:293
  54.2 14.1 %collective-permute-start.12 = (bf16[4,128,256]{2,1,0:T(8,128)(2,1)S(1)}, bf16[4,128,256]{2,1,0:T(8,128)(2,1)S(1)}, u32[]{:S(2)}, u32[]{:S(2)}) collective-permute-start(bf16[4,128,256]{2,1,0:T(8,128)(2,1)S(1)} %get-tuple-element.46), channel_id=1, source_target_pairs={{1,3},{2,0},{5,7},{6,4},{9,11},{10,8},{13,15},{14,12},{17,19},{18,... | collective-permute-start | bytes 786440 | tf_op jit(solution)/shard_map/ppermute | solution.py:295
  55.5 12.8 %collective-permute-start.13 = (bf16[4,128,256]{2,1,0:T(8,128)(2,1)S(1)}, bf16[4,128,256]{2,1,0:T(8,128)(2,1)S(1)}, u32[]{:S(2)}, u32[]{:S(2)}) collective-permute-start(bf16[4,128,256]{2,1,0:T(8,128)(2,1)S(1)} %get-tuple-element.47), channel_id=1, source_target_pairs={{1,2},{2,1},{5,6},{6,5},{9,10},{10,9},{13,14},{14,13},{17,18},{18,... | collective-permute-start | bytes 786440 | tf_op jit(solution)/shard_map/ppermute | solution.py:296
  58.0 14.8 %collective-permute-start.17 = (bf16[4,128,256]{2,1,0:T(8,128)(2,1)S(1)}, bf16[4,128,256]{2,1,0:T(8,128)(2,1)S(1)}, u32[]{:S(2)}, u32[]{:S(2)}) collective-permute-start(bf16[4,128,256]{2,1,0:T(8,128)(2,1)S(1)} %mix_features.7), channel_id=1, source_target_pairs={{2,3},{1,0},{6,7},{5,4},{10,11},{9,8},{14,15},{13,12},{18,19},{17,... | collective-permute-start | bytes 786440 | tf_op jit(solution)/shard_map/ppermute | solution.py:299
  (3 other events, 15.2 us)

commit v4 on v3

--- a/solution.py
+++ b/solution.py
@@ -10,6 +10,7 @@
 
 COLS = 512
 STEP = 32
+PIECES = 4
 CUTS = (0, 256, 512)
 BF = jnp.bfloat16
 F32 = jnp.float32
@@ -114,10 +115,98 @@
     )(*tables)
 
 
+def prepare_kernel(chans, group, *refs):
+    filter_hbm, key_hbm, value_hbm = refs[:3]
+    outs = refs[3 : 3 + chans]
+    filter_ref, key_ref, value_ref, pair_ref, sems = refs[3 + chans :]
+    home = lax.axis_index("ctx") // group
+    rows = pair_ref.shape[2]
+    step = rows // PIECES
+    copies = []
+    for number in range(PIECES):
+        cut = slice(number * step * COLS, (number + 1) * step * COLS)
+        for kind, (source, target) in enumerate(
+            ((filter_hbm, filter_ref), (key_hbm, key_ref), (value_hbm, value_ref))
+        ):
+            copy = pltpu.make_async_copy(
+                source.at[:, cut], target.at[:, cut], sems.at[kind, number]
+            )
+            copy.start()
+            copies.append(copy)
+    shape = (chans, 16, COLS)
+    for number in range(PIECES):
+        for copy in copies[3 * number : 3 * number + 3]:
+            copy.wait()
+        for first in range(number * step, (number + 1) * step, 16):
+            cut = slice(first * COLS, (first + 16) * COLS)
+            pair_ref[:, 0, first : first + 16] = filter_ref[:, cut].astype(BF).reshape(shape)
+            signal = key_ref[:, cut].astype(F32) * value_ref[:, cut].astype(F32)
+            pair_ref[:, 1, first : first + 16] = signal.astype(BF).reshape(shape)
+    for rel in range(chans):
+        outs[rel][...] = pair_ref[home ^ rel]
+
+
+def run_prepare(long_filter, key, value, group):
+    chans, tok_count = key.shape
+    rows = tok_count // COLS
+    return pl.pallas_call(
+        functools.partial(prepare_kernel, chans, group),
+        out_shape=(jax.ShapeDtypeStruct((2, rows, COLS), BF),) * chans,
+        in_specs=[HBM] * 3,
+        out_specs=(VMEM,) * chans,
+        scratch_shapes=[
+            pltpu.VMEM((chans, tok_count), F32),
+            pltpu.VMEM((chans, tok_count), BF),
+            pltpu.VMEM((chans, tok_count), BF),
+            pltpu.VMEM((chans, 2, rows, COLS), BF),
+            pltpu.SemaphoreType.DMA((3, PIECES)),
+        ],
+        compiler_params=params(60),
+        cost_estimate=cost(4 * chans * tok_count),
+        name="prepare_blocks",
+    )(long_filter, key, value)
+
+
+def finish_kernel(first_ref, acc_ref, got_ref, out_hbm, out_ref, sems):
+    feats, rows, _ = first_ref.shape
+    step = rows // PIECES
+    copies = []
+    for number in range(PIECES):
+        for row in range(number * step, (number + 1) * step, 16):
+            cut = slice(row, row + 16)
+            second = (acc_ref[:, cut] + got_ref[:, cut].astype(F32)).astype(BF)
+            whole = jnp.concatenate([first_ref[:, cut], second], 2)
+            out_ref[:, row * COLS : (row + 16) * COLS] = whole.reshape(feats, 16 * COLS)
+        cut = slice(number * step * COLS, (number + 1) * step * COLS)
+        copy = pltpu.make_async_copy(out_ref.at[:, cut], out_hbm.at[:, cut], sems.at[number])
+        copy.start()
+        copies.append(copy)
+    for copy in copies:
+        copy.wait()
+
+
+def run_finish(first, acc, got):
+    feats, rows, _ = first.shape
+    return pl.pallas_call(
+        finish_kernel,
+        out_shape=jax.ShapeDtypeStruct((feats, rows * COLS), BF),
+        in_specs=[VMEM] * 3,
+        out_specs=HBM,
+        scratch_shapes=[
+            pltpu.VMEM((feats, rows * COLS), BF),
+            pltpu.SemaphoreType.DMA((PIECES,)),
+        ],
+        compiler_params=params(12),
+        cost_estimate=cost(feats * rows * COLS),
+        name="finish",
+    )(first, acc, got)
+
+
 def spectrum_kernel(chans, group, scale, *refs):
     count = chans * group
-    blocks, (left_ref, wave_ref, turn_ref, out_ref) = refs[:count], refs[count : count + 4]
-    x_ref, mid_ref, prod_ref, spec_ref = refs[count + 4 :]
+    blocks = refs[:count]
+    left_ref, wave_ref, turn_ref, prod_ref, out_ref = refs[count : count + 5]
+    x_ref, mid_ref, spec_ref = refs[count + 5 :]
     rows = blocks[0].shape[1]
     own = mid_ref.shape[0]
     home = lax.axis_index("ctx") // group
@@ -153,13 +242,17 @@
                     out_re * fil_re - out_im * fil_im
                 ).astype(BF)
                 prod_ref[:, 2 * COLS + tile : 2 * COLS + tile + 256] = -prod_im
-    for tile in range(0, COLS, 256):
-        cut = slice(tile, tile + 256)
-        val_im = dot(prod_ref[:, : 2 * COLS], wave_ref[:, cut])
-        val_re = dot(prod_ref[:, COLS:], wave_ref[:, cut])
-        tab_re, tab_im = turn_ref[0, :, cut], turn_ref[1, :, cut]
-        out_ref[:own, cut] = (val_re * tab_re + val_im * tab_im).astype(BF)
-        out_ref[own:, cut] = (val_im * tab_re - val_re * tab_im).astype(BF)
+    back_stage(CUTS[0], CUTS[1], prod_ref, wave_ref, turn_ref, out_ref)
+
+
+def back_stage(low, high, prod_ref, wave_ref, turn_ref, out_ref):
+    own = prod_ref.shape[0]
+    cut = slice(low, high)
+    val_im = dot(prod_ref[:, : 2 * COLS], wave_ref[:, cut])
+    val_re = dot(prod_ref[:, COLS:], wave_ref[:, cut])
+    tab_re, tab_im = turn_ref[0, :, cut], turn_ref[1, :, cut]
+    out_ref[:own] = (val_re * tab_re + val_im * tab_im).astype(BF)
+    out_ref[own:] = (val_im * tab_re - val_re * tab_im).astype(BF)
 
 
 def position_kernel(chans, group, *refs):
@@ -176,18 +269,16 @@
         outs[rel][...] = sum_ref[pl.ds(pl.multiple_of((home ^ rel) * rows, rows), rows)]
 
 
-def gate_kernel(chans, group, *refs):
+def gate_kernel(chans, group, low, high, *refs):
     parts = refs[:chans]
-    query_ref, key_ref, value_ref, gain_ref = refs[chans : chans + 4]
-    outs = refs[chans + 4 :]
+    query_ref, key_ref, value_ref, gain_ref, out_ref = refs[chans:]
+    cut = slice(low, high)
     home = lax.axis_index("ctx") // group
     for rel in range(chans):
         chan = home ^ rel
-        signal = key_ref[chan].astype(F32) * value_ref[chan].astype(F32)
+        signal = key_ref[chan, :, cut].astype(F32) * value_ref[chan, :, cut].astype(F32)
         total = parts[rel][...].astype(F32) + gain_ref[chan] * signal
-        gated = (query_ref[chan].astype(F32) * total).astype(BF)
-        for out, low, high in zip(outs, CUTS[:-1], CUTS[1:]):
-            out[chan] = gated[:, low:high]
+        out_ref[chan] = (query_ref[chan, :, cut].astype(F32) * total).astype(BF)
 
 
 def run_spectrum(blocks, chans, group, tables, scale):
@@ -195,12 +286,14 @@
     own, big = left.shape[0] // 2, left.shape[1]
     return pl.pallas_call(
         functools.partial(spectrum_kernel, chans, group, scale),
-        out_shape=jax.ShapeDtypeStruct((2 * own, COLS), BF),
+        out_shape=(
+            jax.ShapeDtypeStruct((own, 3 * COLS), BF),
+            jax.ShapeDtypeStruct((2 * own, CUTS[1] - CUTS[0]), BF),
+        ),
         in_specs=[VMEM] * (len(blocks) + 3),
-        out_specs=VMEM,
+        out_specs=(VMEM, VMEM),
         scratch_shapes=[
             pltpu.VMEM((2, big, COLS), BF),
-            pltpu.VMEM((own, 3 * COLS), BF),
             pltpu.VMEM((own, 3 * COLS), BF),
             pltpu.VMEM((2, own, COLS), F32),
         ],
@@ -210,33 +303,45 @@
     )(*blocks, left, wave, turn)
 
 
+def run_back(prod, tables, low, high):
+    _, _, wave, turn = tables
+    own = prod.shape[0]
+    return pl.pallas_call(
+        functools.partial(back_stage, low, high),
+        out_shape=jax.ShapeDtypeStruct((2 * own, high - low), BF),
+        in_specs=[VMEM] * 3,
+        out_specs=VMEM,
+        compiler_params=params(12),
+        cost_estimate=cost(8 * own * COLS * (high - low)),
+        name="back_columns",
+    )(prod, wave, turn)
+
+
 def run_position(parts, chans, group, table):
     out_rows, depth = table.shape
+    cols = parts[0].shape[1]
     rows = out_rows // chans
     return pl.pallas_call(
         functools.partial(position_kernel, chans, group),
-        out_shape=(jax.ShapeDtypeStruct((rows, COLS), BF),) * chans,
+        out_shape=(jax.ShapeDtypeStruct((rows, cols), BF),) * chans,
         in_specs=[VMEM] * (group + 1),
         out_specs=(VMEM,) * chans,
-        scratch_shapes=[pltpu.VMEM((out_rows, COLS), BF)],
+        scratch_shapes=[pltpu.VMEM((out_rows, cols), BF)],
         compiler_params=params(12),
-        cost_estimate=cost(2 * out_rows * depth * COLS),
+        cost_estimate=cost(2 * out_rows * depth * cols),
         name="back_positions",
     )(*parts, table)
 
 
-def run_gate(parts, query, key, value, gain, group):
+def run_gate(parts, query, key, value, gain, group, low, high):
     chans, rows, _ = query.shape
     return pl.pallas_call(
-        functools.partial(gate_kernel, chans, group),
-        out_shape=tuple(
-            jax.ShapeDtypeStruct((chans, rows, high - low), BF)
-            for low, high in zip(CUTS[:-1], CUTS[1:])
-        ),
+        functools.partial(gate_kernel, chans, group, low, high),
+        out_shape=jax.ShapeDtypeStruct((chans, rows, high - low), BF),
         in_specs=[VMEM] * (chans + 3) + [SMEM],
-        out_specs=(VMEM,) * (len(CUTS) - 1),
+        out_specs=VMEM,
         compiler_params=params(12),
-        cost_estimate=cost(4 * chans * rows * COLS),
+        cost_estimate=cost(4 * chans * rows * (high - low)),
         name="gate",
     )(*parts, query, key, value, gain)
 
@@ -287,13 +392,14 @@
     weight = out_weight.astype(F32)
     mix = functools.partial(run_mix, planes, weight)
     swapped, gathered = gated
-    pair = lax.ppermute(swapped, "tp", [(0, 1), (1, 0), (2, 3), (3, 2)])
     far = lax.ppermute(gathered, "tp", [(0, 2), (3, 1)])
     mid = lax.ppermute(gathered, "tp", [(1, 2), (2, 1)])
-    edge = lax.ppermute(gathered, "tp", [(0, 1), (3, 2)])
+    pair = lax.ppermute(swapped, "tp", [(0, 1), (1, 0), (2, 3), (3, 2)])
     to_mid, to_far = mix((own_at, pair_at), ((mid_at, BF), (far_at, BF)), (swapped, pair))
     from_far = lax.ppermute(to_far, "tp", [(1, 3), (2, 0)])
     from_mid = lax.ppermute(to_mid, "tp", [(1, 2), (2, 1)])
+    gathered, _ = lax.optimization_barrier((gathered, to_mid))
+    edge = lax.ppermute(gathered, "tp", [(0, 1), (3, 2)])
     far, mid, to_mid, to_far = lax.optimization_barrier((far, mid, to_mid, to_far))
     (to_edge,) = mix((own_at, far_at, mid_at), ((edge_at, BF),), (gathered, far, mid))
     from_edge = lax.ppermute(to_edge, "tp", [(2, 3), (1, 0)])
@@ -303,14 +409,14 @@
     )
     done = (acc_swapped + from_far.astype(F32) + from_mid.astype(F32)).astype(BF)
     done, acc_gathered = lax.optimization_barrier((done, acc_gathered))
-    return [done, (acc_gathered + from_edge.astype(F32)).astype(BF)]
+    return run_finish(done, acc_gathered, from_edge)
 
 
 def gather_mix(gated, out_weight):
     plane = lax.axis_index("tp")
     outs = out_weight.shape[1] // lax.axis_size("tp")
     own_cols = lax.dynamic_slice_in_dim(out_weight, plane * outs, outs, 1)
-    return [
+    mixed = [
         jnp.einsum(
             "co,crl->orl",
             own_cols,
@@ -319,6 +425,7 @@
         ).astype(BF)
         for own in gated
     ]
+    return jnp.concatenate(mixed, 2).reshape(outs, -1)
 
 
 def local(query_gate, key_branch, value_branch, long_filter, skip_gain, out_weight):
@@ -327,7 +434,6 @@
     rows = tok_count // COLS
     group = ctx_count // chans
     length = ctx_count * tok_count
-    home = lax.axis_index("ctx") // group
     shape = (chans, rows, COLS)
     tables = run_tables(group, make_tables(ctx_count, group, chans, rows))
 
@@ -353,18 +459,28 @@
     query = query_gate.reshape(shape)
     key = key_branch.reshape(shape)
     value = value_branch.reshape(shape)
-    signal = (key.astype(F32) * value.astype(F32)).astype(BF)
-    pairs = jnp.stack([long_filter.astype(BF).reshape(shape), signal], 1)
-    blocks = [lax.dynamic_index_in_dim(pairs, home ^ rel, 0, False) for rel in range(chans)]
-    blocks = swap(blocks)
+    blocks = run_prepare(long_filter, key_branch, value_branch, group)
+    blocks = swap(list(blocks))
     blocks, tables = lax.optimization_barrier((blocks, tables))
     blocks += [shift(part, -step) for step in range(1, group) for part in blocks]
-    back = run_spectrum(blocks, chans, group, tables, 1.0 / length)
-    parts = [back] + [shift(back, -step) for step in range(1, group)]
-    parts = swap(list(run_position(parts, chans, group, tables[1])))
-    gated = run_gate(parts, query, key, value, skip_gain, group)
-    mixed = (line_mix if lax.axis_size("tp") == 4 else gather_mix)(gated, out_weight)
-    return jnp.concatenate(mixed, 2).reshape(-1, tok_count)
+    spans = list(zip(CUTS[:-1], CUTS[1:]))
+    prod, back = run_spectrum(blocks, chans, group, tables, 1.0 / length)
+    backs = [back] + [run_back(prod, tables, *span) for span in spans[1:]]
+    places = []
+    for back in backs:
+        parts = [back] + [shift(back, -step) for step in range(1, group)]
+        places.append(run_position(parts, chans, group, tables[1]))
+    gated = []
+    parts = swap(list(places[0]))
+    for number, span in enumerate(spans):
+        if number + 1 < len(spans):
+            parts, _ = lax.optimization_barrier((parts, places[number + 1]))
+        if number > 0:
+            parts, gated[-1] = lax.optimization_barrier((parts, gated[-1]))
+        gated.append(run_gate(parts, query, key, value, skip_gain, group, *span))
+        if number + 1 < len(spans):
+            parts = swap(list(places[number + 1]))
+    return (line_mix if lax.axis_size("tp") == 4 else gather_mix)(gated, out_weight)
 
 
 def solution(mesh):

time: 74.4 us -> 72.7 us (0.977)
  waiting for transfers between devices: 30.7 us -> 22.4 us
  Pallas kernels: 15.5 us -> 20.4 us
  starting transfers between devices: 22.5 us -> 26.6 us
  other arithmetic: 3.3 us -> 0.09 us
  local copies, waits for them, and re-layouts: 1.84 us -> 2.65 us
    pallas_call x1 -> x5, Pallas kernels: 0.85 us -> 6.02 us  [the longest x1 2.87 us: run_prepare(): pl.pallas_call(functools.partial(prepare_kernel, chans, group), out_shape...]
    ppermute x6 -> x9, waiting for transfers between devices: 15.2 us -> 10.4 us  [swap(): got.append(lax.ppermute(values[rel], 'ctx', pairs))]
    ppermute x6 -> x9, starting transfers between devices: 8.1 us -> 11.7 us  [swap(): got.append(lax.ppermute(values[rel], 'ctx', pairs))]
    convert_element_type x3 -> x0, other arithmetic: 3.05 us -> none  [the longest x1 1.57 us: local(): signal = (key.astype(F32) * value.astype(F32)).astype(BF)]
    ppermute x5 -> x6, waiting for transfers between devices: 4.16 us -> 2.26 us  [shift(): return lax.ppermute(value, 'ctx', pairs)]
    unnamed x20 -> x21, local copies, waits for them, and re-layouts: 1.35 us -> 2.36 us
    ppermute x5 -> x6, starting transfers between devices: 1.22 us -> 1.66 us  [shift(): return lax.ppermute(value, 'ctx', pairs)]
  transfers between devices with their start and end apart: 18 -> 22, of which waited for: 13 -> 12; matrix products, arithmetic and copies ran while one was open for 1% -> 1% of each run, Pallas kernels for 10% -> 15%
where the time goes in v4:
time: 72.7 us; the launch traced here: 72.4 us
  starting transfers between devices  26.6 us (37%)
  waiting for transfers between devices  22.4 us (31%)
  Pallas kernels  20.4 us (28%)
  local copies, waits for them, and re-layouts  2.65 us (4%)
    ppermute x9, starting transfers between devices, swap(): got.append(lax.ppermute(values[rel], 'ctx', pairs))  11.7 us
    ppermute x9, waiting for transfers between devices, swap(): got.append(lax.ppermute(values[rel], 'ctx', pairs))  10.4 us
    pallas_call x1, Pallas kernels, run_spectrum(): pl.pallas_call(functools.partial(spectrum_kernel, chans, group, scale), o...  5.63 us
    ppermute x1, waiting for transfers between devices, line_mix(): from_far = lax.ppermute(to_far, 'tp', [(1, 3), (2, 0)])  5.45 us
    pallas_call x4, Pallas kernels, run_mix(): pl.pallas_call(functools.partial(mix_kernel, chans, slots, outputs), out_...  5.21 us
    ppermute x1, starting transfers between devices, line_mix(): far = lax.ppermute(gathered, 'tp', [(0, 2), (3, 1)])  4.51 us
    ppermute x1, waiting for transfers between devices, line_mix(): from_edge = lax.ppermute(to_edge, 'tp', [(2, 3), (1, 0)])  4.27 us
    ppermute x1, starting transfers between devices, line_mix(): edge = lax.ppermute(gathered, 'tp', [(0, 1), (3, 2)])  3.27 us
  transfers between devices with their start and end apart: 22, of which 12 were waited for; matrix products, arithmetic and copies ran while one was open for 1% of the time, Pallas kernels for 15%

profile of v4, /device:TPU:0, one launch (start us, length us, event | category | flops | bytes accessed | tf_op | source)
XLA Modules:
  0.0 72.4 jit_solution(7285883318655117628)
XLA Ops:
  0.0 2.9 %prepare_blocks.1 = (bf16[2,128,512]{2,1,0:T(8,128)(2,1)}, bf16[2,128,512]{2,1,0:T(8,128)(2,1)}, bf16[2,128,512]{2,1,0:T(8,128)(2,1)}, bf16[2,128,512]{2,1,0:T(8,128)(2,1)}) custom-call(f32[4,65536]{1,0:T(4,128)} %refs_0_.2, bf16[4,65536]{1,0:T(4,128)(2,1)} %refs_1_.2, bf16[4,65536]{1,0:T(4,128)(2,1)} %refs_2_.2), custom_call_target="tpu_custom_call" | custom-call | flops 1048576 | tf_op jit(solution)/shard_map/prepare_blocks/pallas_call | solution.py:152
  2.9 3.0 %collective-permute-start = (bf16[2,128,512]{2,1,0:T(8,128)(2,1)}, bf16[2,128,512]{2,1,0:T(8,128)(2,1)S(1)}, u32[]{:S(2)}, u32[]{:S(2)}) collective-permute-start(bf16[2,128,512]{2,1,0:T(8,128)(2,1)} %get-tuple-element.48), channel_id=1, source_target_pairs={{0,8},{4,12},{8,0},{12,4},{16,24},{20,28},{24,16},{28,20},{1,9},{5... | collective-permute-start | bytes 786440 | tf_op jit(solution)/shard_map/ppermute | solution.py:448
  5.9 1.5 %collective-permute-start.1 = (bf16[2,128,512]{2,1,0:T(8,128)(2,1)}, bf16[2,128,512]{2,1,0:T(8,128)(2,1)S(1)}, u32[]{:S(2)}, u32[]{:S(2)}) collective-permute-start(bf16[2,128,512]{2,1,0:T(8,128)(2,1)} %get-tuple-element.49), channel_id=1, source_target_pairs={{0,16},{4,20},{8,24},{12,28},{16,0},{20,4},{24,8},{28,12},{1,17},{... | collective-permute-start | bytes 786440 | tf_op jit(solution)/shard_map/ppermute | solution.py:448
  7.4 2.2 %copy-done.2 = bf16[2,1024,1024]{2,1,0:T(8,128)(2,1)S(1)} copy-done((bf16[2,1024,1024]{2,1,0:T(8,128)(2,1)S(1)}, bf16[2,1024,1024]{2,1,0:T(8,128)(2,1)}, u32[]{:S(2)}) %copy-start.2) | copy-done | bytes 4194328
  9.7 2.1 %load_tables.1 = (bf16[1024,1024]{1,0:T(8,128)(2,1)S(1)}, bf16[512,2048]{1,0:T(8,128)(2,1)S(1)}, bf16[1024,512]{1,0:T(8,128)(2,1)S(1)}, f32[2,512,512]{2,1,0:T(8,128)S(1)}) custom-call(bf16[2,1024,1024]{2,1,0:T(8,128)(2,1)S(1)} %copy-done.2, bf16[2,512,2048]{2,1,0:T(8,128)(2,1)} %constant.23.clone.refs_1_, bf16[1024,512]{1,0:T(8,128)(2,1)S(1)} %copy-done.3, ...), custom_call_target="tpu_custom_call" | custom-call | flops 3000000000 | tf_op jit(solution)/shard_map/load_tables/pallas_call | solution.py:97
  11.7 1.5 %collective-permute-done.refs_1_ = bf16[2,128,512]{2,1,0:T(8,128)(2,1)S(1)} collective-permute-done((bf16[2,128,512]{2,1,0:T(8,128)(2,1)}, bf16[2,128,512]{2,1,0:T(8,128)(2,1)S(1)}, u32[]{:S(2)}, u32[]{:S(2)}) %collective-permute-start) | collective-permute-done | bytes 262176 | tf_op jit(solution)/shard_map/ppermute | solution.py:448
  13.2 6.2 %collective-permute-done.1.refs_2_ = bf16[2,128,512]{2,1,0:T(8,128)(2,1)S(1)} collective-permute-done((bf16[2,128,512]{2,1,0:T(8,128)(2,1)}, bf16[2,128,512]{2,1,0:T(8,128)(2,1)S(1)}, u32[]{:S(2)}, u32[]{:S(2)}) %collective-permute-start.1) | collective-permute-done | bytes 262176 | tf_op jit(solution)/shard_map/ppermute | solution.py:448
  22.2 5.6 %spectrum_product.1 = (bf16[512,1536]{1,0:T(8,128)(2,1)S(1)}, bf16[1024,256]{1,0:T(8,128)(2,1)S(1)}) custom-call(bf16[2,128,512]{2,1,0:T(8,128)(2,1)S(1)} %copy-done.1, bf16[2,128,512]{2,1,0:T(8,128)(2,1)S(1)} %collective-permute-done.refs_1_, bf16[2,128,512]{2,1,0:T(8,128)(2,1)S(1)} %collective-permute-done.1.refs_2_, ...), custom_call_target="tpu_custom_call" | custom-call | flops 5368709120 | tf_op jit(solution)/shard_map/spectrum_product/pallas_call | solution.py:287
  30.5 1.3 %collective-permute-start.12 = (bf16[128,256]{1,0:T(8,128)(2,1)S(1)}, bf16[128,256]{1,0:T(8,128)(2,1)S(1)}, u32[]{:S(2)}, u32[]{:S(2)}) collective-permute-start(bf16[128,256]{1,0:T(8,128)(2,1)S(1)} %get-tuple-element.70), channel_id=1, source_target_pairs={{0,8},{4,12},{8,0},{12,4},{16,24},{20,28},{24,16},{28,20},{1,9},{5... | collective-permute-start | bytes 196616 | tf_op jit(solution)/shard_map/ppermute | solution.py:448
  32.7 1.4 %collective-permute-start.14 = (bf16[128,256]{1,0:T(8,128)(2,1)S(1)}, bf16[128,256]{1,0:T(8,128)(2,1)S(1)}, u32[]{:S(2)}, u32[]{:S(2)}) collective-permute-start(bf16[128,256]{1,0:T(8,128)(2,1)S(1)} %get-tuple-element.72), channel_id=1, source_target_pairs={{0,24},{4,28},{8,16},{12,20},{16,8},{20,12},{24,0},{28,4},{1,25},{... | collective-permute-start | bytes 196616 | tf_op jit(solution)/shard_map/ppermute | solution.py:448
  34.8 1.6 %collective-permute-start.10 = (bf16[128,256]{1,0:T(8,128)(2,1)S(1)}, bf16[128,256]{1,0:T(8,128)(2,1)S(1)}, u32[]{:S(2)}, u32[]{:S(2)}) collective-permute-start(bf16[128,256]{1,0:T(8,128)(2,1)S(1)} %get-tuple-element.67), channel_id=1, source_target_pairs={{0,24},{4,28},{8,16},{12,20},{16,8},{20,12},{24,0},{28,4},{1,25},{... | collective-permute-start | bytes 196616 | tf_op jit(solution)/shard_map/ppermute | solution.py:448
  36.4 1.5 %collective-permute-start.8 = (bf16[128,256]{1,0:T(8,128)(2,1)S(1)}, bf16[128,256]{1,0:T(8,128)(2,1)S(1)}, u32[]{:S(2)}, u32[]{:S(2)}) collective-permute-start(bf16[128,256]{1,0:T(8,128)(2,1)S(1)} %get-tuple-element.65), channel_id=1, source_target_pairs={{0,8},{4,12},{8,0},{12,4},{16,24},{20,28},{24,16},{28,20},{1,9},{5... | collective-permute-start | bytes 196616 | tf_op jit(solution)/shard_map/ppermute | solution.py:448
  40.8 1.3 %collective-permute-done.9.refs_2_ = bf16[128,256]{1,0:T(8,128)(2,1)S(1)} collective-permute-done((bf16[128,256]{1,0:T(8,128)(2,1)S(1)}, bf16[128,256]{1,0:T(8,128)(2,1)S(1)}, u32[]{:S(2)}, u32[]{:S(2)}) %collective-permute-start.9) | collective-permute-done | bytes 65568 | tf_op jit(solution)/shard_map/ppermute | solution.py:448
  42.2 1.6 %collective-permute-start.15 = (bf16[4,128,256]{2,1,0:T(8,128)(2,1)S(1)}, bf16[4,128,256]{2,1,0:T(8,128)(2,1)S(1)}, u32[]{:S(2)}, u32[]{:S(2)}) collective-permute-start(bf16[4,128,256]{2,1,0:T(8,128)(2,1)S(1)} %gate.2.refs_0_), channel_id=1, source_target_pairs={{0,1},{1,0},{2,3},{3,2},{4,5},{5,4},{6,7},{7,6},{8,9},{9,8},{10,11... | collective-permute-start | bytes 786440 | tf_op jit(solution)/shard_map/ppermute | solution.py:397
  44.5 4.5 %collective-permute-start.18 = (bf16[4,128,256]{2,1,0:T(8,128)(2,1)S(1)}, bf16[4,128,256]{2,1,0:T(8,128)(2,1)S(1)}, u32[]{:S(2)}, u32[]{:S(2)}) collective-permute-start(bf16[4,128,256]{2,1,0:T(8,128)(2,1)S(1)} %gate.3.refs_0_), channel_id=1, source_target_pairs={{0,2},{3,1},{4,6},{7,5},{8,10},{11,9},{12,14},{15,13},{16,18},{19,... | collective-permute-start | bytes 786440 | tf_op jit(solution)/shard_map/ppermute | solution.py:395
  49.8 1.4 %mix_features.5 = (bf16[4,128,256]{2,1,0:T(8,128)(2,1)S(1)}, bf16[4,128,256]{2,1,0:T(8,128)(2,1)S(1)}) custom-call(s32[5]{0:T(128)S(1)} %stack.23.plane_ref, f32[16,16]{1,0:T(8,128)S(1)} %convert_element_type.12.weight_ref, bf16[4,128,256]{2,1,0:T(8,128)(2,1)S(1)} %gate.2.refs_0_, bf16[4,128,256]{2,1,0:T(8,128)(2,1)S(1)} %collective-permute-done.15.refs_1_), custom_call_target="tpu_custom_call" | custom-call | flops 4194304 | tf_op jit(solution)/shard_map/mix_features/pallas_call | solution.py:374
  51.2 3.3 %collective-permute-start.20 = (bf16[4,128,256]{2,1,0:T(8,128)(2,1)S(1)}, bf16[4,128,256]{2,1,0:T(8,128)(2,1)S(1)}, u32[]{:S(2)}, u32[]{:S(2)}) collective-permute-start(bf16[4,128,256]{2,1,0:T(8,128)(2,1)S(1)} %gate.3.refs_0_), channel_id=1, source_target_pairs={{0,1},{3,2},{4,5},{7,6},{8,9},{11,10},{12,13},{15,14},{16,17},{19,... | collective-permute-start | bytes 786440 | tf_op jit(solution)/shard_map/ppermute | solution.py:402
  54.5 1.3 %collective-permute-start.16 = (bf16[4,128,256]{2,1,0:T(8,128)(2,1)S(1)}, bf16[4,128,256]{2,1,0:T(8,128)(2,1)S(1)}, u32[]{:S(2)}, u32[]{:S(2)}) collective-permute-start(bf16[4,128,256]{2,1,0:T(8,128)(2,1)S(1)} %get-tuple-element.78), channel_id=1, source_target_pairs={{1,3},{2,0},{5,7},{6,4},{9,11},{10,8},{13,15},{14,12},{17,19},{18,... | collective-permute-start | bytes 786440 | tf_op jit(solution)/shard_map/ppermute | solution.py:399
  56.5 1.3 %mix_features.7 = bf16[4,128,256]{2,1,0:T(8,128)(2,1)S(1)} custom-call(s32[5]{0:T(128)S(1)} %stack.23.plane_ref, f32[16,16]{1,0:T(8,128)S(1)} %convert_element_type.12.weight_ref, bf16[4,128,256]{2,1,0:T(8,128)(2,1)S(1)} %gate.3.refs_0_, bf16[4,128,256]{2,1,0:T(8,128)(2,1)S(1)} %collective-permute-done.18.refs_1_, ...), custom_call_target="tpu_custom_call" | custom-call | flops 3145728 | tf_op jit(solution)/shard_map/mix_features/pallas_call | solution.py:374
  57.7 1.3 %collective-permute-start.21 = (bf16[4,128,256]{2,1,0:T(8,128)(2,1)S(1)}, bf16[4,128,256]{2,1,0:T(8,128)(2,1)S(1)}, u32[]{:S(2)}, u32[]{:S(2)}) collective-permute-start(bf16[4,128,256]{2,1,0:T(8,128)(2,1)S(1)} %mix_features.7), channel_id=1, source_target_pairs={{2,3},{1,0},{6,7},{5,4},{10,11},{9,8},{14,15},{13,12},{18,19},{17,... | collective-permute-start | bytes 786440 | tf_op jit(solution)/shard_map/ppermute | solution.py:405
  59.0 1.1 %mix_features.4 = f32[4,128,256]{2,1,0:T(8,128)S(1)} custom-call(s32[5]{0:T(128)S(1)} %stack.23.plane_ref, f32[16,16]{1,0:T(8,128)S(1)} %convert_element_type.12.weight_ref, bf16[4,128,256]{2,1,0:T(8,128)(2,1)S(1)} %gate.2.refs_0_, bf16[4,128,256]{2,1,0:T(8,128)(2,1)S(1)} %collective-permute-done.15.refs_1_), custom_call_target="tpu_custom_call" | custom-call | flops 2097152 | tf_op jit(solution)/shard_map/mix_features/pallas_call | solution.py:374
  60.1 1.5 %mix_features.6.acc_ref = f32[4,128,256]{2,1,0:T(8,128)S(1)} custom-call(s32[5]{0:T(128)S(1)} %stack.23.plane_ref, f32[16,16]{1,0:T(8,128)S(1)} %convert_element_type.12.weight_ref, bf16[4,128,256]{2,1,0:T(8,128)(2,1)S(1)} %gate.3.refs_0_, bf16[4,128,256]{2,1,0:T(8,128)(2,1)S(1)} %collective-permute-done.18.refs_1_, ...), custom_call_target="tpu_custom_call" | custom-call | flops 4194304 | tf_op jit(solution)/shard_map/mix_features/pallas_call | solution.py:374
  61.6 5.5 %collective-permute-done.16 = bf16[4,128,256]{2,1,0:T(8,128)(2,1)S(1)} collective-permute-done((bf16[4,128,256]{2,1,0:T(8,128)(2,1)S(1)}, bf16[4,128,256]{2,1,0:T(8,128)(2,1)S(1)}, u32[]{:S(2)}, u32[]{:S(2)}) %collective-permute-start.16) | collective-permute-done | bytes 262176 | tf_op jit(solution)/shard_map/ppermute | solution.py:399
  67.2 4.3 %collective-permute-done.21.got_ref = bf16[4,128,256]{2,1,0:T(8,128)(2,1)S(1)} collective-permute-done((bf16[4,128,256]{2,1,0:T(8,128)(2,1)S(1)}, bf16[4,128,256]{2,1,0:T(8,128)(2,1)S(1)}, u32[]{:S(2)}, u32[]{:S(2)}) %collective-permute-start.21) | collective-permute-done | bytes 262176 | tf_op jit(solution)/shard_map/ppermute | solution.py:405
  (58 shorter events, 13.1 us)
Async XLA Ops:
  2.9 10.4 %collective-permute-start = (bf16[2,128,512]{2,1,0:T(8,128)(2,1)}, bf16[2,128,512]{2,1,0:T(8,128)(2,1)S(1)}, u32[]{:S(2)}, u32[]{:S(2)}) collective-permute-start(bf16[2,128,512]{2,1,0:T(8,128)(2,1)} %get-tuple-element.48), channel_id=1, source_target_pairs={{0,8},{4,12},{8,0},{12,4},{16,24},{20,28},{24,16},{28,20},{1,9},{5... | collective-permute-start | bytes 786440 | tf_op jit(solution)/shard_map/ppermute | solution.py:448
  5.9 13.6 %collective-permute-start.1 = (bf16[2,128,512]{2,1,0:T(8,128)(2,1)}, bf16[2,128,512]{2,1,0:T(8,128)(2,1)S(1)}, u32[]{:S(2)}, u32[]{:S(2)}) collective-permute-start(bf16[2,128,512]{2,1,0:T(8,128)(2,1)} %get-tuple-element.49), channel_id=1, source_target_pairs={{0,16},{4,20},{8,24},{12,28},{16,0},{20,4},{24,8},{28,12},{1,17},{... | collective-permute-start | bytes 786440 | tf_op jit(solution)/shard_map/ppermute | solution.py:448
  7.4 12.1 %copy-start.1 = (bf16[2,128,512]{2,1,0:T(8,128)(2,1)S(1)}, bf16[2,128,512]{2,1,0:T(8,128)(2,1)}, u32[]{:S(2)}) copy-start(bf16[2,128,512]{2,1,0:T(8,128)(2,1)} %get-tuple-element.55.refs_0_) | copy-start | bytes 786436
  7.4 12.1 %collective-permute-start.2 = (bf16[2,128,512]{2,1,0:T(8,128)(2,1)}, bf16[2,128,512]{2,1,0:T(8,128)(2,1)S(1)}, u32[]{:S(2)}, u32[]{:S(2)}) collective-permute-start(bf16[2,128,512]{2,1,0:T(8,128)(2,1)} %get-tuple-element.50), channel_id=1, source_target_pairs={{0,24},{4,28},{8,16},{12,20},{16,8},{20,12},{24,0},{28,4},{1,25},{... | collective-permute-start | bytes 786440 | tf_op jit(solution)/shard_map/ppermute | solution.py:448
  19.5 1.5 %collective-permute-start.3 = (bf16[2,128,512]{2,1,0:T(8,128)(2,1)S(1)}, bf16[2,128,512]{2,1,0:T(8,128)(2,1)S(1)}, u32[]{:S(2)}, u32[]{:S(2)}) collective-permute-start(bf16[2,128,512]{2,1,0:T(8,128)(2,1)S(1)} %copy-done.1), channel_id=1, source_target_pairs={{0,4},{4,0},{8,12},{12,8},{16,20},{20,16},{24,28},{28,24},{1,5},{5... | collective-permute-start | bytes 786440 | tf_op jit(solution)/shard_map/ppermute | solution.py:457
  19.5 1.9 %collective-permute-start.4 = (bf16[2,128,512]{2,1,0:T(8,128)(2,1)S(1)}, bf16[2,128,512]{2,1,0:T(8,128)(2,1)S(1)}, u32[]{:S(2)}, u32[]{:S(2)}) collective-permute-start(bf16[2,128,512]{2,1,0:T(8,128)(2,1)S(1)} %collective-permute-done.refs_1_), channel_id=1, source_target_pairs={{0,4},{4,0},{8,12},{12,8},{16,20},{20,16},{24,28},{28,24},{1,5},{5... | collective-permute-start | bytes 786440 | tf_op jit(solution)/shard_map/ppermute | solution.py:457
  20.0 1.8 %collective-permute-start.5 = (bf16[2,128,512]{2,1,0:T(8,128)(2,1)S(1)}, bf16[2,128,512]{2,1,0:T(8,128)(2,1)S(1)}, u32[]{:S(2)}, u32[]{:S(2)}) collective-permute-start(bf16[2,128,512]{2,1,0:T(8,128)(2,1)S(1)} %collective-permute-done.1.refs_2_), channel_id=1, source_target_pairs={{0,4},{4,0},{8,12},{12,8},{16,20},{20,16},{24,28},{28,24},{1,5},{5... | collective-permute-start | bytes 786440 | tf_op jit(solution)/shard_map/ppermute | solution.py:457
  20.1 2.1 %collective-permute-start.6 = (bf16[2,128,512]{2,1,0:T(8,128)(2,1)S(1)}, bf16[2,128,512]{2,1,0:T(8,128)(2,1)S(1)}, u32[]{:S(2)}, u32[]{:S(2)}) collective-permute-start(bf16[2,128,512]{2,1,0:T(8,128)(2,1)S(1)} %collective-permute-done.2.refs_3_), channel_id=1, source_target_pairs={{0,4},{4,0},{8,12},{12,8},{16,20},{20,16},{24,28},{28,24},{1,5},{5... | collective-permute-start | bytes 786440 | tf_op jit(solution)/shard_map/ppermute | solution.py:457
  27.8 2.0 %collective-permute-start.11 = (bf16[1024,256]{1,0:T(8,128)(2,1)S(1)}, bf16[1024,256]{1,0:T(8,128)(2,1)S(1)}, u32[]{:S(2)}, u32[]{:S(2)}) collective-permute-start(bf16[1024,256]{1,0:T(8,128)(2,1)S(1)} %get-tuple-element.68.refs_0_), channel_id=1, source_target_pairs={{0,4},{4,0},{8,12},{12,8},{16,20},{20,16},{24,28},{28,24},{1,5},{5... | collective-permute-start | bytes 1572872 | tf_op jit(solution)/shard_map/ppermute | solution.py:457
  28.7 5.4 %collective-permute-start.7 = (bf16[1024,256]{1,0:T(8,128)(2,1)S(1)}, bf16[1024,256]{1,0:T(8,128)(2,1)S(1)}, u32[]{:S(2)}, u32[]{:S(2)}) collective-permute-start(bf16[1024,256]{1,0:T(8,128)(2,1)S(1)} %back_columns.1.refs_0_), channel_id=1, source_target_pairs={{0,4},{4,0},{8,12},{12,8},{16,20},{20,16},{24,28},{28,24},{1,5},{5... | collective-permute-start | bytes 1572872 | tf_op jit(solution)/shard_map/ppermute | solution.py:457
  30.5 7.4 %collective-permute-start.12 = (bf16[128,256]{1,0:T(8,128)(2,1)S(1)}, bf16[128,256]{1,0:T(8,128)(2,1)S(1)}, u32[]{:S(2)}, u32[]{:S(2)}) collective-permute-start(bf16[128,256]{1,0:T(8,128)(2,1)S(1)} %get-tuple-element.70), channel_id=1, source_target_pairs={{0,8},{4,12},{8,0},{12,4},{16,24},{20,28},{24,16},{28,20},{1,9},{5... | collective-permute-start | bytes 196616 | tf_op jit(solution)/shard_map/ppermute | solution.py:448
  31.8 6.9 %collective-permute-start.13 = (bf16[128,256]{1,0:T(8,128)(2,1)S(1)}, bf16[128,256]{1,0:T(8,128)(2,1)S(1)}, u32[]{:S(2)}, u32[]{:S(2)}) collective-permute-start(bf16[128,256]{1,0:T(8,128)(2,1)S(1)} %get-tuple-element.71), channel_id=1, source_target_pairs={{0,16},{4,20},{8,24},{12,28},{16,0},{20,4},{24,8},{28,12},{1,17},{... | collective-permute-start | bytes 196616 | tf_op jit(solution)/shard_map/ppermute | solution.py:448
  32.7 6.1 %collective-permute-start.14 = (bf16[128,256]{1,0:T(8,128)(2,1)S(1)}, bf16[128,256]{1,0:T(8,128)(2,1)S(1)}, u32[]{:S(2)}, u32[]{:S(2)}) collective-permute-start(bf16[128,256]{1,0:T(8,128)(2,1)S(1)} %get-tuple-element.72), channel_id=1, source_target_pairs={{0,24},{4,28},{8,16},{12,20},{16,8},{20,12},{24,0},{28,4},{1,25},{... | collective-permute-start | bytes 196616 | tf_op jit(solution)/shard_map/ppermute | solution.py:448
  34.8 5.3 %collective-permute-start.10 = (bf16[128,256]{1,0:T(8,128)(2,1)S(1)}, bf16[128,256]{1,0:T(8,128)(2,1)S(1)}, u32[]{:S(2)}, u32[]{:S(2)}) collective-permute-start(bf16[128,256]{1,0:T(8,128)(2,1)S(1)} %get-tuple-element.67), channel_id=1, source_target_pairs={{0,24},{4,28},{8,16},{12,20},{16,8},{20,12},{24,0},{28,4},{1,25},{... | collective-permute-start | bytes 196616 | tf_op jit(solution)/shard_map/ppermute | solution.py:448
  36.4 4.4 %collective-permute-start.8 = (bf16[128,256]{1,0:T(8,128)(2,1)S(1)}, bf16[128,256]{1,0:T(8,128)(2,1)S(1)}, u32[]{:S(2)}, u32[]{:S(2)}) collective-permute-start(bf16[128,256]{1,0:T(8,128)(2,1)S(1)} %get-tuple-element.65), channel_id=1, source_target_pairs={{0,8},{4,12},{8,0},{12,4},{16,24},{20,28},{24,16},{28,20},{1,9},{5... | collective-permute-start | bytes 196616 | tf_op jit(solution)/shard_map/ppermute | solution.py:448
  37.9 4.3 %collective-permute-start.9 = (bf16[128,256]{1,0:T(8,128)(2,1)S(1)}, bf16[128,256]{1,0:T(8,128)(2,1)S(1)}, u32[]{:S(2)}, u32[]{:S(2)}) collective-permute-start(bf16[128,256]{1,0:T(8,128)(2,1)S(1)} %get-tuple-element.66), channel_id=1, source_target_pairs={{0,16},{4,20},{8,24},{12,28},{16,0},{20,4},{24,8},{28,12},{1,17},{... | collective-permute-start | bytes 196616 | tf_op jit(solution)/shard_map/ppermute | solution.py:448
  38.7 10.9 %copy-start.9 = (bf16[16,16]{1,0:T(8,128)(2,1)S(1)}, bf16[16,16]{1,0:T(8,128)(2,1)}, u32[]{:S(2)}) copy-start(bf16[16,16]{1,0:T(8,128)(2,1)} %param.16) | copy-start | bytes 1540
  42.2 7.6 %collective-permute-start.15 = (bf16[4,128,256]{2,1,0:T(8,128)(2,1)S(1)}, bf16[4,128,256]{2,1,0:T(8,128)(2,1)S(1)}, u32[]{:S(2)}, u32[]{:S(2)}) collective-permute-start(bf16[4,128,256]{2,1,0:T(8,128)(2,1)S(1)} %gate.2.refs_0_), channel_id=1, source_target_pairs={{0,1},{1,0},{2,3},{3,2},{4,5},{5,4},{6,7},{7,6},{8,9},{9,8},{10,11... | collective-permute-start | bytes 786440 | tf_op jit(solution)/shard_map/ppermute | solution.py:397
  44.5 12.0 %collective-permute-start.18 = (bf16[4,128,256]{2,1,0:T(8,128)(2,1)S(1)}, bf16[4,128,256]{2,1,0:T(8,128)(2,1)S(1)}, u32[]{:S(2)}, u32[]{:S(2)}) collective-permute-start(bf16[4,128,256]{2,1,0:T(8,128)(2,1)S(1)} %gate.3.refs_0_), channel_id=1, source_target_pairs={{0,2},{3,1},{4,6},{7,5},{8,10},{11,9},{12,14},{15,13},{16,18},{19,... | collective-permute-start | bytes 786440 | tf_op jit(solution)/shard_map/ppermute | solution.py:395
  49.0 7.5 %collective-permute-start.19 = (bf16[4,128,256]{2,1,0:T(8,128)(2,1)S(1)}, bf16[4,128,256]{2,1,0:T(8,128)(2,1)S(1)}, u32[]{:S(2)}, u32[]{:S(2)}) collective-permute-start(bf16[4,128,256]{2,1,0:T(8,128)(2,1)S(1)} %gate.3.refs_0_), channel_id=1, source_target_pairs={{1,2},{2,1},{5,6},{6,5},{9,10},{10,9},{13,14},{14,13},{17,18},{18,... | collective-permute-start | bytes 786440 | tf_op jit(solution)/shard_map/ppermute | solution.py:396
  51.2 9.0 %collective-permute-start.20 = (bf16[4,128,256]{2,1,0:T(8,128)(2,1)S(1)}, bf16[4,128,256]{2,1,0:T(8,128)(2,1)S(1)}, u32[]{:S(2)}, u32[]{:S(2)}) collective-permute-start(bf16[4,128,256]{2,1,0:T(8,128)(2,1)S(1)} %gate.3.refs_0_), channel_id=1, source_target_pairs={{0,1},{3,2},{4,5},{7,6},{8,9},{11,10},{12,13},{15,14},{16,17},{19,... | collective-permute-start | bytes 786440 | tf_op jit(solution)/shard_map/ppermute | solution.py:402
  54.5 12.6 %collective-permute-start.16 = (bf16[4,128,256]{2,1,0:T(8,128)(2,1)S(1)}, bf16[4,128,256]{2,1,0:T(8,128)(2,1)S(1)}, u32[]{:S(2)}, u32[]{:S(2)}) collective-permute-start(bf16[4,128,256]{2,1,0:T(8,128)(2,1)S(1)} %get-tuple-element.78), channel_id=1, source_target_pairs={{1,3},{2,0},{5,7},{6,4},{9,11},{10,8},{13,15},{14,12},{17,19},{18,... | collective-permute-start | bytes 786440 | tf_op jit(solution)/shard_map/ppermute | solution.py:399
  55.8 11.3 %collective-permute-start.17 = (bf16[4,128,256]{2,1,0:T(8,128)(2,1)S(1)}, bf16[4,128,256]{2,1,0:T(8,128)(2,1)S(1)}, u32[]{:S(2)}, u32[]{:S(2)}) collective-permute-start(bf16[4,128,256]{2,1,0:T(8,128)(2,1)S(1)} %get-tuple-element.79), channel_id=1, source_target_pairs={{1,2},{2,1},{5,6},{6,5},{9,10},{10,9},{13,14},{14,13},{17,18},{18,... | collective-permute-start | bytes 786440 | tf_op jit(solution)/shard_map/ppermute | solution.py:400
  57.7 13.7 %collective-permute-start.21 = (bf16[4,128,256]{2,1,0:T(8,128)(2,1)S(1)}, bf16[4,128,256]{2,1,0:T(8,128)(2,1)S(1)}, u32[]{:S(2)}, u32[]{:S(2)}) collective-permute-start(bf16[4,128,256]{2,1,0:T(8,128)(2,1)S(1)} %mix_features.7), channel_id=1, source_target_pairs={{2,3},{1,0},{6,7},{5,4},{10,11},{9,8},{14,15},{13,12},{18,19},{17,... | collective-permute-start | bytes 786440 | tf_op jit(solution)/shard_map/ppermute | solution.py:405
  (8 other events, 50.2 us)

commit v5 on v4

--- a/solution.py
+++ b/solution.py
@@ -461,7 +461,7 @@
     value = value_branch.reshape(shape)
     blocks = run_prepare(long_filter, key_branch, value_branch, group)
     blocks = swap(list(blocks))
-    blocks, tables = lax.optimization_barrier((blocks, tables))
+    blocks[-1], tables = lax.optimization_barrier((blocks[-1], tables))
     blocks += [shift(part, -step) for step in range(1, group) for part in blocks]
     spans = list(zip(CUTS[:-1], CUTS[1:]))
     prod, back = run_spectrum(blocks, chans, group, tables, 1.0 / length)

time: 72.7 us -> 71 us (0.977)
  waiting for transfers between devices: 22.4 us -> 21.3 us
    ppermute x9, waiting for transfers between devices: 10.4 us -> 9.67 us  [swap(): got.append(lax.ppermute(values[rel], 'ctx', pairs))]
  transfers between devices with their start and end apart: 22 -> 22, of which waited for: 12 -> 11; matrix products, arithmetic and copies ran while one was open for 1% -> 1% of each run, Pallas kernels for 15% -> 15%
where the time goes in v5:
time: 71 us; the launch traced here: 70.7 us
  starting transfers between devices  26 us (37%)
  waiting for transfers between devices  21.3 us (30%)
  Pallas kernels  20.4 us (29%)
  local copies, waits for them, and re-layouts  2.64 us (4%)
    ppermute x9, starting transfers between devices, swap(): got.append(lax.ppermute(values[rel], 'ctx', pairs))  11.7 us
    ppermute x9, waiting for transfers between devices, swap(): got.append(lax.ppermute(values[rel], 'ctx', pairs))  9.67 us
    pallas_call x1, Pallas kernels, run_spectrum(): pl.pallas_call(functools.partial(spectrum_kernel, chans, group, scale), o...  5.64 us
    ppermute x1, waiting for transfers between devices, line_mix(): from_far = lax.ppermute(to_far, 'tp', [(1, 3), (2, 0)])  5.44 us
    pallas_call x4, Pallas kernels, run_mix(): pl.pallas_call(functools.partial(mix_kernel, chans, slots, outputs), out_...  5.21 us
    ppermute x1, starting transfers between devices, line_mix(): far = lax.ppermute(gathered, 'tp', [(0, 2), (3, 1)])  4.51 us
    ppermute x1, waiting for transfers between devices, line_mix(): from_edge = lax.ppermute(to_edge, 'tp', [(2, 3), (1, 0)])  4.18 us
    ppermute x1, starting transfers between devices, line_mix(): edge = lax.ppermute(gathered, 'tp', [(0, 1), (3, 2)])  3.11 us
  transfers between devices with their start and end apart: 22, of which 11 were waited for; matrix products, arithmetic and copies ran while one was open for 1% of the time, Pallas kernels for 15%

profile of v5, /device:TPU:0, one launch (start us, length us, event | category | flops | bytes accessed | tf_op | source)
XLA Modules:
  0.0 70.7 jit_solution(17599240871717182184)
XLA Ops:
  0.0 2.9 %prepare_blocks.1 = (bf16[2,128,512]{2,1,0:T(8,128)(2,1)}, bf16[2,128,512]{2,1,0:T(8,128)(2,1)}, bf16[2,128,512]{2,1,0:T(8,128)(2,1)}, bf16[2,128,512]{2,1,0:T(8,128)(2,1)}) custom-call(f32[4,65536]{1,0:T(4,128)} %refs_0_.2, bf16[4,65536]{1,0:T(4,128)(2,1)} %refs_1_.2, bf16[4,65536]{1,0:T(4,128)(2,1)} %refs_2_.2), custom_call_target="tpu_custom_call" | custom-call | flops 1048576 | tf_op jit(solution)/shard_map/prepare_blocks/pallas_call | solution.py:152
  2.9 4.0 %collective-permute-start.2 = (bf16[2,128,512]{2,1,0:T(8,128)(2,1)}, bf16[2,128,512]{2,1,0:T(8,128)(2,1)S(1)}, u32[]{:S(2)}, u32[]{:S(2)}) collective-permute-start(bf16[2,128,512]{2,1,0:T(8,128)(2,1)} %get-tuple-element.47), channel_id=1, source_target_pairs={{0,24},{4,28},{8,16},{12,20},{16,8},{20,12},{24,0},{28,4},{1,25},{... | collective-permute-start | bytes 786440 | tf_op jit(solution)/shard_map/ppermute | solution.py:448
  7.5 2.2 %copy-done.2 = bf16[2,1024,1024]{2,1,0:T(8,128)(2,1)S(1)} copy-done((bf16[2,1024,1024]{2,1,0:T(8,128)(2,1)S(1)}, bf16[2,1024,1024]{2,1,0:T(8,128)(2,1)}, u32[]{:S(2)}) %copy-start.2) | copy-done | bytes 4194328
  9.7 2.1 %load_tables.1 = (bf16[1024,1024]{1,0:T(8,128)(2,1)S(1)}, bf16[512,2048]{1,0:T(8,128)(2,1)S(1)}, bf16[1024,512]{1,0:T(8,128)(2,1)S(1)}, f32[2,512,512]{2,1,0:T(8,128)S(1)}) custom-call(bf16[2,1024,1024]{2,1,0:T(8,128)(2,1)S(1)} %copy-done.2, bf16[2,512,2048]{2,1,0:T(8,128)(2,1)} %constant.23.clone.refs_1_, bf16[1024,512]{1,0:T(8,128)(2,1)S(1)} %copy-done.3, ...), custom_call_target="tpu_custom_call" | custom-call | flops 3000000000 | tf_op jit(solution)/shard_map/load_tables/pallas_call | solution.py:97
  11.8 2.4 %collective-permute-done.2.refs_3_ = bf16[2,128,512]{2,1,0:T(8,128)(2,1)S(1)} collective-permute-done((bf16[2,128,512]{2,1,0:T(8,128)(2,1)}, bf16[2,128,512]{2,1,0:T(8,128)(2,1)S(1)}, u32[]{:S(2)}, u32[]{:S(2)}) %collective-permute-start.2) | collective-permute-done | bytes 262176 | tf_op jit(solution)/shard_map/ppermute | solution.py:448
  14.2 5.0 %collective-permute-done.refs_1_ = bf16[2,128,512]{2,1,0:T(8,128)(2,1)S(1)} collective-permute-done((bf16[2,128,512]{2,1,0:T(8,128)(2,1)}, bf16[2,128,512]{2,1,0:T(8,128)(2,1)S(1)}, u32[]{:S(2)}, u32[]{:S(2)}) %collective-permute-start) | collective-permute-done | bytes 262176 | tf_op jit(solution)/shard_map/ppermute | solution.py:448
  19.8 1.0 %collective-permute-done.4.refs_5_ = bf16[2,128,512]{2,1,0:T(8,128)(2,1)S(1)} collective-permute-done((bf16[2,128,512]{2,1,0:T(8,128)(2,1)S(1)}, bf16[2,128,512]{2,1,0:T(8,128)(2,1)S(1)}, u32[]{:S(2)}, u32[]{:S(2)}) %collective-permute-start.4) | collective-permute-done | bytes 262176 | tf_op jit(solution)/shard_map/ppermute | solution.py:457
  21.2 5.6 %spectrum_product.1 = (bf16[512,1536]{1,0:T(8,128)(2,1)S(1)}, bf16[1024,256]{1,0:T(8,128)(2,1)S(1)}) custom-call(bf16[2,128,512]{2,1,0:T(8,128)(2,1)S(1)} %copy-done.1, bf16[2,128,512]{2,1,0:T(8,128)(2,1)S(1)} %collective-permute-done.refs_1_, bf16[2,128,512]{2,1,0:T(8,128)(2,1)S(1)} %collective-permute-done.1.refs_2_, ...), custom_call_target="tpu_custom_call" | custom-call | flops 5368709120 | tf_op jit(solution)/shard_map/spectrum_product/pallas_call | solution.py:287
  29.6 1.5 %collective-permute-start.12 = (bf16[128,256]{1,0:T(8,128)(2,1)S(1)}, bf16[128,256]{1,0:T(8,128)(2,1)S(1)}, u32[]{:S(2)}, u32[]{:S(2)}) collective-permute-start(bf16[128,256]{1,0:T(8,128)(2,1)S(1)} %get-tuple-element.64), channel_id=1, source_target_pairs={{0,8},{4,12},{8,0},{12,4},{16,24},{20,28},{24,16},{28,20},{1,9},{5... | collective-permute-start | bytes 196616 | tf_op jit(solution)/shard_map/ppermute | solution.py:448
  31.1 1.1 %collective-permute-start.13 = (bf16[128,256]{1,0:T(8,128)(2,1)S(1)}, bf16[128,256]{1,0:T(8,128)(2,1)S(1)}, u32[]{:S(2)}, u32[]{:S(2)}) collective-permute-start(bf16[128,256]{1,0:T(8,128)(2,1)S(1)} %get-tuple-element.65), channel_id=1, source_target_pairs={{0,16},{4,20},{8,24},{12,28},{16,0},{20,4},{24,8},{28,12},{1,17},{... | collective-permute-start | bytes 196616 | tf_op jit(solution)/shard_map/ppermute | solution.py:448
  33.9 2.0 %collective-permute-start.10 = (bf16[128,256]{1,0:T(8,128)(2,1)S(1)}, bf16[128,256]{1,0:T(8,128)(2,1)S(1)}, u32[]{:S(2)}, u32[]{:S(2)}) collective-permute-start(bf16[128,256]{1,0:T(8,128)(2,1)S(1)} %get-tuple-element.61), channel_id=1, source_target_pairs={{0,24},{4,28},{8,16},{12,20},{16,8},{20,12},{24,0},{28,4},{1,25},{... | collective-permute-start | bytes 196616 | tf_op jit(solution)/shard_map/ppermute | solution.py:448
  36.4 1.0 %collective-permute-start.9 = (bf16[128,256]{1,0:T(8,128)(2,1)S(1)}, bf16[128,256]{1,0:T(8,128)(2,1)S(1)}, u32[]{:S(2)}, u32[]{:S(2)}) collective-permute-start(bf16[128,256]{1,0:T(8,128)(2,1)S(1)} %get-tuple-element.60), channel_id=1, source_target_pairs={{0,16},{4,20},{8,24},{12,28},{16,0},{20,4},{24,8},{28,12},{1,17},{... | collective-permute-start | bytes 196616 | tf_op jit(solution)/shard_map/ppermute | solution.py:448
  40.7 1.6 %collective-permute-start.15 = (bf16[4,128,256]{2,1,0:T(8,128)(2,1)S(1)}, bf16[4,128,256]{2,1,0:T(8,128)(2,1)S(1)}, u32[]{:S(2)}, u32[]{:S(2)}) collective-permute-start(bf16[4,128,256]{2,1,0:T(8,128)(2,1)S(1)} %gate.2.refs_0_), channel_id=1, source_target_pairs={{0,1},{1,0},{2,3},{3,2},{4,5},{5,4},{6,7},{7,6},{8,9},{9,8},{10,11... | collective-permute-start | bytes 786440 | tf_op jit(solution)/shard_map/ppermute | solution.py:397
  43.0 4.5 %collective-permute-start.18 = (bf16[4,128,256]{2,1,0:T(8,128)(2,1)S(1)}, bf16[4,128,256]{2,1,0:T(8,128)(2,1)S(1)}, u32[]{:S(2)}, u32[]{:S(2)}) collective-permute-start(bf16[4,128,256]{2,1,0:T(8,128)(2,1)S(1)} %gate.3.refs_0_), channel_id=1, source_target_pairs={{0,2},{3,1},{4,6},{7,5},{8,10},{11,9},{12,14},{15,13},{16,18},{19,... | collective-permute-start | bytes 786440 | tf_op jit(solution)/shard_map/ppermute | solution.py:395
  48.3 1.4 %mix_features.5 = (bf16[4,128,256]{2,1,0:T(8,128)(2,1)S(1)}, bf16[4,128,256]{2,1,0:T(8,128)(2,1)S(1)}) custom-call(s32[5]{0:T(128)S(1)} %stack.23.plane_ref, f32[16,16]{1,0:T(8,128)S(1)} %convert_element_type.12.weight_ref, bf16[4,128,256]{2,1,0:T(8,128)(2,1)S(1)} %gate.2.refs_0_, bf16[4,128,256]{2,1,0:T(8,128)(2,1)S(1)} %collective-permute-done.15.refs_1_), custom_call_target="tpu_custom_call" | custom-call | flops 4194304 | tf_op jit(solution)/shard_map/mix_features/pallas_call | solution.py:374
  49.7 3.1 %collective-permute-start.20 = (bf16[4,128,256]{2,1,0:T(8,128)(2,1)S(1)}, bf16[4,128,256]{2,1,0:T(8,128)(2,1)S(1)}, u32[]{:S(2)}, u32[]{:S(2)}) collective-permute-start(bf16[4,128,256]{2,1,0:T(8,128)(2,1)S(1)} %gate.3.refs_0_), channel_id=1, source_target_pairs={{0,1},{3,2},{4,5},{7,6},{8,9},{11,10},{12,13},{15,14},{16,17},{19,... | collective-permute-start | bytes 786440 | tf_op jit(solution)/shard_map/ppermute | solution.py:402
  52.9 1.3 %collective-permute-start.16 = (bf16[4,128,256]{2,1,0:T(8,128)(2,1)S(1)}, bf16[4,128,256]{2,1,0:T(8,128)(2,1)S(1)}, u32[]{:S(2)}, u32[]{:S(2)}) collective-permute-start(bf16[4,128,256]{2,1,0:T(8,128)(2,1)S(1)} %get-tuple-element.72), channel_id=1, source_target_pairs={{1,3},{2,0},{5,7},{6,4},{9,11},{10,8},{13,15},{14,12},{17,19},{18,... | collective-permute-start | bytes 786440 | tf_op jit(solution)/shard_map/ppermute | solution.py:399
  54.9 1.3 %mix_features.7 = bf16[4,128,256]{2,1,0:T(8,128)(2,1)S(1)} custom-call(s32[5]{0:T(128)S(1)} %stack.23.plane_ref, f32[16,16]{1,0:T(8,128)S(1)} %convert_element_type.12.weight_ref, bf16[4,128,256]{2,1,0:T(8,128)(2,1)S(1)} %gate.3.refs_0_, bf16[4,128,256]{2,1,0:T(8,128)(2,1)S(1)} %collective-permute-done.18.refs_1_, ...), custom_call_target="tpu_custom_call" | custom-call | flops 3145728 | tf_op jit(solution)/shard_map/mix_features/pallas_call | solution.py:374
  56.1 1.3 %collective-permute-start.21 = (bf16[4,128,256]{2,1,0:T(8,128)(2,1)S(1)}, bf16[4,128,256]{2,1,0:T(8,128)(2,1)S(1)}, u32[]{:S(2)}, u32[]{:S(2)}) collective-permute-start(bf16[4,128,256]{2,1,0:T(8,128)(2,1)S(1)} %mix_features.7), channel_id=1, source_target_pairs={{2,3},{1,0},{6,7},{5,4},{10,11},{9,8},{14,15},{13,12},{18,19},{17,... | collective-permute-start | bytes 786440 | tf_op jit(solution)/shard_map/ppermute | solution.py:405
  57.4 1.1 %mix_features.4 = f32[4,128,256]{2,1,0:T(8,128)S(1)} custom-call(s32[5]{0:T(128)S(1)} %stack.23.plane_ref, f32[16,16]{1,0:T(8,128)S(1)} %convert_element_type.12.weight_ref, bf16[4,128,256]{2,1,0:T(8,128)(2,1)S(1)} %gate.2.refs_0_, bf16[4,128,256]{2,1,0:T(8,128)(2,1)S(1)} %collective-permute-done.15.refs_1_), custom_call_target="tpu_custom_call" | custom-call | flops 2097152 | tf_op jit(solution)/shard_map/mix_features/pallas_call | solution.py:374
  58.5 1.5 %mix_features.6.acc_ref = f32[4,128,256]{2,1,0:T(8,128)S(1)} custom-call(s32[5]{0:T(128)S(1)} %stack.23.plane_ref, f32[16,16]{1,0:T(8,128)S(1)} %convert_element_type.12.weight_ref, bf16[4,128,256]{2,1,0:T(8,128)(2,1)S(1)} %gate.3.refs_0_, bf16[4,128,256]{2,1,0:T(8,128)(2,1)S(1)} %collective-permute-done.18.refs_1_, ...), custom_call_target="tpu_custom_call" | custom-call | flops 4194304 | tf_op jit(solution)/shard_map/mix_features/pallas_call | solution.py:374
  60.0 5.4 %collective-permute-done.16 = bf16[4,128,256]{2,1,0:T(8,128)(2,1)S(1)} collective-permute-done((bf16[4,128,256]{2,1,0:T(8,128)(2,1)S(1)}, bf16[4,128,256]{2,1,0:T(8,128)(2,1)S(1)}, u32[]{:S(2)}, u32[]{:S(2)}) %collective-permute-start.16) | collective-permute-done | bytes 262176 | tf_op jit(solution)/shard_map/ppermute | solution.py:399
  65.6 4.2 %collective-permute-done.21.got_ref = bf16[4,128,256]{2,1,0:T(8,128)(2,1)S(1)} collective-permute-done((bf16[4,128,256]{2,1,0:T(8,128)(2,1)S(1)}, bf16[4,128,256]{2,1,0:T(8,128)(2,1)S(1)}, u32[]{:S(2)}, u32[]{:S(2)}) %collective-permute-start.21) | collective-permute-done | bytes 262176 | tf_op jit(solution)/shard_map/ppermute | solution.py:405
  69.7 1.0 %finish.1 = bf16[4,65536]{1,0:T(4,128)(2,1)} custom-call(bf16[4,128,256]{2,1,0:T(8,128)(2,1)S(1)} %add_convert_fusion.first_ref, f32[4,128,256]{2,1,0:T(8,128)S(1)} %mix_features.6.acc_ref, bf16[4,128,256]{2,1,0:T(8,128)(2,1)S(1)} %collective-permute-done.21.got_ref), custom_call_target="tpu_custom_call" | custom-call | flops 262144 | tf_op jit(solution)/shard_map/finish/pallas_call | solution.py:190
  (58 shorter events, 12.0 us)
Async XLA Ops:
  2.9 11.4 %collective-permute-start.2 = (bf16[2,128,512]{2,1,0:T(8,128)(2,1)}, bf16[2,128,512]{2,1,0:T(8,128)(2,1)S(1)}, u32[]{:S(2)}, u32[]{:S(2)}) collective-permute-start(bf16[2,128,512]{2,1,0:T(8,128)(2,1)} %get-tuple-element.47), channel_id=1, source_target_pairs={{0,24},{4,28},{8,16},{12,20},{16,8},{20,12},{24,0},{28,4},{1,25},{... | collective-permute-start | bytes 786440 | tf_op jit(solution)/shard_map/ppermute | solution.py:448
  6.8 12.4 %collective-permute-start = (bf16[2,128,512]{2,1,0:T(8,128)(2,1)}, bf16[2,128,512]{2,1,0:T(8,128)(2,1)S(1)}, u32[]{:S(2)}, u32[]{:S(2)}) collective-permute-start(bf16[2,128,512]{2,1,0:T(8,128)(2,1)} %get-tuple-element.45), channel_id=1, source_target_pairs={{0,8},{4,12},{8,0},{12,4},{16,24},{20,28},{24,16},{28,20},{1,9},{5... | collective-permute-start | bytes 786440 | tf_op jit(solution)/shard_map/ppermute | solution.py:448
  7.4 11.9 %collective-permute-start.1 = (bf16[2,128,512]{2,1,0:T(8,128)(2,1)}, bf16[2,128,512]{2,1,0:T(8,128)(2,1)S(1)}, u32[]{:S(2)}, u32[]{:S(2)}) collective-permute-start(bf16[2,128,512]{2,1,0:T(8,128)(2,1)} %get-tuple-element.46), channel_id=1, source_target_pairs={{0,16},{4,20},{8,24},{12,28},{16,0},{20,4},{24,8},{28,12},{1,17},{... | collective-permute-start | bytes 786440 | tf_op jit(solution)/shard_map/ppermute | solution.py:448
  7.5 13.7 %copy-start.1 = (bf16[2,128,512]{2,1,0:T(8,128)(2,1)S(1)}, bf16[2,128,512]{2,1,0:T(8,128)(2,1)}, u32[]{:S(2)}) copy-start(bf16[2,128,512]{2,1,0:T(8,128)(2,1)} %get-tuple-element.44.refs_0_) | copy-start | bytes 786436
  7.5 12.3 %collective-permute-start.3 = (bf16[2,128,512]{2,1,0:T(8,128)(2,1)}, bf16[2,128,512]{2,1,0:T(8,128)(2,1)S(1)}, u32[]{:S(2)}, u32[]{:S(2)}) collective-permute-start(bf16[2,128,512]{2,1,0:T(8,128)(2,1)} %get-tuple-element.44.refs_0_), channel_id=1, source_target_pairs={{0,4},{4,0},{8,12},{12,8},{16,20},{20,16},{24,28},{28,24},{1,5},{5... | collective-permute-start | bytes 786440 | tf_op jit(solution)/shard_map/ppermute | solution.py:457
  14.2 5.6 %collective-permute-start.6 = (bf16[2,128,512]{2,1,0:T(8,128)(2,1)S(1)}, bf16[2,128,512]{2,1,0:T(8,128)(2,1)S(1)}, u32[]{:S(2)}, u32[]{:S(2)}) collective-permute-start(bf16[2,128,512]{2,1,0:T(8,128)(2,1)S(1)} %collective-permute-done.2.refs_3_), channel_id=1, source_target_pairs={{0,4},{4,0},{8,12},{12,8},{16,20},{20,16},{24,28},{28,24},{1,5},{5... | collective-permute-start | bytes 786440 | tf_op jit(solution)/shard_map/ppermute | solution.py:457
  19.3 1.5 %collective-permute-start.4 = (bf16[2,128,512]{2,1,0:T(8,128)(2,1)S(1)}, bf16[2,128,512]{2,1,0:T(8,128)(2,1)S(1)}, u32[]{:S(2)}, u32[]{:S(2)}) collective-permute-start(bf16[2,128,512]{2,1,0:T(8,128)(2,1)S(1)} %collective-permute-done.refs_1_), channel_id=1, source_target_pairs={{0,4},{4,0},{8,12},{12,8},{16,20},{20,16},{24,28},{28,24},{1,5},{5... | collective-permute-start | bytes 786440 | tf_op jit(solution)/shard_map/ppermute | solution.py:457
  19.3 1.9 %collective-permute-start.5 = (bf16[2,128,512]{2,1,0:T(8,128)(2,1)S(1)}, bf16[2,128,512]{2,1,0:T(8,128)(2,1)S(1)}, u32[]{:S(2)}, u32[]{:S(2)}) collective-permute-start(bf16[2,128,512]{2,1,0:T(8,128)(2,1)S(1)} %collective-permute-done.1.refs_2_), channel_id=1, source_target_pairs={{0,4},{4,0},{8,12},{12,8},{16,20},{20,16},{24,28},{28,24},{1,5},{5... | collective-permute-start | bytes 786440 | tf_op jit(solution)/shard_map/ppermute | solution.py:457
  26.8 2.0 %collective-permute-start.11 = (bf16[1024,256]{1,0:T(8,128)(2,1)S(1)}, bf16[1024,256]{1,0:T(8,128)(2,1)S(1)}, u32[]{:S(2)}, u32[]{:S(2)}) collective-permute-start(bf16[1024,256]{1,0:T(8,128)(2,1)S(1)} %get-tuple-element.62.refs_0_), channel_id=1, source_target_pairs={{0,4},{4,0},{8,12},{12,8},{16,20},{20,16},{24,28},{28,24},{1,5},{5... | collective-permute-start | bytes 1572872 | tf_op jit(solution)/shard_map/ppermute | solution.py:457
  27.8 5.4 %collective-permute-start.7 = (bf16[1024,256]{1,0:T(8,128)(2,1)S(1)}, bf16[1024,256]{1,0:T(8,128)(2,1)S(1)}, u32[]{:S(2)}, u32[]{:S(2)}) collective-permute-start(bf16[1024,256]{1,0:T(8,128)(2,1)S(1)} %back_columns.1.refs_0_), channel_id=1, source_target_pairs={{0,4},{4,0},{8,12},{12,8},{16,20},{20,16},{24,28},{28,24},{1,5},{5... | collective-permute-start | bytes 1572872 | tf_op jit(solution)/shard_map/ppermute | solution.py:457
  29.6 6.9 %collective-permute-start.12 = (bf16[128,256]{1,0:T(8,128)(2,1)S(1)}, bf16[128,256]{1,0:T(8,128)(2,1)S(1)}, u32[]{:S(2)}, u32[]{:S(2)}) collective-permute-start(bf16[128,256]{1,0:T(8,128)(2,1)S(1)} %get-tuple-element.64), channel_id=1, source_target_pairs={{0,8},{4,12},{8,0},{12,4},{16,24},{20,28},{24,16},{28,20},{1,9},{5... | collective-permute-start | bytes 196616 | tf_op jit(solution)/shard_map/ppermute | solution.py:448
  31.1 6.6 %collective-permute-start.13 = (bf16[128,256]{1,0:T(8,128)(2,1)S(1)}, bf16[128,256]{1,0:T(8,128)(2,1)S(1)}, u32[]{:S(2)}, u32[]{:S(2)}) collective-permute-start(bf16[128,256]{1,0:T(8,128)(2,1)S(1)} %get-tuple-element.65), channel_id=1, source_target_pairs={{0,16},{4,20},{8,24},{12,28},{16,0},{20,4},{24,8},{28,12},{1,17},{... | collective-permute-start | bytes 196616 | tf_op jit(solution)/shard_map/ppermute | solution.py:448
  32.2 5.8 %collective-permute-start.14 = (bf16[128,256]{1,0:T(8,128)(2,1)S(1)}, bf16[128,256]{1,0:T(8,128)(2,1)S(1)}, u32[]{:S(2)}, u32[]{:S(2)}) collective-permute-start(bf16[128,256]{1,0:T(8,128)(2,1)S(1)} %get-tuple-element.66), channel_id=1, source_target_pairs={{0,24},{4,28},{8,16},{12,20},{16,8},{20,12},{24,0},{28,4},{1,25},{... | collective-permute-start | bytes 196616 | tf_op jit(solution)/shard_map/ppermute | solution.py:448
  33.9 5.6 %collective-permute-start.10 = (bf16[128,256]{1,0:T(8,128)(2,1)S(1)}, bf16[128,256]{1,0:T(8,128)(2,1)S(1)}, u32[]{:S(2)}, u32[]{:S(2)}) collective-permute-start(bf16[128,256]{1,0:T(8,128)(2,1)S(1)} %get-tuple-element.61), channel_id=1, source_target_pairs={{0,24},{4,28},{8,16},{12,20},{16,8},{20,12},{24,0},{28,4},{1,25},{... | collective-permute-start | bytes 196616 | tf_op jit(solution)/shard_map/ppermute | solution.py:448
  35.9 4.3 %collective-permute-start.8 = (bf16[128,256]{1,0:T(8,128)(2,1)S(1)}, bf16[128,256]{1,0:T(8,128)(2,1)S(1)}, u32[]{:S(2)}, u32[]{:S(2)}) collective-permute-start(bf16[128,256]{1,0:T(8,128)(2,1)S(1)} %get-tuple-element.59), channel_id=1, source_target_pairs={{0,8},{4,12},{8,0},{12,4},{16,24},{20,28},{24,16},{28,20},{1,9},{5... | collective-permute-start | bytes 196616 | tf_op jit(solution)/shard_map/ppermute | solution.py:448
  36.4 4.3 %collective-permute-start.9 = (bf16[128,256]{1,0:T(8,128)(2,1)S(1)}, bf16[128,256]{1,0:T(8,128)(2,1)S(1)}, u32[]{:S(2)}, u32[]{:S(2)}) collective-permute-start(bf16[128,256]{1,0:T(8,128)(2,1)S(1)} %get-tuple-element.60), channel_id=1, source_target_pairs={{0,16},{4,20},{8,24},{12,28},{16,0},{20,4},{24,8},{28,12},{1,17},{... | collective-permute-start | bytes 196616 | tf_op jit(solution)/shard_map/ppermute | solution.py:448
  38.0 10.3 %copy-start.9 = (bf16[16,16]{1,0:T(8,128)(2,1)S(1)}, bf16[16,16]{1,0:T(8,128)(2,1)}, u32[]{:S(2)}) copy-start(bf16[16,16]{1,0:T(8,128)(2,1)} %param.16) | copy-start | bytes 1540
  40.7 7.6 %collective-permute-start.15 = (bf16[4,128,256]{2,1,0:T(8,128)(2,1)S(1)}, bf16[4,128,256]{2,1,0:T(8,128)(2,1)S(1)}, u32[]{:S(2)}, u32[]{:S(2)}) collective-permute-start(bf16[4,128,256]{2,1,0:T(8,128)(2,1)S(1)} %gate.2.refs_0_), channel_id=1, source_target_pairs={{0,1},{1,0},{2,3},{3,2},{4,5},{5,4},{6,7},{7,6},{8,9},{9,8},{10,11... | collective-permute-start | bytes 786440 | tf_op jit(solution)/shard_map/ppermute | solution.py:397
  43.0 11.8 %collective-permute-start.18 = (bf16[4,128,256]{2,1,0:T(8,128)(2,1)S(1)}, bf16[4,128,256]{2,1,0:T(8,128)(2,1)S(1)}, u32[]{:S(2)}, u32[]{:S(2)}) collective-permute-start(bf16[4,128,256]{2,1,0:T(8,128)(2,1)S(1)} %gate.3.refs_0_), channel_id=1, source_target_pairs={{0,2},{3,1},{4,6},{7,5},{8,10},{11,9},{12,14},{15,13},{16,18},{19,... | collective-permute-start | bytes 786440 | tf_op jit(solution)/shard_map/ppermute | solution.py:395
  47.5 7.3 %collective-permute-start.19 = (bf16[4,128,256]{2,1,0:T(8,128)(2,1)S(1)}, bf16[4,128,256]{2,1,0:T(8,128)(2,1)S(1)}, u32[]{:S(2)}, u32[]{:S(2)}) collective-permute-start(bf16[4,128,256]{2,1,0:T(8,128)(2,1)S(1)} %gate.3.refs_0_), channel_id=1, source_target_pairs={{1,2},{2,1},{5,6},{6,5},{9,10},{10,9},{13,14},{14,13},{17,18},{18,... | collective-permute-start | bytes 786440 | tf_op jit(solution)/shard_map/ppermute | solution.py:396
  49.7 8.8 %collective-permute-start.20 = (bf16[4,128,256]{2,1,0:T(8,128)(2,1)S(1)}, bf16[4,128,256]{2,1,0:T(8,128)(2,1)S(1)}, u32[]{:S(2)}, u32[]{:S(2)}) collective-permute-start(bf16[4,128,256]{2,1,0:T(8,128)(2,1)S(1)} %gate.3.refs_0_), channel_id=1, source_target_pairs={{0,1},{3,2},{4,5},{7,6},{8,9},{11,10},{12,13},{15,14},{16,17},{19,... | collective-permute-start | bytes 786440 | tf_op jit(solution)/shard_map/ppermute | solution.py:402
  52.9 12.6 %collective-permute-start.16 = (bf16[4,128,256]{2,1,0:T(8,128)(2,1)S(1)}, bf16[4,128,256]{2,1,0:T(8,128)(2,1)S(1)}, u32[]{:S(2)}, u32[]{:S(2)}) collective-permute-start(bf16[4,128,256]{2,1,0:T(8,128)(2,1)S(1)} %get-tuple-element.72), channel_id=1, source_target_pairs={{1,3},{2,0},{5,7},{6,4},{9,11},{10,8},{13,15},{14,12},{17,19},{18,... | collective-permute-start | bytes 786440 | tf_op jit(solution)/shard_map/ppermute | solution.py:399
  54.2 11.3 %collective-permute-start.17 = (bf16[4,128,256]{2,1,0:T(8,128)(2,1)S(1)}, bf16[4,128,256]{2,1,0:T(8,128)(2,1)S(1)}, u32[]{:S(2)}, u32[]{:S(2)}) collective-permute-start(bf16[4,128,256]{2,1,0:T(8,128)(2,1)S(1)} %get-tuple-element.73), channel_id=1, source_target_pairs={{1,2},{2,1},{5,6},{6,5},{9,10},{10,9},{13,14},{14,13},{17,18},{18,... | collective-permute-start | bytes 786440 | tf_op jit(solution)/shard_map/ppermute | solution.py:400
  56.1 13.6 %collective-permute-start.21 = (bf16[4,128,256]{2,1,0:T(8,128)(2,1)S(1)}, bf16[4,128,256]{2,1,0:T(8,128)(2,1)S(1)}, u32[]{:S(2)}, u32[]{:S(2)}) collective-permute-start(bf16[4,128,256]{2,1,0:T(8,128)(2,1)S(1)} %mix_features.7), channel_id=1, source_target_pairs={{2,3},{1,0},{6,7},{5,4},{10,11},{9,8},{14,15},{13,12},{18,19},{17,... | collective-permute-start | bytes 786440 | tf_op jit(solution)/shard_map/ppermute | solution.py:405
  (8 other events, 50.1 us)

commit v6 on v5

--- a/solution.py
+++ b/solution.py
@@ -218,8 +218,8 @@
     for kind in range(2):
         for tile in range(0, COLS, 256):
             cut = slice(tile, tile + 256)
-            val = dot(left_ref[...], x_ref[kind, :, cut])
-            val_re, val_im = val[:own], val[own:]
+            val_re = dot(left_ref[:own], x_ref[kind, :, cut])
+            val_im = dot(left_ref[own:], x_ref[kind, :, cut])
             tab_re, tab_im = turn_ref[0, :, cut], turn_ref[1, :, cut]
             mid_re = (val_re * tab_re - val_im * tab_im).astype(BF)
             mid_ref[:, cut] = mid_re

time: 71 us -> 70.7 us (level)
  no operation moved by 1% of the time
where the time goes in v6:
time: 70.7 us; the launch traced here: 70.5 us
  starting transfers between devices  26 us (37%)
  waiting for transfers between devices  21.3 us (30%)
  Pallas kernels  20.1 us (28%)
  local copies, waits for them, and re-layouts  2.64 us (4%)
    ppermute x9, starting transfers between devices, swap(): got.append(lax.ppermute(values[rel], 'ctx', pairs))  11.7 us
    ppermute x9, waiting for transfers between devices, swap(): got.append(lax.ppermute(values[rel], 'ctx', pairs))  9.68 us
    ppermute x1, waiting for transfers between devices, line_mix(): from_far = lax.ppermute(to_far, 'tp', [(1, 3), (2, 0)])  5.45 us
    pallas_call x1, Pallas kernels, run_spectrum(): pl.pallas_call(functools.partial(spectrum_kernel, chans, group, scale), o...  5.37 us
    pallas_call x4, Pallas kernels, run_mix(): pl.pallas_call(functools.partial(mix_kernel, chans, slots, outputs), out_...  5.21 us
    ppermute x1, starting transfers between devices, line_mix(): far = lax.ppermute(gathered, 'tp', [(0, 2), (3, 1)])  4.51 us
    ppermute x1, waiting for transfers between devices, line_mix(): from_edge = lax.ppermute(to_edge, 'tp', [(2, 3), (1, 0)])  4.18 us
    ppermute x1, starting transfers between devices, line_mix(): edge = lax.ppermute(gathered, 'tp', [(0, 1), (3, 2)])  3.1 us
  transfers between devices with their start and end apart: 22, of which 11 were waited for; matrix products, arithmetic and copies ran while one was open for 1% of the time, Pallas kernels for 15%

profile of v6, /device:TPU:0, one launch (start us, length us, event | category | flops | bytes accessed | tf_op | source)
XLA Modules:
  0.0 70.5 jit_solution(657682187562822370)
XLA Ops:
  0.0 2.9 %prepare_blocks.1 = (bf16[2,128,512]{2,1,0:T(8,128)(2,1)}, bf16[2,128,512]{2,1,0:T(8,128)(2,1)}, bf16[2,128,512]{2,1,0:T(8,128)(2,1)}, bf16[2,128,512]{2,1,0:T(8,128)(2,1)}) custom-call(f32[4,65536]{1,0:T(4,128)} %refs_0_.2, bf16[4,65536]{1,0:T(4,128)(2,1)} %refs_1_.2, bf16[4,65536]{1,0:T(4,128)(2,1)} %refs_2_.2), custom_call_target="tpu_custom_call" | custom-call | flops 1048576 | tf_op jit(solution)/shard_map/prepare_blocks/pallas_call | solution.py:152
  2.9 4.0 %collective-permute-start.2 = (bf16[2,128,512]{2,1,0:T(8,128)(2,1)}, bf16[2,128,512]{2,1,0:T(8,128)(2,1)S(1)}, u32[]{:S(2)}, u32[]{:S(2)}) collective-permute-start(bf16[2,128,512]{2,1,0:T(8,128)(2,1)} %get-tuple-element.47), channel_id=1, source_target_pairs={{0,24},{4,28},{8,16},{12,20},{16,8},{20,12},{24,0},{28,4},{1,25},{... | collective-permute-start | bytes 786440 | tf_op jit(solution)/shard_map/ppermute | solution.py:448
  7.5 2.2 %copy-done.2 = bf16[2,1024,1024]{2,1,0:T(8,128)(2,1)S(1)} copy-done((bf16[2,1024,1024]{2,1,0:T(8,128)(2,1)S(1)}, bf16[2,1024,1024]{2,1,0:T(8,128)(2,1)}, u32[]{:S(2)}) %copy-start.2) | copy-done | bytes 4194328
  9.7 2.1 %load_tables.1 = (bf16[1024,1024]{1,0:T(8,128)(2,1)S(1)}, bf16[512,2048]{1,0:T(8,128)(2,1)S(1)}, bf16[1024,512]{1,0:T(8,128)(2,1)S(1)}, f32[2,512,512]{2,1,0:T(8,128)S(1)}) custom-call(bf16[2,1024,1024]{2,1,0:T(8,128)(2,1)S(1)} %copy-done.2, bf16[2,512,2048]{2,1,0:T(8,128)(2,1)} %constant.23.clone.refs_1_, bf16[1024,512]{1,0:T(8,128)(2,1)S(1)} %copy-done.3, ...), custom_call_target="tpu_custom_call" | custom-call | flops 3000000000 | tf_op jit(solution)/shard_map/load_tables/pallas_call | solution.py:97
  11.8 2.4 %collective-permute-done.2.refs_3_ = bf16[2,128,512]{2,1,0:T(8,128)(2,1)S(1)} collective-permute-done((bf16[2,128,512]{2,1,0:T(8,128)(2,1)}, bf16[2,128,512]{2,1,0:T(8,128)(2,1)S(1)}, u32[]{:S(2)}, u32[]{:S(2)}) %collective-permute-start.2) | collective-permute-done | bytes 262176 | tf_op jit(solution)/shard_map/ppermute | solution.py:448
  14.2 5.0 %collective-permute-done.refs_1_ = bf16[2,128,512]{2,1,0:T(8,128)(2,1)S(1)} collective-permute-done((bf16[2,128,512]{2,1,0:T(8,128)(2,1)}, bf16[2,128,512]{2,1,0:T(8,128)(2,1)S(1)}, u32[]{:S(2)}, u32[]{:S(2)}) %collective-permute-start) | collective-permute-done | bytes 262176 | tf_op jit(solution)/shard_map/ppermute | solution.py:448
  19.8 1.0 %collective-permute-done.4.refs_5_ = bf16[2,128,512]{2,1,0:T(8,128)(2,1)S(1)} collective-permute-done((bf16[2,128,512]{2,1,0:T(8,128)(2,1)S(1)}, bf16[2,128,512]{2,1,0:T(8,128)(2,1)S(1)}, u32[]{:S(2)}, u32[]{:S(2)}) %collective-permute-start.4) | collective-permute-done | bytes 262176 | tf_op jit(solution)/shard_map/ppermute | solution.py:457
  21.2 5.4 %spectrum_product.1 = (bf16[512,1536]{1,0:T(8,128)(2,1)S(1)}, bf16[1024,256]{1,0:T(8,128)(2,1)S(1)}) custom-call(bf16[2,128,512]{2,1,0:T(8,128)(2,1)S(1)} %copy-done.1, bf16[2,128,512]{2,1,0:T(8,128)(2,1)S(1)} %collective-permute-done.refs_1_, bf16[2,128,512]{2,1,0:T(8,128)(2,1)S(1)} %collective-permute-done.1.refs_2_, ...), custom_call_target="tpu_custom_call" | custom-call | flops 5368709120 | tf_op jit(solution)/shard_map/spectrum_product/pallas_call | solution.py:287
  29.3 1.6 %collective-permute-start.12 = (bf16[128,256]{1,0:T(8,128)(2,1)S(1)}, bf16[128,256]{1,0:T(8,128)(2,1)S(1)}, u32[]{:S(2)}, u32[]{:S(2)}) collective-permute-start(bf16[128,256]{1,0:T(8,128)(2,1)S(1)} %get-tuple-element.64), channel_id=1, source_target_pairs={{0,8},{4,12},{8,0},{12,4},{16,24},{20,28},{24,16},{28,20},{1,9},{5... | collective-permute-start | bytes 196616 | tf_op jit(solution)/shard_map/ppermute | solution.py:448
  30.9 1.0 %collective-permute-start.13 = (bf16[128,256]{1,0:T(8,128)(2,1)S(1)}, bf16[128,256]{1,0:T(8,128)(2,1)S(1)}, u32[]{:S(2)}, u32[]{:S(2)}) collective-permute-start(bf16[128,256]{1,0:T(8,128)(2,1)S(1)} %get-tuple-element.65), channel_id=1, source_target_pairs={{0,16},{4,20},{8,24},{12,28},{16,0},{20,4},{24,8},{28,12},{1,17},{... | collective-permute-start | bytes 196616 | tf_op jit(solution)/shard_map/ppermute | solution.py:448
  33.6 2.0 %collective-permute-start.10 = (bf16[128,256]{1,0:T(8,128)(2,1)S(1)}, bf16[128,256]{1,0:T(8,128)(2,1)S(1)}, u32[]{:S(2)}, u32[]{:S(2)}) collective-permute-start(bf16[128,256]{1,0:T(8,128)(2,1)S(1)} %get-tuple-element.61), channel_id=1, source_target_pairs={{0,24},{4,28},{8,16},{12,20},{16,8},{20,12},{24,0},{28,4},{1,25},{... | collective-permute-start | bytes 196616 | tf_op jit(solution)/shard_map/ppermute | solution.py:448
  36.2 1.0 %collective-permute-start.9 = (bf16[128,256]{1,0:T(8,128)(2,1)S(1)}, bf16[128,256]{1,0:T(8,128)(2,1)S(1)}, u32[]{:S(2)}, u32[]{:S(2)}) collective-permute-start(bf16[128,256]{1,0:T(8,128)(2,1)S(1)} %get-tuple-element.60), channel_id=1, source_target_pairs={{0,16},{4,20},{8,24},{12,28},{16,0},{20,4},{24,8},{28,12},{1,17},{... | collective-permute-start | bytes 196616 | tf_op jit(solution)/shard_map/ppermute | solution.py:448
  40.4 1.6 %collective-permute-start.15 = (bf16[4,128,256]{2,1,0:T(8,128)(2,1)S(1)}, bf16[4,128,256]{2,1,0:T(8,128)(2,1)S(1)}, u32[]{:S(2)}, u32[]{:S(2)}) collective-permute-start(bf16[4,128,256]{2,1,0:T(8,128)(2,1)S(1)} %gate.2.refs_0_), channel_id=1, source_target_pairs={{0,1},{1,0},{2,3},{3,2},{4,5},{5,4},{6,7},{7,6},{8,9},{9,8},{10,11... | collective-permute-start | bytes 786440 | tf_op jit(solution)/shard_map/ppermute | solution.py:397
  42.8 4.5 %collective-permute-start.18 = (bf16[4,128,256]{2,1,0:T(8,128)(2,1)S(1)}, bf16[4,128,256]{2,1,0:T(8,128)(2,1)S(1)}, u32[]{:S(2)}, u32[]{:S(2)}) collective-permute-start(bf16[4,128,256]{2,1,0:T(8,128)(2,1)S(1)} %gate.3.refs_0_), channel_id=1, source_target_pairs={{0,2},{3,1},{4,6},{7,5},{8,10},{11,9},{12,14},{15,13},{16,18},{19,... | collective-permute-start | bytes 786440 | tf_op jit(solution)/shard_map/ppermute | solution.py:395
  48.1 1.4 %mix_features.5 = (bf16[4,128,256]{2,1,0:T(8,128)(2,1)S(1)}, bf16[4,128,256]{2,1,0:T(8,128)(2,1)S(1)}) custom-call(s32[5]{0:T(128)S(1)} %stack.23.plane_ref, f32[16,16]{1,0:T(8,128)S(1)} %convert_element_type.12.weight_ref, bf16[4,128,256]{2,1,0:T(8,128)(2,1)S(1)} %gate.2.refs_0_, bf16[4,128,256]{2,1,0:T(8,128)(2,1)S(1)} %collective-permute-done.15.refs_1_), custom_call_target="tpu_custom_call" | custom-call | flops 4194304 | tf_op jit(solution)/shard_map/mix_features/pallas_call | solution.py:374
  49.5 3.1 %collective-permute-start.20 = (bf16[4,128,256]{2,1,0:T(8,128)(2,1)S(1)}, bf16[4,128,256]{2,1,0:T(8,128)(2,1)S(1)}, u32[]{:S(2)}, u32[]{:S(2)}) collective-permute-start(bf16[4,128,256]{2,1,0:T(8,128)(2,1)S(1)} %gate.3.refs_0_), channel_id=1, source_target_pairs={{0,1},{3,2},{4,5},{7,6},{8,9},{11,10},{12,13},{15,14},{16,17},{19,... | collective-permute-start | bytes 786440 | tf_op jit(solution)/shard_map/ppermute | solution.py:402
  52.6 1.3 %collective-permute-start.16 = (bf16[4,128,256]{2,1,0:T(8,128)(2,1)S(1)}, bf16[4,128,256]{2,1,0:T(8,128)(2,1)S(1)}, u32[]{:S(2)}, u32[]{:S(2)}) collective-permute-start(bf16[4,128,256]{2,1,0:T(8,128)(2,1)S(1)} %get-tuple-element.72), channel_id=1, source_target_pairs={{1,3},{2,0},{5,7},{6,4},{9,11},{10,8},{13,15},{14,12},{17,19},{18,... | collective-permute-start | bytes 786440 | tf_op jit(solution)/shard_map/ppermute | solution.py:399
  54.6 1.3 %mix_features.7 = bf16[4,128,256]{2,1,0:T(8,128)(2,1)S(1)} custom-call(s32[5]{0:T(128)S(1)} %stack.23.plane_ref, f32[16,16]{1,0:T(8,128)S(1)} %convert_element_type.12.weight_ref, bf16[4,128,256]{2,1,0:T(8,128)(2,1)S(1)} %gate.3.refs_0_, bf16[4,128,256]{2,1,0:T(8,128)(2,1)S(1)} %collective-permute-done.18.refs_1_, ...), custom_call_target="tpu_custom_call" | custom-call | flops 3145728 | tf_op jit(solution)/shard_map/mix_features/pallas_call | solution.py:374
  55.9 1.3 %collective-permute-start.21 = (bf16[4,128,256]{2,1,0:T(8,128)(2,1)S(1)}, bf16[4,128,256]{2,1,0:T(8,128)(2,1)S(1)}, u32[]{:S(2)}, u32[]{:S(2)}) collective-permute-start(bf16[4,128,256]{2,1,0:T(8,128)(2,1)S(1)} %mix_features.7), channel_id=1, source_target_pairs={{2,3},{1,0},{6,7},{5,4},{10,11},{9,8},{14,15},{13,12},{18,19},{17,... | collective-permute-start | bytes 786440 | tf_op jit(solution)/shard_map/ppermute | solution.py:405
  57.2 1.1 %mix_features.4 = f32[4,128,256]{2,1,0:T(8,128)S(1)} custom-call(s32[5]{0:T(128)S(1)} %stack.23.plane_ref, f32[16,16]{1,0:T(8,128)S(1)} %convert_element_type.12.weight_ref, bf16[4,128,256]{2,1,0:T(8,128)(2,1)S(1)} %gate.2.refs_0_, bf16[4,128,256]{2,1,0:T(8,128)(2,1)S(1)} %collective-permute-done.15.refs_1_), custom_call_target="tpu_custom_call" | custom-call | flops 2097152 | tf_op jit(solution)/shard_map/mix_features/pallas_call | solution.py:374
  58.3 1.5 %mix_features.6.acc_ref = f32[4,128,256]{2,1,0:T(8,128)S(1)} custom-call(s32[5]{0:T(128)S(1)} %stack.23.plane_ref, f32[16,16]{1,0:T(8,128)S(1)} %convert_element_type.12.weight_ref, bf16[4,128,256]{2,1,0:T(8,128)(2,1)S(1)} %gate.3.refs_0_, bf16[4,128,256]{2,1,0:T(8,128)(2,1)S(1)} %collective-permute-done.18.refs_1_, ...), custom_call_target="tpu_custom_call" | custom-call | flops 4194304 | tf_op jit(solution)/shard_map/mix_features/pallas_call | solution.py:374
  59.7 5.4 %collective-permute-done.16 = bf16[4,128,256]{2,1,0:T(8,128)(2,1)S(1)} collective-permute-done((bf16[4,128,256]{2,1,0:T(8,128)(2,1)S(1)}, bf16[4,128,256]{2,1,0:T(8,128)(2,1)S(1)}, u32[]{:S(2)}, u32[]{:S(2)}) %collective-permute-start.16) | collective-permute-done | bytes 262176 | tf_op jit(solution)/shard_map/ppermute | solution.py:399
  65.3 4.2 %collective-permute-done.21.got_ref = bf16[4,128,256]{2,1,0:T(8,128)(2,1)S(1)} collective-permute-done((bf16[4,128,256]{2,1,0:T(8,128)(2,1)S(1)}, bf16[4,128,256]{2,1,0:T(8,128)(2,1)S(1)}, u32[]{:S(2)}, u32[]{:S(2)}) %collective-permute-start.21) | collective-permute-done | bytes 262176 | tf_op jit(solution)/shard_map/ppermute | solution.py:405
  69.5 1.0 %finish.1 = bf16[4,65536]{1,0:T(4,128)(2,1)} custom-call(bf16[4,128,256]{2,1,0:T(8,128)(2,1)S(1)} %add_convert_fusion.first_ref, f32[4,128,256]{2,1,0:T(8,128)S(1)} %mix_features.6.acc_ref, bf16[4,128,256]{2,1,0:T(8,128)(2,1)S(1)} %collective-permute-done.21.got_ref), custom_call_target="tpu_custom_call" | custom-call | flops 262144 | tf_op jit(solution)/shard_map/finish/pallas_call | solution.py:190
  (58 shorter events, 12.0 us)
Async XLA Ops:
  2.9 11.4 %collective-permute-start.2 = (bf16[2,128,512]{2,1,0:T(8,128)(2,1)}, bf16[2,128,512]{2,1,0:T(8,128)(2,1)S(1)}, u32[]{:S(2)}, u32[]{:S(2)}) collective-permute-start(bf16[2,128,512]{2,1,0:T(8,128)(2,1)} %get-tuple-element.47), channel_id=1, source_target_pairs={{0,24},{4,28},{8,16},{12,20},{16,8},{20,12},{24,0},{28,4},{1,25},{... | collective-permute-start | bytes 786440 | tf_op jit(solution)/shard_map/ppermute | solution.py:448
  6.8 12.4 %collective-permute-start = (bf16[2,128,512]{2,1,0:T(8,128)(2,1)}, bf16[2,128,512]{2,1,0:T(8,128)(2,1)S(1)}, u32[]{:S(2)}, u32[]{:S(2)}) collective-permute-start(bf16[2,128,512]{2,1,0:T(8,128)(2,1)} %get-tuple-element.45), channel_id=1, source_target_pairs={{0,8},{4,12},{8,0},{12,4},{16,24},{20,28},{24,16},{28,20},{1,9},{5... | collective-permute-start | bytes 786440 | tf_op jit(solution)/shard_map/ppermute | solution.py:448
  7.4 11.9 %collective-permute-start.1 = (bf16[2,128,512]{2,1,0:T(8,128)(2,1)}, bf16[2,128,512]{2,1,0:T(8,128)(2,1)S(1)}, u32[]{:S(2)}, u32[]{:S(2)}) collective-permute-start(bf16[2,128,512]{2,1,0:T(8,128)(2,1)} %get-tuple-element.46), channel_id=1, source_target_pairs={{0,16},{4,20},{8,24},{12,28},{16,0},{20,4},{24,8},{28,12},{1,17},{... | collective-permute-start | bytes 786440 | tf_op jit(solution)/shard_map/ppermute | solution.py:448
  7.5 13.7 %copy-start.1 = (bf16[2,128,512]{2,1,0:T(8,128)(2,1)S(1)}, bf16[2,128,512]{2,1,0:T(8,128)(2,1)}, u32[]{:S(2)}) copy-start(bf16[2,128,512]{2,1,0:T(8,128)(2,1)} %get-tuple-element.44.refs_0_) | copy-start | bytes 786436
  7.5 12.3 %collective-permute-start.3 = (bf16[2,128,512]{2,1,0:T(8,128)(2,1)}, bf16[2,128,512]{2,1,0:T(8,128)(2,1)S(1)}, u32[]{:S(2)}, u32[]{:S(2)}) collective-permute-start(bf16[2,128,512]{2,1,0:T(8,128)(2,1)} %get-tuple-element.44.refs_0_), channel_id=1, source_target_pairs={{0,4},{4,0},{8,12},{12,8},{16,20},{20,16},{24,28},{28,24},{1,5},{5... | collective-permute-start | bytes 786440 | tf_op jit(solution)/shard_map/ppermute | solution.py:457
  14.2 5.6 %collective-permute-start.6 = (bf16[2,128,512]{2,1,0:T(8,128)(2,1)S(1)}, bf16[2,128,512]{2,1,0:T(8,128)(2,1)S(1)}, u32[]{:S(2)}, u32[]{:S(2)}) collective-permute-start(bf16[2,128,512]{2,1,0:T(8,128)(2,1)S(1)} %collective-permute-done.2.refs_3_), channel_id=1, source_target_pairs={{0,4},{4,0},{8,12},{12,8},{16,20},{20,16},{24,28},{28,24},{1,5},{5... | collective-permute-start | bytes 786440 | tf_op jit(solution)/shard_map/ppermute | solution.py:457
  19.3 1.5 %collective-permute-start.4 = (bf16[2,128,512]{2,1,0:T(8,128)(2,1)S(1)}, bf16[2,128,512]{2,1,0:T(8,128)(2,1)S(1)}, u32[]{:S(2)}, u32[]{:S(2)}) collective-permute-start(bf16[2,128,512]{2,1,0:T(8,128)(2,1)S(1)} %collective-permute-done.refs_1_), channel_id=1, source_target_pairs={{0,4},{4,0},{8,12},{12,8},{16,20},{20,16},{24,28},{28,24},{1,5},{5... | collective-permute-start | bytes 786440 | tf_op jit(solution)/shard_map/ppermute | solution.py:457
  19.3 1.9 %collective-permute-start.5 = (bf16[2,128,512]{2,1,0:T(8,128)(2,1)S(1)}, bf16[2,128,512]{2,1,0:T(8,128)(2,1)S(1)}, u32[]{:S(2)}, u32[]{:S(2)}) collective-permute-start(bf16[2,128,512]{2,1,0:T(8,128)(2,1)S(1)} %collective-permute-done.1.refs_2_), channel_id=1, source_target_pairs={{0,4},{4,0},{8,12},{12,8},{16,20},{20,16},{24,28},{28,24},{1,5},{5... | collective-permute-start | bytes 786440 | tf_op jit(solution)/shard_map/ppermute | solution.py:457
  26.6 2.0 %collective-permute-start.11 = (bf16[1024,256]{1,0:T(8,128)(2,1)S(1)}, bf16[1024,256]{1,0:T(8,128)(2,1)S(1)}, u32[]{:S(2)}, u32[]{:S(2)}) collective-permute-start(bf16[1024,256]{1,0:T(8,128)(2,1)S(1)} %get-tuple-element.62.refs_0_), channel_id=1, source_target_pairs={{0,4},{4,0},{8,12},{12,8},{16,20},{20,16},{24,28},{28,24},{1,5},{5... | collective-permute-start | bytes 1572872 | tf_op jit(solution)/shard_map/ppermute | solution.py:457
  27.5 5.4 %collective-permute-start.7 = (bf16[1024,256]{1,0:T(8,128)(2,1)S(1)}, bf16[1024,256]{1,0:T(8,128)(2,1)S(1)}, u32[]{:S(2)}, u32[]{:S(2)}) collective-permute-start(bf16[1024,256]{1,0:T(8,128)(2,1)S(1)} %back_columns.1.refs_0_), channel_id=1, source_target_pairs={{0,4},{4,0},{8,12},{12,8},{16,20},{20,16},{24,28},{28,24},{1,5},{5... | collective-permute-start | bytes 1572872 | tf_op jit(solution)/shard_map/ppermute | solution.py:457
  29.3 6.9 %collective-permute-start.12 = (bf16[128,256]{1,0:T(8,128)(2,1)S(1)}, bf16[128,256]{1,0:T(8,128)(2,1)S(1)}, u32[]{:S(2)}, u32[]{:S(2)}) collective-permute-start(bf16[128,256]{1,0:T(8,128)(2,1)S(1)} %get-tuple-element.64), channel_id=1, source_target_pairs={{0,8},{4,12},{8,0},{12,4},{16,24},{20,28},{24,16},{28,20},{1,9},{5... | collective-permute-start | bytes 196616 | tf_op jit(solution)/shard_map/ppermute | solution.py:448
  30.9 6.6 %collective-permute-start.13 = (bf16[128,256]{1,0:T(8,128)(2,1)S(1)}, bf16[128,256]{1,0:T(8,128)(2,1)S(1)}, u32[]{:S(2)}, u32[]{:S(2)}) collective-permute-start(bf16[128,256]{1,0:T(8,128)(2,1)S(1)} %get-tuple-element.65), channel_id=1, source_target_pairs={{0,16},{4,20},{8,24},{12,28},{16,0},{20,4},{24,8},{28,12},{1,17},{... | collective-permute-start | bytes 196616 | tf_op jit(solution)/shard_map/ppermute | solution.py:448
  31.9 5.8 %collective-permute-start.14 = (bf16[128,256]{1,0:T(8,128)(2,1)S(1)}, bf16[128,256]{1,0:T(8,128)(2,1)S(1)}, u32[]{:S(2)}, u32[]{:S(2)}) collective-permute-start(bf16[128,256]{1,0:T(8,128)(2,1)S(1)} %get-tuple-element.66), channel_id=1, source_target_pairs={{0,24},{4,28},{8,16},{12,20},{16,8},{20,12},{24,0},{28,4},{1,25},{... | collective-permute-start | bytes 196616 | tf_op jit(solution)/shard_map/ppermute | solution.py:448
  33.6 5.6 %collective-permute-start.10 = (bf16[128,256]{1,0:T(8,128)(2,1)S(1)}, bf16[128,256]{1,0:T(8,128)(2,1)S(1)}, u32[]{:S(2)}, u32[]{:S(2)}) collective-permute-start(bf16[128,256]{1,0:T(8,128)(2,1)S(1)} %get-tuple-element.61), channel_id=1, source_target_pairs={{0,24},{4,28},{8,16},{12,20},{16,8},{20,12},{24,0},{28,4},{1,25},{... | collective-permute-start | bytes 196616 | tf_op jit(solution)/shard_map/ppermute | solution.py:448
  35.6 4.3 %collective-permute-start.8 = (bf16[128,256]{1,0:T(8,128)(2,1)S(1)}, bf16[128,256]{1,0:T(8,128)(2,1)S(1)}, u32[]{:S(2)}, u32[]{:S(2)}) collective-permute-start(bf16[128,256]{1,0:T(8,128)(2,1)S(1)} %get-tuple-element.59), channel_id=1, source_target_pairs={{0,8},{4,12},{8,0},{12,4},{16,24},{20,28},{24,16},{28,20},{1,9},{5... | collective-permute-start | bytes 196616 | tf_op jit(solution)/shard_map/ppermute | solution.py:448
  36.2 4.3 %collective-permute-start.9 = (bf16[128,256]{1,0:T(8,128)(2,1)S(1)}, bf16[128,256]{1,0:T(8,128)(2,1)S(1)}, u32[]{:S(2)}, u32[]{:S(2)}) collective-permute-start(bf16[128,256]{1,0:T(8,128)(2,1)S(1)} %get-tuple-element.60), channel_id=1, source_target_pairs={{0,16},{4,20},{8,24},{12,28},{16,0},{20,4},{24,8},{28,12},{1,17},{... | collective-permute-start | bytes 196616 | tf_op jit(solution)/shard_map/ppermute | solution.py:448
  37.7 10.3 %copy-start.9 = (bf16[16,16]{1,0:T(8,128)(2,1)S(1)}, bf16[16,16]{1,0:T(8,128)(2,1)}, u32[]{:S(2)}) copy-start(bf16[16,16]{1,0:T(8,128)(2,1)} %param.16) | copy-start | bytes 1540
  40.4 7.6 %collective-permute-start.15 = (bf16[4,128,256]{2,1,0:T(8,128)(2,1)S(1)}, bf16[4,128,256]{2,1,0:T(8,128)(2,1)S(1)}, u32[]{:S(2)}, u32[]{:S(2)}) collective-permute-start(bf16[4,128,256]{2,1,0:T(8,128)(2,1)S(1)} %gate.2.refs_0_), channel_id=1, source_target_pairs={{0,1},{1,0},{2,3},{3,2},{4,5},{5,4},{6,7},{7,6},{8,9},{9,8},{10,11... | collective-permute-start | bytes 786440 | tf_op jit(solution)/shard_map/ppermute | solution.py:397
  42.8 11.8 %collective-permute-start.18 = (bf16[4,128,256]{2,1,0:T(8,128)(2,1)S(1)}, bf16[4,128,256]{2,1,0:T(8,128)(2,1)S(1)}, u32[]{:S(2)}, u32[]{:S(2)}) collective-permute-start(bf16[4,128,256]{2,1,0:T(8,128)(2,1)S(1)} %gate.3.refs_0_), channel_id=1, source_target_pairs={{0,2},{3,1},{4,6},{7,5},{8,10},{11,9},{12,14},{15,13},{16,18},{19,... | collective-permute-start | bytes 786440 | tf_op jit(solution)/shard_map/ppermute | solution.py:395
  47.3 7.3 %collective-permute-start.19 = (bf16[4,128,256]{2,1,0:T(8,128)(2,1)S(1)}, bf16[4,128,256]{2,1,0:T(8,128)(2,1)S(1)}, u32[]{:S(2)}, u32[]{:S(2)}) collective-permute-start(bf16[4,128,256]{2,1,0:T(8,128)(2,1)S(1)} %gate.3.refs_0_), channel_id=1, source_target_pairs={{1,2},{2,1},{5,6},{6,5},{9,10},{10,9},{13,14},{14,13},{17,18},{18,... | collective-permute-start | bytes 786440 | tf_op jit(solution)/shard_map/ppermute | solution.py:396
  49.5 8.8 %collective-permute-start.20 = (bf16[4,128,256]{2,1,0:T(8,128)(2,1)S(1)}, bf16[4,128,256]{2,1,0:T(8,128)(2,1)S(1)}, u32[]{:S(2)}, u32[]{:S(2)}) collective-permute-start(bf16[4,128,256]{2,1,0:T(8,128)(2,1)S(1)} %gate.3.refs_0_), channel_id=1, source_target_pairs={{0,1},{3,2},{4,5},{7,6},{8,9},{11,10},{12,13},{15,14},{16,17},{19,... | collective-permute-start | bytes 786440 | tf_op jit(solution)/shard_map/ppermute | solution.py:402
  52.6 12.6 %collective-permute-start.16 = (bf16[4,128,256]{2,1,0:T(8,128)(2,1)S(1)}, bf16[4,128,256]{2,1,0:T(8,128)(2,1)S(1)}, u32[]{:S(2)}, u32[]{:S(2)}) collective-permute-start(bf16[4,128,256]{2,1,0:T(8,128)(2,1)S(1)} %get-tuple-element.72), channel_id=1, source_target_pairs={{1,3},{2,0},{5,7},{6,4},{9,11},{10,8},{13,15},{14,12},{17,19},{18,... | collective-permute-start | bytes 786440 | tf_op jit(solution)/shard_map/ppermute | solution.py:399
  53.9 11.3 %collective-permute-start.17 = (bf16[4,128,256]{2,1,0:T(8,128)(2,1)S(1)}, bf16[4,128,256]{2,1,0:T(8,128)(2,1)S(1)}, u32[]{:S(2)}, u32[]{:S(2)}) collective-permute-start(bf16[4,128,256]{2,1,0:T(8,128)(2,1)S(1)} %get-tuple-element.73), channel_id=1, source_target_pairs={{1,2},{2,1},{5,6},{6,5},{9,10},{10,9},{13,14},{14,13},{17,18},{18,... | collective-permute-start | bytes 786440 | tf_op jit(solution)/shard_map/ppermute | solution.py:400
  55.9 13.6 %collective-permute-start.21 = (bf16[4,128,256]{2,1,0:T(8,128)(2,1)S(1)}, bf16[4,128,256]{2,1,0:T(8,128)(2,1)S(1)}, u32[]{:S(2)}, u32[]{:S(2)}) collective-permute-start(bf16[4,128,256]{2,1,0:T(8,128)(2,1)S(1)} %mix_features.7), channel_id=1, source_target_pairs={{2,3},{1,0},{6,7},{5,4},{10,11},{9,8},{14,15},{13,12},{18,19},{17,... | collective-permute-start | bytes 786440 | tf_op jit(solution)/shard_map/ppermute | solution.py:405
  (8 other events, 50.1 us)

commit v7 on v6

--- a/solution.py
+++ b/solution.py
@@ -202,24 +202,62 @@
     )(first, acc, got)
 
 
-def spectrum_kernel(chans, group, scale, *refs):
-    count = chans * group
-    blocks = refs[:count]
-    left_ref, wave_ref, turn_ref, prod_ref, out_ref = refs[count : count + 5]
-    x_ref, mid_ref, spec_ref = refs[count + 5 :]
+def early_kernel(chans, group, early, late, *refs):
+    count = len(early) * group
+    blocks, (left_ref, sum_ref, rest_ref) = refs[:count], refs[count : count + 3]
+    x_ref, part_ref = refs[count + 3 :]
     rows = blocks[0].shape[1]
-    own = mid_ref.shape[0]
     home = lax.axis_index("ctx") // group
-    for step in range(group):
-        for rel in range(chans):
+    for rels, target in ((early, part_ref), (late, rest_ref)):
+        for number in range(len(rels) * group):
+            step, rel = number // len(rels), rels[number % len(rels)]
             first = pl.multiple_of((step * chans + (home ^ rel)) * rows, rows)
-            for kind in range(2):
-                x_ref[kind, pl.ds(first, rows)] = blocks[step * chans + rel][kind]
+            target[:, number * rows : (number + 1) * rows] = left_ref[:, pl.ds(first, rows)]
+    for number, block in enumerate(blocks):
+        for kind in range(2):
+            x_ref[kind, number * rows : (number + 1) * rows] = block[kind]
+    half = sum_ref.shape[1] // 2
     for kind in range(2):
         for tile in range(0, COLS, 256):
             cut = slice(tile, tile + 256)
-            val_re = dot(left_ref[:own], x_ref[kind, :, cut])
-            val_im = dot(left_ref[own:], x_ref[kind, :, cut])
+            sum_ref[kind, :half, cut] = dot(part_ref[:half], x_ref[kind, :, cut])
+            sum_ref[kind, half:, cut] = dot(part_ref[half:], x_ref[kind, :, cut])
+
+
+def run_early(blocks, chans, group, early, late, left):
+    size, big = left.shape
+    rows = big // (chans * group)
+    width, rest = len(early) * group * rows, len(late) * group * rows
+    return pl.pallas_call(
+        functools.partial(early_kernel, chans, group, early, late),
+        out_shape=(
+            jax.ShapeDtypeStruct((2, size, COLS), F32),
+            jax.ShapeDtypeStruct((size, rest), BF),
+        ),
+        in_specs=[VMEM] * (len(blocks) + 1),
+        out_specs=(VMEM, VMEM),
+        scratch_shapes=[pltpu.VMEM((2, width, COLS), BF), pltpu.VMEM((size, width), BF)],
+        compiler_params=params(12),
+        cost_estimate=cost(4 * size * COLS * width),
+        name="early_stage",
+    )(*blocks, left)
+
+
+def spectrum_kernel(scale, *refs):
+    count = len(refs) - 9
+    blocks = refs[:count]
+    sum_ref, left_ref, wave_ref, turn_ref, prod_ref, out_ref = refs[count : count + 6]
+    x_ref, mid_ref, spec_ref = refs[count + 6 :]
+    rows = blocks[0].shape[1]
+    own = mid_ref.shape[0]
+    for number, block in enumerate(blocks):
+        for kind in range(2):
+            x_ref[kind, number * rows : (number + 1) * rows] = block[kind]
+    for kind in range(2):
+        for tile in range(0, COLS, 256):
+            cut = slice(tile, tile + 256)
+            val_re = dot(left_ref[:own], x_ref[kind, :, cut]) + sum_ref[kind, :own, cut]
+            val_im = dot(left_ref[own:], x_ref[kind, :, cut]) + sum_ref[kind, own:, cut]
             tab_re, tab_im = turn_ref[0, :, cut], turn_ref[1, :, cut]
             mid_re = (val_re * tab_re - val_im * tab_im).astype(BF)
             mid_ref[:, cut] = mid_re
@@ -281,26 +319,26 @@
         out_ref[chan] = (query_ref[chan, :, cut].astype(F32) * total).astype(BF)
 
 
-def run_spectrum(blocks, chans, group, tables, scale):
-    left, _, wave, turn = tables
-    own, big = left.shape[0] // 2, left.shape[1]
-    return pl.pallas_call(
-        functools.partial(spectrum_kernel, chans, group, scale),
+def run_spectrum(blocks, sums, left, tables, scale):
+    _, _, wave, turn = tables
+    own, width = left.shape[0] // 2, left.shape[1]
+    return pl.pallas_call(
+        functools.partial(spectrum_kernel, scale),
         out_shape=(
             jax.ShapeDtypeStruct((own, 3 * COLS), BF),
             jax.ShapeDtypeStruct((2 * own, CUTS[1] - CUTS[0]), BF),
         ),
-        in_specs=[VMEM] * (len(blocks) + 3),
+        in_specs=[VMEM] * (len(blocks) + 4),
         out_specs=(VMEM, VMEM),
         scratch_shapes=[
-            pltpu.VMEM((2, big, COLS), BF),
+            pltpu.VMEM((2, width, COLS), BF),
             pltpu.VMEM((own, 3 * COLS), BF),
             pltpu.VMEM((2, own, COLS), F32),
         ],
         compiler_params=params(20),
-        cost_estimate=cost(8 * own * COLS * (big + 3 * COLS)),
+        cost_estimate=cost(8 * own * COLS * (width + 3 * COLS)),
         name="spectrum_product",
-    )(*blocks, left, wave, turn)
+    )(*blocks, sums, left, wave, turn)
 
 
 def run_back(prod, tables, low, high):
@@ -461,10 +499,18 @@
     value = value_branch.reshape(shape)
     blocks = run_prepare(long_filter, key_branch, value_branch, group)
     blocks = swap(list(blocks))
+    early = (0, chans - 1)
+    late = tuple(range(1, chans - 1))
     blocks[-1], tables = lax.optimization_barrier((blocks[-1], tables))
-    blocks += [shift(part, -step) for step in range(1, group) for part in blocks]
+
+    def share(rels, values):
+        values = [values[rel] for rel in rels]
+        return values + [shift(part, -step) for step in range(1, group) for part in values]
+
+    sums, rest = run_early(share(early, blocks), chans, group, early, late, tables[0])
+    blocks = share(late, blocks)
     spans = list(zip(CUTS[:-1], CUTS[1:]))
-    prod, back = run_spectrum(blocks, chans, group, tables, 1.0 / length)
+    prod, back = run_spectrum(blocks, sums, rest, tables, 1.0 / length)
     backs = [back] + [run_back(prod, tables, *span) for span in spans[1:]]
     places = []
     for back in backs:

time: 70.7 us -> 70 us (0.990)
  waiting for transfers between devices: 21.3 us -> 20 us
    ppermute x6, waiting for transfers between devices: 2.02 us -> 0.63 us  [shift(): return lax.ppermute(value, 'ctx', pairs)]
    pallas_call x1 -> x2, Pallas kernels: 5.37 us -> 5.96 us  [the longest x1 4.31 us: run_spectrum(): pl.pallas_call(functools.partial(spectrum_kernel, scale), out_shape=(jax....]
  transfers between devices with their start and end apart: 22 -> 22, of which waited for: 11 -> 9; matrix products, arithmetic and copies ran while one was open for 1% -> 1% of each run, Pallas kernels for 15% -> 18%
where the time goes in v7:
time: 70 us; the launch traced here: 69.7 us
  starting transfers between devices  26.1 us (37%)
  Pallas kernels  20.7 us (30%)
  waiting for transfers between devices  20 us (29%)
  local copies, waits for them, and re-layouts  2.61 us (4%)
    ppermute x9, starting transfers between devices, swap(): got.append(lax.ppermute(values[rel], 'ctx', pairs))  11.8 us
    ppermute x9, waiting for transfers between devices, swap(): got.append(lax.ppermute(values[rel], 'ctx', pairs))  9.68 us
    ppermute x1, waiting for transfers between devices, line_mix(): from_far = lax.ppermute(to_far, 'tp', [(1, 3), (2, 0)])  5.44 us
    pallas_call x4, Pallas kernels, run_mix(): pl.pallas_call(functools.partial(mix_kernel, chans, slots, outputs), out_...  5.21 us
    ppermute x1, starting transfers between devices, line_mix(): far = lax.ppermute(gathered, 'tp', [(0, 2), (3, 1)])  4.51 us
    pallas_call x1, Pallas kernels, run_spectrum(): pl.pallas_call(functools.partial(spectrum_kernel, scale), out_shape=(jax....  4.31 us
    ppermute x1, waiting for transfers between devices, line_mix(): from_edge = lax.ppermute(to_edge, 'tp', [(2, 3), (1, 0)])  4.18 us
    ppermute x1, starting transfers between devices, line_mix(): edge = lax.ppermute(gathered, 'tp', [(0, 1), (3, 2)])  3.11 us
  transfers between devices with their start and end apart: 22, of which 9 were waited for; matrix products, arithmetic and copies ran while one was open for 1% of the time, Pallas kernels for 18%

profile of v7, /device:TPU:0, one launch (start us, length us, event | category | flops | bytes accessed | tf_op | source)
XLA Modules:
  0.0 69.7 jit_solution(16582266439021485257)
XLA Ops:
  0.0 2.9 %prepare_blocks.1 = (bf16[2,128,512]{2,1,0:T(8,128)(2,1)}, bf16[2,128,512]{2,1,0:T(8,128)(2,1)}, bf16[2,128,512]{2,1,0:T(8,128)(2,1)}, bf16[2,128,512]{2,1,0:T(8,128)(2,1)}) custom-call(f32[4,65536]{1,0:T(4,128)} %refs_0_.2, bf16[4,65536]{1,0:T(4,128)(2,1)} %refs_1_.2, bf16[4,65536]{1,0:T(4,128)(2,1)} %refs_2_.2), custom_call_target="tpu_custom_call" | custom-call | flops 1048576 | tf_op jit(solution)/shard_map/prepare_blocks/pallas_call | solution.py:152
  2.9 4.0 %collective-permute-start.4 = (bf16[2,128,512]{2,1,0:T(8,128)(2,1)}, bf16[2,128,512]{2,1,0:T(8,128)(2,1)S(1)}, u32[]{:S(2)}, u32[]{:S(2)}) collective-permute-start(bf16[2,128,512]{2,1,0:T(8,128)(2,1)} %get-tuple-element.49), channel_id=1, source_target_pairs={{0,24},{4,28},{8,16},{12,20},{16,8},{20,12},{24,0},{28,4},{1,25},{... | collective-permute-start | bytes 786440 | tf_op jit(solution)/shard_map/ppermute | solution.py:486
  7.6 2.2 %copy-done.2 = bf16[2,1024,1024]{2,1,0:T(8,128)(2,1)S(1)} copy-done((bf16[2,1024,1024]{2,1,0:T(8,128)(2,1)S(1)}, bf16[2,1024,1024]{2,1,0:T(8,128)(2,1)}, u32[]{:S(2)}) %copy-start.2) | copy-done | bytes 4194328
  9.8 2.1 %load_tables.1 = (bf16[1024,1024]{1,0:T(8,128)(2,1)S(1)}, bf16[512,2048]{1,0:T(8,128)(2,1)S(1)}, bf16[1024,512]{1,0:T(8,128)(2,1)S(1)}, f32[2,512,512]{2,1,0:T(8,128)S(1)}) custom-call(bf16[2,1024,1024]{2,1,0:T(8,128)(2,1)S(1)} %copy-done.2, bf16[2,512,2048]{2,1,0:T(8,128)(2,1)} %constant.23.clone.refs_1_, bf16[1024,512]{1,0:T(8,128)(2,1)S(1)} %copy-done.3, ...), custom_call_target="tpu_custom_call" | custom-call | flops 3000000000 | tf_op jit(solution)/shard_map/load_tables/pallas_call | solution.py:97
  11.8 2.4 %collective-permute-done.4.refs_1_ = bf16[2,128,512]{2,1,0:T(8,128)(2,1)S(1)} collective-permute-done((bf16[2,128,512]{2,1,0:T(8,128)(2,1)}, bf16[2,128,512]{2,1,0:T(8,128)(2,1)S(1)}, u32[]{:S(2)}, u32[]{:S(2)}) %collective-permute-start.4) | collective-permute-done | bytes 262176 | tf_op jit(solution)/shard_map/ppermute | solution.py:486
  14.2 5.0 %collective-permute-done.refs_0_ = bf16[2,128,512]{2,1,0:T(8,128)(2,1)S(1)} collective-permute-done((bf16[2,128,512]{2,1,0:T(8,128)(2,1)}, bf16[2,128,512]{2,1,0:T(8,128)(2,1)S(1)}, u32[]{:S(2)}, u32[]{:S(2)}) %collective-permute-start) | collective-permute-done | bytes 262176 | tf_op jit(solution)/shard_map/ppermute | solution.py:486
  19.8 1.6 %early_stage.1 = (f32[2,1024,512]{2,1,0:T(8,128)S(1)}, bf16[1024,512]{1,0:T(8,128)(2,1)S(1)}) custom-call(bf16[2,128,512]{2,1,0:T(8,128)(2,1)S(1)} %copy-done.1, bf16[2,128,512]{2,1,0:T(8,128)(2,1)S(1)} %collective-permute-done.4.refs_1_, bf16[2,128,512]{2,1,0:T(8,128)(2,1)S(1)} %collective-permute-done.5.refs_2_, ...), custom_call_target="tpu_custom_call" | custom-call | flops 1073741824 | tf_op jit(solution)/shard_map/early_stage/pallas_call | solution.py:231
  21.5 4.3 %spectrum_product.1 = (bf16[512,1536]{1,0:T(8,128)(2,1)S(1)}, bf16[1024,256]{1,0:T(8,128)(2,1)S(1)}) custom-call(bf16[2,128,512]{2,1,0:T(8,128)(2,1)S(1)} %collective-permute-done.refs_0_, bf16[2,128,512]{2,1,0:T(8,128)(2,1)S(1)} %collective-permute-done.1.refs_1_, bf16[2,128,512]{2,1,0:T(8,128)(2,1)S(1)} %collective-permute-done.2.refs_2_, ...), custom_call_target="tpu_custom_call" | custom-call | flops 4294967296 | tf_op jit(solution)/shard_map/spectrum_product/pallas_call | solution.py:325
  28.5 1.6 %collective-permute-start.12 = (bf16[128,256]{1,0:T(8,128)(2,1)S(1)}, bf16[128,256]{1,0:T(8,128)(2,1)S(1)}, u32[]{:S(2)}, u32[]{:S(2)}) collective-permute-start(bf16[128,256]{1,0:T(8,128)(2,1)S(1)} %get-tuple-element.68), channel_id=1, source_target_pairs={{0,8},{4,12},{8,0},{12,4},{16,24},{20,28},{24,16},{28,20},{1,9},{5... | collective-permute-start | bytes 196616 | tf_op jit(solution)/shard_map/ppermute | solution.py:486
  30.1 1.0 %collective-permute-start.13 = (bf16[128,256]{1,0:T(8,128)(2,1)S(1)}, bf16[128,256]{1,0:T(8,128)(2,1)S(1)}, u32[]{:S(2)}, u32[]{:S(2)}) collective-permute-start(bf16[128,256]{1,0:T(8,128)(2,1)S(1)} %get-tuple-element.69), channel_id=1, source_target_pairs={{0,16},{4,20},{8,24},{12,28},{16,0},{20,4},{24,8},{28,12},{1,17},{... | collective-permute-start | bytes 196616 | tf_op jit(solution)/shard_map/ppermute | solution.py:486
  32.8 2.1 %collective-permute-start.10 = (bf16[128,256]{1,0:T(8,128)(2,1)S(1)}, bf16[128,256]{1,0:T(8,128)(2,1)S(1)}, u32[]{:S(2)}, u32[]{:S(2)}) collective-permute-start(bf16[128,256]{1,0:T(8,128)(2,1)S(1)} %get-tuple-element.65), channel_id=1, source_target_pairs={{0,24},{4,28},{8,16},{12,20},{16,8},{20,12},{24,0},{28,4},{1,25},{... | collective-permute-start | bytes 196616 | tf_op jit(solution)/shard_map/ppermute | solution.py:486
  35.4 1.0 %collective-permute-start.9 = (bf16[128,256]{1,0:T(8,128)(2,1)S(1)}, bf16[128,256]{1,0:T(8,128)(2,1)S(1)}, u32[]{:S(2)}, u32[]{:S(2)}) collective-permute-start(bf16[128,256]{1,0:T(8,128)(2,1)S(1)} %get-tuple-element.64), channel_id=1, source_target_pairs={{0,16},{4,20},{8,24},{12,28},{16,0},{20,4},{24,8},{28,12},{1,17},{... | collective-permute-start | bytes 196616 | tf_op jit(solution)/shard_map/ppermute | solution.py:486
  39.7 1.6 %collective-permute-start.15 = (bf16[4,128,256]{2,1,0:T(8,128)(2,1)S(1)}, bf16[4,128,256]{2,1,0:T(8,128)(2,1)S(1)}, u32[]{:S(2)}, u32[]{:S(2)}) collective-permute-start(bf16[4,128,256]{2,1,0:T(8,128)(2,1)S(1)} %gate.2.refs_0_), channel_id=1, source_target_pairs={{0,1},{1,0},{2,3},{3,2},{4,5},{5,4},{6,7},{7,6},{8,9},{9,8},{10,11... | collective-permute-start | bytes 786440 | tf_op jit(solution)/shard_map/ppermute | solution.py:435
  42.0 4.5 %collective-permute-start.18 = (bf16[4,128,256]{2,1,0:T(8,128)(2,1)S(1)}, bf16[4,128,256]{2,1,0:T(8,128)(2,1)S(1)}, u32[]{:S(2)}, u32[]{:S(2)}) collective-permute-start(bf16[4,128,256]{2,1,0:T(8,128)(2,1)S(1)} %gate.3.refs_0_), channel_id=1, source_target_pairs={{0,2},{3,1},{4,6},{7,5},{8,10},{11,9},{12,14},{15,13},{16,18},{19,... | collective-permute-start | bytes 786440 | tf_op jit(solution)/shard_map/ppermute | solution.py:433
  47.3 1.4 %mix_features.5 = (bf16[4,128,256]{2,1,0:T(8,128)(2,1)S(1)}, bf16[4,128,256]{2,1,0:T(8,128)(2,1)S(1)}) custom-call(s32[5]{0:T(128)S(1)} %stack.23.plane_ref, f32[16,16]{1,0:T(8,128)S(1)} %convert_element_type.12.weight_ref, bf16[4,128,256]{2,1,0:T(8,128)(2,1)S(1)} %gate.2.refs_0_, bf16[4,128,256]{2,1,0:T(8,128)(2,1)S(1)} %collective-permute-done.15.refs_1_), custom_call_target="tpu_custom_call" | custom-call | flops 4194304 | tf_op jit(solution)/shard_map/mix_features/pallas_call | solution.py:412
  48.7 3.1 %collective-permute-start.20 = (bf16[4,128,256]{2,1,0:T(8,128)(2,1)S(1)}, bf16[4,128,256]{2,1,0:T(8,128)(2,1)S(1)}, u32[]{:S(2)}, u32[]{:S(2)}) collective-permute-start(bf16[4,128,256]{2,1,0:T(8,128)(2,1)S(1)} %gate.3.refs_0_), channel_id=1, source_target_pairs={{0,1},{3,2},{4,5},{7,6},{8,9},{11,10},{12,13},{15,14},{16,17},{19,... | collective-permute-start | bytes 786440 | tf_op jit(solution)/shard_map/ppermute | solution.py:440
  51.8 1.3 %collective-permute-start.16 = (bf16[4,128,256]{2,1,0:T(8,128)(2,1)S(1)}, bf16[4,128,256]{2,1,0:T(8,128)(2,1)S(1)}, u32[]{:S(2)}, u32[]{:S(2)}) collective-permute-start(bf16[4,128,256]{2,1,0:T(8,128)(2,1)S(1)} %get-tuple-element.76), channel_id=1, source_target_pairs={{1,3},{2,0},{5,7},{6,4},{9,11},{10,8},{13,15},{14,12},{17,19},{18,... | collective-permute-start | bytes 786440 | tf_op jit(solution)/shard_map/ppermute | solution.py:437
  53.9 1.3 %mix_features.7 = bf16[4,128,256]{2,1,0:T(8,128)(2,1)S(1)} custom-call(s32[5]{0:T(128)S(1)} %stack.23.plane_ref, f32[16,16]{1,0:T(8,128)S(1)} %convert_element_type.12.weight_ref, bf16[4,128,256]{2,1,0:T(8,128)(2,1)S(1)} %gate.3.refs_0_, bf16[4,128,256]{2,1,0:T(8,128)(2,1)S(1)} %collective-permute-done.18.refs_1_, ...), custom_call_target="tpu_custom_call" | custom-call | flops 3145728 | tf_op jit(solution)/shard_map/mix_features/pallas_call | solution.py:412
  55.1 1.3 %collective-permute-start.21 = (bf16[4,128,256]{2,1,0:T(8,128)(2,1)S(1)}, bf16[4,128,256]{2,1,0:T(8,128)(2,1)S(1)}, u32[]{:S(2)}, u32[]{:S(2)}) collective-permute-start(bf16[4,128,256]{2,1,0:T(8,128)(2,1)S(1)} %mix_features.7), channel_id=1, source_target_pairs={{2,3},{1,0},{6,7},{5,4},{10,11},{9,8},{14,15},{13,12},{18,19},{17,... | collective-permute-start | bytes 786440 | tf_op jit(solution)/shard_map/ppermute | solution.py:443
  56.4 1.1 %mix_features.4 = f32[4,128,256]{2,1,0:T(8,128)S(1)} custom-call(s32[5]{0:T(128)S(1)} %stack.23.plane_ref, f32[16,16]{1,0:T(8,128)S(1)} %convert_element_type.12.weight_ref, bf16[4,128,256]{2,1,0:T(8,128)(2,1)S(1)} %gate.2.refs_0_, bf16[4,128,256]{2,1,0:T(8,128)(2,1)S(1)} %collective-permute-done.15.refs_1_), custom_call_target="tpu_custom_call" | custom-call | flops 2097152 | tf_op jit(solution)/shard_map/mix_features/pallas_call | solution.py:412
  57.5 1.5 %mix_features.6.acc_ref = f32[4,128,256]{2,1,0:T(8,128)S(1)} custom-call(s32[5]{0:T(128)S(1)} %stack.23.plane_ref, f32[16,16]{1,0:T(8,128)S(1)} %convert_element_type.12.weight_ref, bf16[4,128,256]{2,1,0:T(8,128)(2,1)S(1)} %gate.3.refs_0_, bf16[4,128,256]{2,1,0:T(8,128)(2,1)S(1)} %collective-permute-done.18.refs_1_, ...), custom_call_target="tpu_custom_call" | custom-call | flops 4194304 | tf_op jit(solution)/shard_map/mix_features/pallas_call | solution.py:412
  59.0 5.4 %collective-permute-done.16 = bf16[4,128,256]{2,1,0:T(8,128)(2,1)S(1)} collective-permute-done((bf16[4,128,256]{2,1,0:T(8,128)(2,1)S(1)}, bf16[4,128,256]{2,1,0:T(8,128)(2,1)S(1)}, u32[]{:S(2)}, u32[]{:S(2)}) %collective-permute-start.16) | collective-permute-done | bytes 262176 | tf_op jit(solution)/shard_map/ppermute | solution.py:437
  64.5 4.2 %collective-permute-done.21.got_ref = bf16[4,128,256]{2,1,0:T(8,128)(2,1)S(1)} collective-permute-done((bf16[4,128,256]{2,1,0:T(8,128)(2,1)S(1)}, bf16[4,128,256]{2,1,0:T(8,128)(2,1)S(1)}, u32[]{:S(2)}, u32[]{:S(2)}) %collective-permute-start.21) | collective-permute-done | bytes 262176 | tf_op jit(solution)/shard_map/ppermute | solution.py:443
  68.7 1.0 %finish.1 = bf16[4,65536]{1,0:T(4,128)(2,1)} custom-call(bf16[4,128,256]{2,1,0:T(8,128)(2,1)S(1)} %add_convert_fusion.first_ref, f32[4,128,256]{2,1,0:T(8,128)S(1)} %mix_features.6.acc_ref, bf16[4,128,256]{2,1,0:T(8,128)(2,1)S(1)} %collective-permute-done.21.got_ref), custom_call_target="tpu_custom_call" | custom-call | flops 262144 | tf_op jit(solution)/shard_map/finish/pallas_call | solution.py:190
  (59 shorter events, 11.7 us)
Async XLA Ops:
  2.9 11.4 %collective-permute-start.4 = (bf16[2,128,512]{2,1,0:T(8,128)(2,1)}, bf16[2,128,512]{2,1,0:T(8,128)(2,1)S(1)}, u32[]{:S(2)}, u32[]{:S(2)}) collective-permute-start(bf16[2,128,512]{2,1,0:T(8,128)(2,1)} %get-tuple-element.49), channel_id=1, source_target_pairs={{0,24},{4,28},{8,16},{12,20},{16,8},{20,12},{24,0},{28,4},{1,25},{... | collective-permute-start | bytes 786440 | tf_op jit(solution)/shard_map/ppermute | solution.py:486
  6.8 12.9 %collective-permute-start.5 = (bf16[2,128,512]{2,1,0:T(8,128)(2,1)}, bf16[2,128,512]{2,1,0:T(8,128)(2,1)S(1)}, u32[]{:S(2)}, u32[]{:S(2)}) collective-permute-start(bf16[2,128,512]{2,1,0:T(8,128)(2,1)} %get-tuple-element.48.refs_0_), channel_id=1, source_target_pairs={{0,4},{4,0},{8,12},{12,8},{16,20},{20,16},{24,28},{28,24},{1,5},{5... | collective-permute-start | bytes 786440 | tf_op jit(solution)/shard_map/ppermute | solution.py:495
  6.8 12.4 %collective-permute-start = (bf16[2,128,512]{2,1,0:T(8,128)(2,1)}, bf16[2,128,512]{2,1,0:T(8,128)(2,1)S(1)}, u32[]{:S(2)}, u32[]{:S(2)}) collective-permute-start(bf16[2,128,512]{2,1,0:T(8,128)(2,1)} %get-tuple-element.46), channel_id=1, source_target_pairs={{0,8},{4,12},{8,0},{12,4},{16,24},{20,28},{24,16},{28,20},{1,9},{5... | collective-permute-start | bytes 786440 | tf_op jit(solution)/shard_map/ppermute | solution.py:486
  7.4 12.4 %copy-start.1 = (bf16[2,128,512]{2,1,0:T(8,128)(2,1)S(1)}, bf16[2,128,512]{2,1,0:T(8,128)(2,1)}, u32[]{:S(2)}) copy-start(bf16[2,128,512]{2,1,0:T(8,128)(2,1)} %get-tuple-element.48.refs_0_) | copy-start | bytes 786436
  7.4 11.9 %collective-permute-start.1 = (bf16[2,128,512]{2,1,0:T(8,128)(2,1)}, bf16[2,128,512]{2,1,0:T(8,128)(2,1)S(1)}, u32[]{:S(2)}, u32[]{:S(2)}) collective-permute-start(bf16[2,128,512]{2,1,0:T(8,128)(2,1)} %get-tuple-element.47), channel_id=1, source_target_pairs={{0,16},{4,20},{8,24},{12,28},{16,0},{20,4},{24,8},{28,12},{1,17},{... | collective-permute-start | bytes 786440 | tf_op jit(solution)/shard_map/ppermute | solution.py:486
  14.2 5.6 %collective-permute-start.6 = (bf16[2,128,512]{2,1,0:T(8,128)(2,1)S(1)}, bf16[2,128,512]{2,1,0:T(8,128)(2,1)S(1)}, u32[]{:S(2)}, u32[]{:S(2)}) collective-permute-start(bf16[2,128,512]{2,1,0:T(8,128)(2,1)S(1)} %collective-permute-done.4.refs_1_), channel_id=1, source_target_pairs={{0,4},{4,0},{8,12},{12,8},{16,20},{20,16},{24,28},{28,24},{1,5},{5... | collective-permute-start | bytes 786440 | tf_op jit(solution)/shard_map/ppermute | solution.py:495
  19.3 2.2 %collective-permute-start.2 = (bf16[2,128,512]{2,1,0:T(8,128)(2,1)S(1)}, bf16[2,128,512]{2,1,0:T(8,128)(2,1)S(1)}, u32[]{:S(2)}, u32[]{:S(2)}) collective-permute-start(bf16[2,128,512]{2,1,0:T(8,128)(2,1)S(1)} %collective-permute-done.refs_0_), channel_id=1, source_target_pairs={{0,4},{4,0},{8,12},{12,8},{16,20},{20,16},{24,28},{28,24},{1,5},{5... | collective-permute-start | bytes 786440 | tf_op jit(solution)/shard_map/ppermute | solution.py:495
  19.3 2.2 %collective-permute-start.3 = (bf16[2,128,512]{2,1,0:T(8,128)(2,1)S(1)}, bf16[2,128,512]{2,1,0:T(8,128)(2,1)S(1)}, u32[]{:S(2)}, u32[]{:S(2)}) collective-permute-start(bf16[2,128,512]{2,1,0:T(8,128)(2,1)S(1)} %collective-permute-done.1.refs_1_), channel_id=1, source_target_pairs={{0,4},{4,0},{8,12},{12,8},{16,20},{20,16},{24,28},{28,24},{1,5},{5... | collective-permute-start | bytes 786440 | tf_op jit(solution)/shard_map/ppermute | solution.py:495
  25.8 2.0 %collective-permute-start.11 = (bf16[1024,256]{1,0:T(8,128)(2,1)S(1)}, bf16[1024,256]{1,0:T(8,128)(2,1)S(1)}, u32[]{:S(2)}, u32[]{:S(2)}) collective-permute-start(bf16[1024,256]{1,0:T(8,128)(2,1)S(1)} %get-tuple-element.66.refs_0_), channel_id=1, source_target_pairs={{0,4},{4,0},{8,12},{12,8},{16,20},{20,16},{24,28},{28,24},{1,5},{5... | collective-permute-start | bytes 1572872 | tf_op jit(solution)/shard_map/ppermute | solution.py:495
  26.6 5.5 %collective-permute-start.7 = (bf16[1024,256]{1,0:T(8,128)(2,1)S(1)}, bf16[1024,256]{1,0:T(8,128)(2,1)S(1)}, u32[]{:S(2)}, u32[]{:S(2)}) collective-permute-start(bf16[1024,256]{1,0:T(8,128)(2,1)S(1)} %back_columns.1.refs_0_), channel_id=1, source_target_pairs={{0,4},{4,0},{8,12},{12,8},{16,20},{20,16},{24,28},{28,24},{1,5},{5... | collective-permute-start | bytes 1572872 | tf_op jit(solution)/shard_map/ppermute | solution.py:495
  28.5 6.9 %collective-permute-start.12 = (bf16[128,256]{1,0:T(8,128)(2,1)S(1)}, bf16[128,256]{1,0:T(8,128)(2,1)S(1)}, u32[]{:S(2)}, u32[]{:S(2)}) collective-permute-start(bf16[128,256]{1,0:T(8,128)(2,1)S(1)} %get-tuple-element.68), channel_id=1, source_target_pairs={{0,8},{4,12},{8,0},{12,4},{16,24},{20,28},{24,16},{28,20},{1,9},{5... | collective-permute-start | bytes 196616 | tf_op jit(solution)/shard_map/ppermute | solution.py:486
  30.1 6.6 %collective-permute-start.13 = (bf16[128,256]{1,0:T(8,128)(2,1)S(1)}, bf16[128,256]{1,0:T(8,128)(2,1)S(1)}, u32[]{:S(2)}, u32[]{:S(2)}) collective-permute-start(bf16[128,256]{1,0:T(8,128)(2,1)S(1)} %get-tuple-element.69), channel_id=1, source_target_pairs={{0,16},{4,20},{8,24},{12,28},{16,0},{20,4},{24,8},{28,12},{1,17},{... | collective-permute-start | bytes 196616 | tf_op jit(solution)/shard_map/ppermute | solution.py:486
  31.1 5.8 %collective-permute-start.14 = (bf16[128,256]{1,0:T(8,128)(2,1)S(1)}, bf16[128,256]{1,0:T(8,128)(2,1)S(1)}, u32[]{:S(2)}, u32[]{:S(2)}) collective-permute-start(bf16[128,256]{1,0:T(8,128)(2,1)S(1)} %get-tuple-element.70), channel_id=1, source_target_pairs={{0,24},{4,28},{8,16},{12,20},{16,8},{20,12},{24,0},{28,4},{1,25},{... | collective-permute-start | bytes 196616 | tf_op jit(solution)/shard_map/ppermute | solution.py:486
  32.8 5.6 %collective-permute-start.10 = (bf16[128,256]{1,0:T(8,128)(2,1)S(1)}, bf16[128,256]{1,0:T(8,128)(2,1)S(1)}, u32[]{:S(2)}, u32[]{:S(2)}) collective-permute-start(bf16[128,256]{1,0:T(8,128)(2,1)S(1)} %get-tuple-element.65), channel_id=1, source_target_pairs={{0,24},{4,28},{8,16},{12,20},{16,8},{20,12},{24,0},{28,4},{1,25},{... | collective-permute-start | bytes 196616 | tf_op jit(solution)/shard_map/ppermute | solution.py:486
  34.9 4.3 %collective-permute-start.8 = (bf16[128,256]{1,0:T(8,128)(2,1)S(1)}, bf16[128,256]{1,0:T(8,128)(2,1)S(1)}, u32[]{:S(2)}, u32[]{:S(2)}) collective-permute-start(bf16[128,256]{1,0:T(8,128)(2,1)S(1)} %get-tuple-element.63), channel_id=1, source_target_pairs={{0,8},{4,12},{8,0},{12,4},{16,24},{20,28},{24,16},{28,20},{1,9},{5... | collective-permute-start | bytes 196616 | tf_op jit(solution)/shard_map/ppermute | solution.py:486
  35.4 4.3 %collective-permute-start.9 = (bf16[128,256]{1,0:T(8,128)(2,1)S(1)}, bf16[128,256]{1,0:T(8,128)(2,1)S(1)}, u32[]{:S(2)}, u32[]{:S(2)}) collective-permute-start(bf16[128,256]{1,0:T(8,128)(2,1)S(1)} %get-tuple-element.64), channel_id=1, source_target_pairs={{0,16},{4,20},{8,24},{12,28},{16,0},{20,4},{24,8},{28,12},{1,17},{... | collective-permute-start | bytes 196616 | tf_op jit(solution)/shard_map/ppermute | solution.py:486
  36.9 10.3 %copy-start.9 = (bf16[16,16]{1,0:T(8,128)(2,1)S(1)}, bf16[16,16]{1,0:T(8,128)(2,1)}, u32[]{:S(2)}) copy-start(bf16[16,16]{1,0:T(8,128)(2,1)} %param.16) | copy-start | bytes 1540
  39.7 7.6 %collective-permute-start.15 = (bf16[4,128,256]{2,1,0:T(8,128)(2,1)S(1)}, bf16[4,128,256]{2,1,0:T(8,128)(2,1)S(1)}, u32[]{:S(2)}, u32[]{:S(2)}) collective-permute-start(bf16[4,128,256]{2,1,0:T(8,128)(2,1)S(1)} %gate.2.refs_0_), channel_id=1, source_target_pairs={{0,1},{1,0},{2,3},{3,2},{4,5},{5,4},{6,7},{7,6},{8,9},{9,8},{10,11... | collective-permute-start | bytes 786440 | tf_op jit(solution)/shard_map/ppermute | solution.py:435
  42.0 11.8 %collective-permute-start.18 = (bf16[4,128,256]{2,1,0:T(8,128)(2,1)S(1)}, bf16[4,128,256]{2,1,0:T(8,128)(2,1)S(1)}, u32[]{:S(2)}, u32[]{:S(2)}) collective-permute-start(bf16[4,128,256]{2,1,0:T(8,128)(2,1)S(1)} %gate.3.refs_0_), channel_id=1, source_target_pairs={{0,2},{3,1},{4,6},{7,5},{8,10},{11,9},{12,14},{15,13},{16,18},{19,... | collective-permute-start | bytes 786440 | tf_op jit(solution)/shard_map/ppermute | solution.py:433
  46.5 7.3 %collective-permute-start.19 = (bf16[4,128,256]{2,1,0:T(8,128)(2,1)S(1)}, bf16[4,128,256]{2,1,0:T(8,128)(2,1)S(1)}, u32[]{:S(2)}, u32[]{:S(2)}) collective-permute-start(bf16[4,128,256]{2,1,0:T(8,128)(2,1)S(1)} %gate.3.refs_0_), channel_id=1, source_target_pairs={{1,2},{2,1},{5,6},{6,5},{9,10},{10,9},{13,14},{14,13},{17,18},{18,... | collective-permute-start | bytes 786440 | tf_op jit(solution)/shard_map/ppermute | solution.py:434
  48.7 8.8 %collective-permute-start.20 = (bf16[4,128,256]{2,1,0:T(8,128)(2,1)S(1)}, bf16[4,128,256]{2,1,0:T(8,128)(2,1)S(1)}, u32[]{:S(2)}, u32[]{:S(2)}) collective-permute-start(bf16[4,128,256]{2,1,0:T(8,128)(2,1)S(1)} %gate.3.refs_0_), channel_id=1, source_target_pairs={{0,1},{3,2},{4,5},{7,6},{8,9},{11,10},{12,13},{15,14},{16,17},{19,... | collective-permute-start | bytes 786440 | tf_op jit(solution)/shard_map/ppermute | solution.py:440
  51.8 12.6 %collective-permute-start.16 = (bf16[4,128,256]{2,1,0:T(8,128)(2,1)S(1)}, bf16[4,128,256]{2,1,0:T(8,128)(2,1)S(1)}, u32[]{:S(2)}, u32[]{:S(2)}) collective-permute-start(bf16[4,128,256]{2,1,0:T(8,128)(2,1)S(1)} %get-tuple-element.76), channel_id=1, source_target_pairs={{1,3},{2,0},{5,7},{6,4},{9,11},{10,8},{13,15},{14,12},{17,19},{18,... | collective-permute-start | bytes 786440 | tf_op jit(solution)/shard_map/ppermute | solution.py:437
  53.1 11.3 %collective-permute-start.17 = (bf16[4,128,256]{2,1,0:T(8,128)(2,1)S(1)}, bf16[4,128,256]{2,1,0:T(8,128)(2,1)S(1)}, u32[]{:S(2)}, u32[]{:S(2)}) collective-permute-start(bf16[4,128,256]{2,1,0:T(8,128)(2,1)S(1)} %get-tuple-element.77), channel_id=1, source_target_pairs={{1,2},{2,1},{5,6},{6,5},{9,10},{10,9},{13,14},{14,13},{17,18},{18,... | collective-permute-start | bytes 786440 | tf_op jit(solution)/shard_map/ppermute | solution.py:438
  55.1 13.6 %collective-permute-start.21 = (bf16[4,128,256]{2,1,0:T(8,128)(2,1)S(1)}, bf16[4,128,256]{2,1,0:T(8,128)(2,1)S(1)}, u32[]{:S(2)}, u32[]{:S(2)}) collective-permute-start(bf16[4,128,256]{2,1,0:T(8,128)(2,1)S(1)} %mix_features.7), channel_id=1, source_target_pairs={{2,3},{1,0},{6,7},{5,4},{10,11},{9,8},{14,15},{13,12},{18,19},{17,... | collective-permute-start | bytes 786440 | tf_op jit(solution)/shard_map/ppermute | solution.py:443
  (8 other events, 50.2 us)

commit v8 on v7

--- a/solution.py
+++ b/solution.py
@@ -307,15 +307,32 @@
         outs[rel][...] = sum_ref[pl.ds(pl.multiple_of((home ^ rel) * rows, rows), rows)]
 
 
+def skip_kernel(query_ref, key_ref, value_ref, gain_ref, out_ref):
+    for chan in range(query_ref.shape[0]):
+        signal = key_ref[chan].astype(F32) * value_ref[chan].astype(F32)
+        out_ref[chan] = gain_ref[chan] * signal
+
+
+def run_skip(query, key, value, gain):
+    return pl.pallas_call(
+        skip_kernel,
+        out_shape=jax.ShapeDtypeStruct(query.shape, F32),
+        in_specs=[VMEM] * 3 + [SMEM],
+        out_specs=VMEM,
+        compiler_params=params(12),
+        cost_estimate=cost(2 * query.size),
+        name="skip_term",
+    )(query, key, value, gain)
+
+
 def gate_kernel(chans, group, low, high, *refs):
     parts = refs[:chans]
-    query_ref, key_ref, value_ref, gain_ref, out_ref = refs[chans:]
+    query_ref, skip_ref, out_ref = refs[chans:]
     cut = slice(low, high)
     home = lax.axis_index("ctx") // group
     for rel in range(chans):
         chan = home ^ rel
-        signal = key_ref[chan, :, cut].astype(F32) * value_ref[chan, :, cut].astype(F32)
-        total = parts[rel][...].astype(F32) + gain_ref[chan] * signal
+        total = parts[rel][...].astype(F32) + skip_ref[chan, :, cut]
         out_ref[chan] = (query_ref[chan, :, cut].astype(F32) * total).astype(BF)
 
 
@@ -371,17 +388,17 @@
     )(*parts, table)
 
 
-def run_gate(parts, query, key, value, gain, group, low, high):
+def run_gate(parts, query, skip, group, low, high):
     chans, rows, _ = query.shape
     return pl.pallas_call(
         functools.partial(gate_kernel, chans, group, low, high),
         out_shape=jax.ShapeDtypeStruct((chans, rows, high - low), BF),
-        in_specs=[VMEM] * (chans + 3) + [SMEM],
+        in_specs=[VMEM] * (chans + 2),
         out_specs=VMEM,
         compiler_params=params(12),
         cost_estimate=cost(4 * chans * rows * (high - low)),
         name="gate",
-    )(*parts, query, key, value, gain)
+    )(*parts, query, skip)
 
 
 def mix_kernel(chans, slots, outputs, plane_ref, weight_ref, *refs):
@@ -501,7 +518,8 @@
     blocks = swap(list(blocks))
     early = (0, chans - 1)
     late = tuple(range(1, chans - 1))
-    blocks[-1], tables = lax.optimization_barrier((blocks[-1], tables))
+    skip = run_skip(query, key, value, skip_gain)
+    blocks[-1], tables, query, skip = lax.optimization_barrier((blocks[-1], tables, query, skip))
 
     def share(rels, values):
         values = [values[rel] for rel in rels]
@@ -523,7 +541,7 @@
             parts, _ = lax.optimization_barrier((parts, places[number + 1]))
         if number > 0:
             parts, gated[-1] = lax.optimization_barrier((parts, gated[-1]))
-        gated.append(run_gate(parts, query, key, value, skip_gain, group, *span))
+        gated.append(run_gate(parts, query, skip, group, *span))
         if number + 1 < len(spans):
             parts = swap(list(places[number + 1]))
     return (line_mix if lax.axis_size("tp") == 4 else gather_mix)(gated, out_weight)

time: 70 us -> 69.7 us (level)
  starting transfers between devices: 26.1 us -> 27.3 us
    ppermute x1, starting transfers between devices: 3.11 us -> 4.33 us  [line_mix(): edge = lax.ppermute(gathered, 'tp', [(0, 1), (3, 2)])]
    pallas_call x2, Pallas kernels: 1.45 us -> 0.23 us  [run_gate(): pl.pallas_call(functools.partial(gate_kernel, chans, group, low, high), o...]
    unnamed x21, local copies, waits for them, and re-layouts: 2.32 us -> 1.62 us
  transfers between devices with their start and end apart: 22 -> 22, of which waited for: 9 -> 9; matrix products, arithmetic and copies ran while one was open for 1% -> 1% of each run, Pallas kernels for 18% -> 17%
where the time goes in v8:
time: 69.7 us; the launch traced here: 69.4 us
  starting transfers between devices  27.3 us (39%)
  Pallas kernels  20.2 us (29%)
  waiting for transfers between devices  19.6 us (28%)
  local copies, waits for them, and re-layouts  1.91 us (3%)
    ppermute x9, starting transfers between devices, swap(): got.append(lax.ppermute(values[rel], 'ctx', pairs))  11.8 us
    ppermute x9, waiting for transfers between devices, swap(): got.append(lax.ppermute(values[rel], 'ctx', pairs))  10.2 us
    pallas_call x4, Pallas kernels, run_mix(): pl.pallas_call(functools.partial(mix_kernel, chans, slots, outputs), out_...  5.21 us
    ppermute x1, waiting for transfers between devices, line_mix(): from_far = lax.ppermute(to_far, 'tp', [(1, 3), (2, 0)])  4.88 us
    ppermute x1, starting transfers between devices, line_mix(): far = lax.ppermute(gathered, 'tp', [(0, 2), (3, 1)])  4.51 us
    ppermute x1, starting transfers between devices, line_mix(): edge = lax.ppermute(gathered, 'tp', [(0, 1), (3, 2)])  4.33 us
    pallas_call x1, Pallas kernels, run_spectrum(): pl.pallas_call(functools.partial(spectrum_kernel, scale), out_shape=(jax....  4.32 us
    ppermute x1, waiting for transfers between devices, line_mix(): from_edge = lax.ppermute(to_edge, 'tp', [(2, 3), (1, 0)])  3.86 us
  transfers between devices with their start and end apart: 22, of which 9 were waited for; matrix products, arithmetic and copies ran while one was open for 1% of the time, Pallas kernels for 17%

profile of v8, /device:TPU:0, one launch (start us, length us, event | category | flops | bytes accessed | tf_op | source)
XLA Modules:
  0.0 69.4 jit_solution(4865601988066124480)
XLA Ops:
  0.0 2.9 %prepare_blocks.1 = (bf16[2,128,512]{2,1,0:T(8,128)(2,1)}, bf16[2,128,512]{2,1,0:T(8,128)(2,1)}, bf16[2,128,512]{2,1,0:T(8,128)(2,1)}, bf16[2,128,512]{2,1,0:T(8,128)(2,1)}) custom-call(f32[4,65536]{1,0:T(4,128)} %refs_0_.2, bf16[4,65536]{1,0:T(4,128)(2,1)} %refs_1_.2, bf16[4,65536]{1,0:T(4,128)(2,1)} %refs_2_.2), custom_call_target="tpu_custom_call" | custom-call | flops 1048576 | tf_op jit(solution)/shard_map/prepare_blocks/pallas_call | solution.py:152
  2.9 4.0 %collective-permute-start.4 = (bf16[2,128,512]{2,1,0:T(8,128)(2,1)}, bf16[2,128,512]{2,1,0:T(8,128)(2,1)S(1)}, u32[]{:S(2)}, u32[]{:S(2)}) collective-permute-start(bf16[2,128,512]{2,1,0:T(8,128)(2,1)} %get-tuple-element.51), channel_id=1, source_target_pairs={{0,24},{4,28},{8,16},{12,20},{16,8},{20,12},{24,0},{28,4},{1,25},{... | collective-permute-start | bytes 786440 | tf_op jit(solution)/shard_map/ppermute | solution.py:503
  8.8 1.3 %copy-done.2 = bf16[2,1024,1024]{2,1,0:T(8,128)(2,1)S(1)} copy-done((bf16[2,1024,1024]{2,1,0:T(8,128)(2,1)S(1)}, bf16[2,1024,1024]{2,1,0:T(8,128)(2,1)}, u32[]{:S(2)}) %copy-start.2) | copy-done | bytes 4194328
  10.1 2.1 %load_tables.1 = (bf16[1024,1024]{1,0:T(8,128)(2,1)S(1)}, bf16[512,2048]{1,0:T(8,128)(2,1)S(1)}, bf16[1024,512]{1,0:T(8,128)(2,1)S(1)}, f32[2,512,512]{2,1,0:T(8,128)S(1)}) custom-call(bf16[2,1024,1024]{2,1,0:T(8,128)(2,1)S(1)} %copy-done.2, bf16[2,512,2048]{2,1,0:T(8,128)(2,1)} %constant.23.clone.refs_1_, bf16[1024,512]{1,0:T(8,128)(2,1)S(1)} %copy-done.3, ...), custom_call_target="tpu_custom_call" | custom-call | flops 3000000000 | tf_op jit(solution)/shard_map/load_tables/pallas_call | solution.py:97
  12.2 2.0 %collective-permute-done.4.refs_1_ = bf16[2,128,512]{2,1,0:T(8,128)(2,1)S(1)} collective-permute-done((bf16[2,128,512]{2,1,0:T(8,128)(2,1)}, bf16[2,128,512]{2,1,0:T(8,128)(2,1)S(1)}, u32[]{:S(2)}, u32[]{:S(2)}) %collective-permute-start.4) | collective-permute-done | bytes 262176 | tf_op jit(solution)/shard_map/ppermute | solution.py:503
  14.3 5.0 %collective-permute-done.refs_0_ = bf16[2,128,512]{2,1,0:T(8,128)(2,1)S(1)} collective-permute-done((bf16[2,128,512]{2,1,0:T(8,128)(2,1)}, bf16[2,128,512]{2,1,0:T(8,128)(2,1)S(1)}, u32[]{:S(2)}, u32[]{:S(2)}) %collective-permute-start) | collective-permute-done | bytes 262176 | tf_op jit(solution)/shard_map/ppermute | solution.py:503
  19.8 1.6 %early_stage.1 = (f32[2,1024,512]{2,1,0:T(8,128)S(1)}, bf16[1024,512]{1,0:T(8,128)(2,1)S(1)}) custom-call(bf16[2,128,512]{2,1,0:T(8,128)(2,1)S(1)} %copy-done.1, bf16[2,128,512]{2,1,0:T(8,128)(2,1)S(1)} %collective-permute-done.4.refs_1_, bf16[2,128,512]{2,1,0:T(8,128)(2,1)S(1)} %collective-permute-done.5.refs_2_, ...), custom_call_target="tpu_custom_call" | custom-call | flops 1073741824 | tf_op jit(solution)/shard_map/early_stage/pallas_call | solution.py:231
  21.5 4.3 %spectrum_product.1 = (bf16[512,1536]{1,0:T(8,128)(2,1)S(1)}, bf16[1024,256]{1,0:T(8,128)(2,1)S(1)}) custom-call(bf16[2,128,512]{2,1,0:T(8,128)(2,1)S(1)} %collective-permute-done.refs_0_, bf16[2,128,512]{2,1,0:T(8,128)(2,1)S(1)} %collective-permute-done.1.refs_1_, bf16[2,128,512]{2,1,0:T(8,128)(2,1)S(1)} %collective-permute-done.2.refs_2_, ...), custom_call_target="tpu_custom_call" | custom-call | flops 4294967296 | tf_op jit(solution)/shard_map/spectrum_product/pallas_call | solution.py:342
  28.5 1.6 %collective-permute-start.12 = (bf16[128,256]{1,0:T(8,128)(2,1)S(1)}, bf16[128,256]{1,0:T(8,128)(2,1)S(1)}, u32[]{:S(2)}, u32[]{:S(2)}) collective-permute-start(bf16[128,256]{1,0:T(8,128)(2,1)S(1)} %get-tuple-element.70), channel_id=1, source_target_pairs={{0,8},{4,12},{8,0},{12,4},{16,24},{20,28},{24,16},{28,20},{1,9},{5... | collective-permute-start | bytes 196616 | tf_op jit(solution)/shard_map/ppermute | solution.py:503
  30.1 1.0 %collective-permute-start.13 = (bf16[128,256]{1,0:T(8,128)(2,1)S(1)}, bf16[128,256]{1,0:T(8,128)(2,1)S(1)}, u32[]{:S(2)}, u32[]{:S(2)}) collective-permute-start(bf16[128,256]{1,0:T(8,128)(2,1)S(1)} %get-tuple-element.71), channel_id=1, source_target_pairs={{0,16},{4,20},{8,24},{12,28},{16,0},{20,4},{24,8},{28,12},{1,17},{... | collective-permute-start | bytes 196616 | tf_op jit(solution)/shard_map/ppermute | solution.py:503
  32.8 2.1 %collective-permute-start.10 = (bf16[128,256]{1,0:T(8,128)(2,1)S(1)}, bf16[128,256]{1,0:T(8,128)(2,1)S(1)}, u32[]{:S(2)}, u32[]{:S(2)}) collective-permute-start(bf16[128,256]{1,0:T(8,128)(2,1)S(1)} %get-tuple-element.67), channel_id=1, source_target_pairs={{0,24},{4,28},{8,16},{12,20},{16,8},{20,12},{24,0},{28,4},{1,25},{... | collective-permute-start | bytes 196616 | tf_op jit(solution)/shard_map/ppermute | solution.py:503
  37.1 1.4 %collective-permute-done.10.refs_3_ = bf16[128,256]{1,0:T(8,128)(2,1)S(1)} collective-permute-done((bf16[128,256]{1,0:T(8,128)(2,1)S(1)}, bf16[128,256]{1,0:T(8,128)(2,1)S(1)}, u32[]{:S(2)}, u32[]{:S(2)}) %collective-permute-start.10) | collective-permute-done | bytes 65568 | tf_op jit(solution)/shard_map/ppermute | solution.py:503
  39.7 1.6 %collective-permute-start.15 = (bf16[4,128,256]{2,1,0:T(8,128)(2,1)S(1)}, bf16[4,128,256]{2,1,0:T(8,128)(2,1)S(1)}, u32[]{:S(2)}, u32[]{:S(2)}) collective-permute-start(bf16[4,128,256]{2,1,0:T(8,128)(2,1)S(1)} %gate.2.refs_0_), channel_id=1, source_target_pairs={{0,1},{1,0},{2,3},{3,2},{4,5},{5,4},{6,7},{7,6},{8,9},{9,8},{10,11... | collective-permute-start | bytes 786440 | tf_op jit(solution)/shard_map/ppermute | solution.py:452
  41.4 4.5 %collective-permute-start.18 = (bf16[4,128,256]{2,1,0:T(8,128)(2,1)S(1)}, bf16[4,128,256]{2,1,0:T(8,128)(2,1)S(1)}, u32[]{:S(2)}, u32[]{:S(2)}) collective-permute-start(bf16[4,128,256]{2,1,0:T(8,128)(2,1)S(1)} %gate.3.refs_0_), channel_id=1, source_target_pairs={{0,2},{3,1},{4,6},{7,5},{8,10},{11,9},{12,14},{15,13},{16,18},{19,... | collective-permute-start | bytes 786440 | tf_op jit(solution)/shard_map/ppermute | solution.py:450
  46.7 1.4 %mix_features.5 = (bf16[4,128,256]{2,1,0:T(8,128)(2,1)S(1)}, bf16[4,128,256]{2,1,0:T(8,128)(2,1)S(1)}) custom-call(s32[5]{0:T(128)S(1)} %stack.23.plane_ref, f32[16,16]{1,0:T(8,128)S(1)} %convert_element_type.12.weight_ref, bf16[4,128,256]{2,1,0:T(8,128)(2,1)S(1)} %gate.2.refs_0_, bf16[4,128,256]{2,1,0:T(8,128)(2,1)S(1)} %collective-permute-done.15.refs_1_), custom_call_target="tpu_custom_call" | custom-call | flops 4194304 | tf_op jit(solution)/shard_map/mix_features/pallas_call | solution.py:429
  48.1 4.3 %collective-permute-start.20 = (bf16[4,128,256]{2,1,0:T(8,128)(2,1)S(1)}, bf16[4,128,256]{2,1,0:T(8,128)(2,1)S(1)}, u32[]{:S(2)}, u32[]{:S(2)}) collective-permute-start(bf16[4,128,256]{2,1,0:T(8,128)(2,1)S(1)} %gate.3.refs_0_), channel_id=1, source_target_pairs={{0,1},{3,2},{4,5},{7,6},{8,9},{11,10},{12,13},{15,14},{16,17},{19,... | collective-permute-start | bytes 786440 | tf_op jit(solution)/shard_map/ppermute | solution.py:457
  52.5 1.3 %collective-permute-start.16 = (bf16[4,128,256]{2,1,0:T(8,128)(2,1)S(1)}, bf16[4,128,256]{2,1,0:T(8,128)(2,1)S(1)}, u32[]{:S(2)}, u32[]{:S(2)}) collective-permute-start(bf16[4,128,256]{2,1,0:T(8,128)(2,1)S(1)} %get-tuple-element.80), channel_id=1, source_target_pairs={{1,3},{2,0},{5,7},{6,4},{9,11},{10,8},{13,15},{14,12},{17,19},{18,... | collective-permute-start | bytes 786440 | tf_op jit(solution)/shard_map/ppermute | solution.py:454
  54.5 1.3 %mix_features.7 = bf16[4,128,256]{2,1,0:T(8,128)(2,1)S(1)} custom-call(s32[5]{0:T(128)S(1)} %stack.23.plane_ref, f32[16,16]{1,0:T(8,128)S(1)} %convert_element_type.12.weight_ref, bf16[4,128,256]{2,1,0:T(8,128)(2,1)S(1)} %gate.3.refs_0_, bf16[4,128,256]{2,1,0:T(8,128)(2,1)S(1)} %collective-permute-done.18.refs_1_, ...), custom_call_target="tpu_custom_call" | custom-call | flops 3145728 | tf_op jit(solution)/shard_map/mix_features/pallas_call | solution.py:429
  55.7 1.3 %collective-permute-start.21 = (bf16[4,128,256]{2,1,0:T(8,128)(2,1)S(1)}, bf16[4,128,256]{2,1,0:T(8,128)(2,1)S(1)}, u32[]{:S(2)}, u32[]{:S(2)}) collective-permute-start(bf16[4,128,256]{2,1,0:T(8,128)(2,1)S(1)} %mix_features.7), channel_id=1, source_target_pairs={{2,3},{1,0},{6,7},{5,4},{10,11},{9,8},{14,15},{13,12},{18,19},{17,... | collective-permute-start | bytes 786440 | tf_op jit(solution)/shard_map/ppermute | solution.py:460
  57.0 1.1 %mix_features.4 = f32[4,128,256]{2,1,0:T(8,128)S(1)} custom-call(s32[5]{0:T(128)S(1)} %stack.23.plane_ref, f32[16,16]{1,0:T(8,128)S(1)} %convert_element_type.12.weight_ref, bf16[4,128,256]{2,1,0:T(8,128)(2,1)S(1)} %gate.2.refs_0_, bf16[4,128,256]{2,1,0:T(8,128)(2,1)S(1)} %collective-permute-done.15.refs_1_), custom_call_target="tpu_custom_call" | custom-call | flops 2097152 | tf_op jit(solution)/shard_map/mix_features/pallas_call | solution.py:429
  58.1 1.5 %mix_features.6.acc_ref = f32[4,128,256]{2,1,0:T(8,128)S(1)} custom-call(s32[5]{0:T(128)S(1)} %stack.23.plane_ref, f32[16,16]{1,0:T(8,128)S(1)} %convert_element_type.12.weight_ref, bf16[4,128,256]{2,1,0:T(8,128)(2,1)S(1)} %gate.3.refs_0_, bf16[4,128,256]{2,1,0:T(8,128)(2,1)S(1)} %collective-permute-done.18.refs_1_, ...), custom_call_target="tpu_custom_call" | custom-call | flops 4194304 | tf_op jit(solution)/shard_map/mix_features/pallas_call | solution.py:429
  59.6 4.9 %collective-permute-done.16 = bf16[4,128,256]{2,1,0:T(8,128)(2,1)S(1)} collective-permute-done((bf16[4,128,256]{2,1,0:T(8,128)(2,1)S(1)}, bf16[4,128,256]{2,1,0:T(8,128)(2,1)S(1)}, u32[]{:S(2)}, u32[]{:S(2)}) %collective-permute-start.16) | collective-permute-done | bytes 262176 | tf_op jit(solution)/shard_map/ppermute | solution.py:454
  64.6 3.9 %collective-permute-done.21.got_ref = bf16[4,128,256]{2,1,0:T(8,128)(2,1)S(1)} collective-permute-done((bf16[4,128,256]{2,1,0:T(8,128)(2,1)S(1)}, bf16[4,128,256]{2,1,0:T(8,128)(2,1)S(1)}, u32[]{:S(2)}, u32[]{:S(2)}) %collective-permute-start.21) | collective-permute-done | bytes 262176 | tf_op jit(solution)/shard_map/ppermute | solution.py:460
  68.4 1.0 %finish.1 = bf16[4,65536]{1,0:T(4,128)(2,1)} custom-call(bf16[4,128,256]{2,1,0:T(8,128)(2,1)S(1)} %add_convert_fusion.first_ref, f32[4,128,256]{2,1,0:T(8,128)S(1)} %mix_features.6.acc_ref, bf16[4,128,256]{2,1,0:T(8,128)(2,1)S(1)} %collective-permute-done.21.got_ref), custom_call_target="tpu_custom_call" | custom-call | flops 262144 | tf_op jit(solution)/shard_map/finish/pallas_call | solution.py:190
  (60 shorter events, 11.9 us)
Async XLA Ops:
  2.9 11.4 %collective-permute-start.4 = (bf16[2,128,512]{2,1,0:T(8,128)(2,1)}, bf16[2,128,512]{2,1,0:T(8,128)(2,1)S(1)}, u32[]{:S(2)}, u32[]{:S(2)}) collective-permute-start(bf16[2,128,512]{2,1,0:T(8,128)(2,1)} %get-tuple-element.51), channel_id=1, source_target_pairs={{0,24},{4,28},{8,16},{12,20},{16,8},{20,12},{24,0},{28,4},{1,25},{... | collective-permute-start | bytes 786440 | tf_op jit(solution)/shard_map/ppermute | solution.py:503
  6.9 12.9 %collective-permute-start.5 = (bf16[2,128,512]{2,1,0:T(8,128)(2,1)}, bf16[2,128,512]{2,1,0:T(8,128)(2,1)S(1)}, u32[]{:S(2)}, u32[]{:S(2)}) collective-permute-start(bf16[2,128,512]{2,1,0:T(8,128)(2,1)} %get-tuple-element.50.refs_0_), channel_id=1, source_target_pairs={{0,4},{4,0},{8,12},{12,8},{16,20},{20,16},{24,28},{28,24},{1,5},{5... | collective-permute-start | bytes 786440 | tf_op jit(solution)/shard_map/ppermute | solution.py:512
  6.9 12.4 %collective-permute-start = (bf16[2,128,512]{2,1,0:T(8,128)(2,1)}, bf16[2,128,512]{2,1,0:T(8,128)(2,1)S(1)}, u32[]{:S(2)}, u32[]{:S(2)}) collective-permute-start(bf16[2,128,512]{2,1,0:T(8,128)(2,1)} %get-tuple-element.48), channel_id=1, source_target_pairs={{0,8},{4,12},{8,0},{12,4},{16,24},{20,28},{24,16},{28,20},{1,9},{5... | collective-permute-start | bytes 786440 | tf_op jit(solution)/shard_map/ppermute | solution.py:503
  7.4 11.9 %collective-permute-start.1 = (bf16[2,128,512]{2,1,0:T(8,128)(2,1)}, bf16[2,128,512]{2,1,0:T(8,128)(2,1)S(1)}, u32[]{:S(2)}, u32[]{:S(2)}) collective-permute-start(bf16[2,128,512]{2,1,0:T(8,128)(2,1)} %get-tuple-element.49), channel_id=1, source_target_pairs={{0,16},{4,20},{8,24},{12,28},{16,0},{20,4},{24,8},{28,12},{1,17},{... | collective-permute-start | bytes 786440 | tf_op jit(solution)/shard_map/ppermute | solution.py:503
  10.1 9.7 %copy-start.1 = (bf16[2,128,512]{2,1,0:T(8,128)(2,1)S(1)}, bf16[2,128,512]{2,1,0:T(8,128)(2,1)}, u32[]{:S(2)}) copy-start(bf16[2,128,512]{2,1,0:T(8,128)(2,1)} %get-tuple-element.50.refs_0_) | copy-start | bytes 786436
  14.3 5.6 %collective-permute-start.6 = (bf16[2,128,512]{2,1,0:T(8,128)(2,1)S(1)}, bf16[2,128,512]{2,1,0:T(8,128)(2,1)S(1)}, u32[]{:S(2)}, u32[]{:S(2)}) collective-permute-start(bf16[2,128,512]{2,1,0:T(8,128)(2,1)S(1)} %collective-permute-done.4.refs_1_), channel_id=1, source_target_pairs={{0,4},{4,0},{8,12},{12,8},{16,20},{20,16},{24,28},{28,24},{1,5},{5... | collective-permute-start | bytes 786440 | tf_op jit(solution)/shard_map/ppermute | solution.py:512
  19.3 2.2 %collective-permute-start.2 = (bf16[2,128,512]{2,1,0:T(8,128)(2,1)S(1)}, bf16[2,128,512]{2,1,0:T(8,128)(2,1)S(1)}, u32[]{:S(2)}, u32[]{:S(2)}) collective-permute-start(bf16[2,128,512]{2,1,0:T(8,128)(2,1)S(1)} %collective-permute-done.refs_0_), channel_id=1, source_target_pairs={{0,4},{4,0},{8,12},{12,8},{16,20},{20,16},{24,28},{28,24},{1,5},{5... | collective-permute-start | bytes 786440 | tf_op jit(solution)/shard_map/ppermute | solution.py:512
  19.3 2.2 %collective-permute-start.3 = (bf16[2,128,512]{2,1,0:T(8,128)(2,1)S(1)}, bf16[2,128,512]{2,1,0:T(8,128)(2,1)S(1)}, u32[]{:S(2)}, u32[]{:S(2)}) collective-permute-start(bf16[2,128,512]{2,1,0:T(8,128)(2,1)S(1)} %collective-permute-done.1.refs_1_), channel_id=1, source_target_pairs={{0,4},{4,0},{8,12},{12,8},{16,20},{20,16},{24,28},{28,24},{1,5},{5... | collective-permute-start | bytes 786440 | tf_op jit(solution)/shard_map/ppermute | solution.py:512
  25.8 2.0 %collective-permute-start.11 = (bf16[1024,256]{1,0:T(8,128)(2,1)S(1)}, bf16[1024,256]{1,0:T(8,128)(2,1)S(1)}, u32[]{:S(2)}, u32[]{:S(2)}) collective-permute-start(bf16[1024,256]{1,0:T(8,128)(2,1)S(1)} %get-tuple-element.68.refs_0_), channel_id=1, source_target_pairs={{0,4},{4,0},{8,12},{12,8},{16,20},{20,16},{24,28},{28,24},{1,5},{5... | collective-permute-start | bytes 1572872 | tf_op jit(solution)/shard_map/ppermute | solution.py:512
  26.6 5.5 %collective-permute-start.7 = (bf16[1024,256]{1,0:T(8,128)(2,1)S(1)}, bf16[1024,256]{1,0:T(8,128)(2,1)S(1)}, u32[]{:S(2)}, u32[]{:S(2)}) collective-permute-start(bf16[1024,256]{1,0:T(8,128)(2,1)S(1)} %back_columns.1.refs_0_), channel_id=1, source_target_pairs={{0,4},{4,0},{8,12},{12,8},{16,20},{20,16},{24,28},{28,24},{1,5},{5... | collective-permute-start | bytes 1572872 | tf_op jit(solution)/shard_map/ppermute | solution.py:512
  28.5 6.9 %collective-permute-start.12 = (bf16[128,256]{1,0:T(8,128)(2,1)S(1)}, bf16[128,256]{1,0:T(8,128)(2,1)S(1)}, u32[]{:S(2)}, u32[]{:S(2)}) collective-permute-start(bf16[128,256]{1,0:T(8,128)(2,1)S(1)} %get-tuple-element.70), channel_id=1, source_target_pairs={{0,8},{4,12},{8,0},{12,4},{16,24},{20,28},{24,16},{28,20},{1,9},{5... | collective-permute-start | bytes 196616 | tf_op jit(solution)/shard_map/ppermute | solution.py:503
  30.1 6.3 %collective-permute-start.13 = (bf16[128,256]{1,0:T(8,128)(2,1)S(1)}, bf16[128,256]{1,0:T(8,128)(2,1)S(1)}, u32[]{:S(2)}, u32[]{:S(2)}) collective-permute-start(bf16[128,256]{1,0:T(8,128)(2,1)S(1)} %get-tuple-element.71), channel_id=1, source_target_pairs={{0,16},{4,20},{8,24},{12,28},{16,0},{20,4},{24,8},{28,12},{1,17},{... | collective-permute-start | bytes 196616 | tf_op jit(solution)/shard_map/ppermute | solution.py:503
  31.1 5.8 %collective-permute-start.14 = (bf16[128,256]{1,0:T(8,128)(2,1)S(1)}, bf16[128,256]{1,0:T(8,128)(2,1)S(1)}, u32[]{:S(2)}, u32[]{:S(2)}) collective-permute-start(bf16[128,256]{1,0:T(8,128)(2,1)S(1)} %get-tuple-element.72), channel_id=1, source_target_pairs={{0,24},{4,28},{8,16},{12,20},{16,8},{20,12},{24,0},{28,4},{1,25},{... | collective-permute-start | bytes 196616 | tf_op jit(solution)/shard_map/ppermute | solution.py:503
  32.8 5.6 %collective-permute-start.10 = (bf16[128,256]{1,0:T(8,128)(2,1)S(1)}, bf16[128,256]{1,0:T(8,128)(2,1)S(1)}, u32[]{:S(2)}, u32[]{:S(2)}) collective-permute-start(bf16[128,256]{1,0:T(8,128)(2,1)S(1)} %get-tuple-element.67), channel_id=1, source_target_pairs={{0,24},{4,28},{8,16},{12,20},{16,8},{20,12},{24,0},{28,4},{1,25},{... | collective-permute-start | bytes 196616 | tf_op jit(solution)/shard_map/ppermute | solution.py:503
  34.9 4.3 %collective-permute-start.8 = (bf16[128,256]{1,0:T(8,128)(2,1)S(1)}, bf16[128,256]{1,0:T(8,128)(2,1)S(1)}, u32[]{:S(2)}, u32[]{:S(2)}) collective-permute-start(bf16[128,256]{1,0:T(8,128)(2,1)S(1)} %get-tuple-element.65), channel_id=1, source_target_pairs={{0,8},{4,12},{8,0},{12,4},{16,24},{20,28},{24,16},{28,20},{1,9},{5... | collective-permute-start | bytes 196616 | tf_op jit(solution)/shard_map/ppermute | solution.py:503
  35.4 4.3 %collective-permute-start.9 = (bf16[128,256]{1,0:T(8,128)(2,1)S(1)}, bf16[128,256]{1,0:T(8,128)(2,1)S(1)}, u32[]{:S(2)}, u32[]{:S(2)}) collective-permute-start(bf16[128,256]{1,0:T(8,128)(2,1)S(1)} %get-tuple-element.66), channel_id=1, source_target_pairs={{0,16},{4,20},{8,24},{12,28},{16,0},{20,4},{24,8},{28,12},{1,17},{... | collective-permute-start | bytes 196616 | tf_op jit(solution)/shard_map/ppermute | solution.py:503
  36.9 9.7 %copy-start.9 = (bf16[16,16]{1,0:T(8,128)(2,1)S(1)}, bf16[16,16]{1,0:T(8,128)(2,1)}, u32[]{:S(2)}) copy-start(bf16[16,16]{1,0:T(8,128)(2,1)} %param.16) | copy-start | bytes 1540
  39.7 7.0 %collective-permute-start.15 = (bf16[4,128,256]{2,1,0:T(8,128)(2,1)S(1)}, bf16[4,128,256]{2,1,0:T(8,128)(2,1)S(1)}, u32[]{:S(2)}, u32[]{:S(2)}) collective-permute-start(bf16[4,128,256]{2,1,0:T(8,128)(2,1)S(1)} %gate.2.refs_0_), channel_id=1, source_target_pairs={{0,1},{1,0},{2,3},{3,2},{4,5},{5,4},{6,7},{7,6},{8,9},{9,8},{10,11... | collective-permute-start | bytes 786440 | tf_op jit(solution)/shard_map/ppermute | solution.py:452
  41.4 13.1 %collective-permute-start.18 = (bf16[4,128,256]{2,1,0:T(8,128)(2,1)S(1)}, bf16[4,128,256]{2,1,0:T(8,128)(2,1)S(1)}, u32[]{:S(2)}, u32[]{:S(2)}) collective-permute-start(bf16[4,128,256]{2,1,0:T(8,128)(2,1)S(1)} %gate.3.refs_0_), channel_id=1, source_target_pairs={{0,2},{3,1},{4,6},{7,5},{8,10},{11,9},{12,14},{15,13},{16,18},{19,... | collective-permute-start | bytes 786440 | tf_op jit(solution)/shard_map/ppermute | solution.py:450
  45.9 8.6 %collective-permute-start.19 = (bf16[4,128,256]{2,1,0:T(8,128)(2,1)S(1)}, bf16[4,128,256]{2,1,0:T(8,128)(2,1)S(1)}, u32[]{:S(2)}, u32[]{:S(2)}) collective-permute-start(bf16[4,128,256]{2,1,0:T(8,128)(2,1)S(1)} %gate.3.refs_0_), channel_id=1, source_target_pairs={{1,2},{2,1},{5,6},{6,5},{9,10},{10,9},{13,14},{14,13},{17,18},{18,... | collective-permute-start | bytes 786440 | tf_op jit(solution)/shard_map/ppermute | solution.py:451
  48.1 10.0 %collective-permute-start.20 = (bf16[4,128,256]{2,1,0:T(8,128)(2,1)S(1)}, bf16[4,128,256]{2,1,0:T(8,128)(2,1)S(1)}, u32[]{:S(2)}, u32[]{:S(2)}) collective-permute-start(bf16[4,128,256]{2,1,0:T(8,128)(2,1)S(1)} %gate.3.refs_0_), channel_id=1, source_target_pairs={{0,1},{3,2},{4,5},{7,6},{8,9},{11,10},{12,13},{15,14},{16,17},{19,... | collective-permute-start | bytes 786440 | tf_op jit(solution)/shard_map/ppermute | solution.py:457
  52.5 12.0 %collective-permute-start.16 = (bf16[4,128,256]{2,1,0:T(8,128)(2,1)S(1)}, bf16[4,128,256]{2,1,0:T(8,128)(2,1)S(1)}, u32[]{:S(2)}, u32[]{:S(2)}) collective-permute-start(bf16[4,128,256]{2,1,0:T(8,128)(2,1)S(1)} %get-tuple-element.80), channel_id=1, source_target_pairs={{1,3},{2,0},{5,7},{6,4},{9,11},{10,8},{13,15},{14,12},{17,19},{18,... | collective-permute-start | bytes 786440 | tf_op jit(solution)/shard_map/ppermute | solution.py:454
  53.8 10.7 %collective-permute-start.17 = (bf16[4,128,256]{2,1,0:T(8,128)(2,1)S(1)}, bf16[4,128,256]{2,1,0:T(8,128)(2,1)S(1)}, u32[]{:S(2)}, u32[]{:S(2)}) collective-permute-start(bf16[4,128,256]{2,1,0:T(8,128)(2,1)S(1)} %get-tuple-element.81), channel_id=1, source_target_pairs={{1,2},{2,1},{5,6},{6,5},{9,10},{10,9},{13,14},{14,13},{17,18},{18,... | collective-permute-start | bytes 786440 | tf_op jit(solution)/shard_map/ppermute | solution.py:455
  55.7 12.7 %collective-permute-start.21 = (bf16[4,128,256]{2,1,0:T(8,128)(2,1)S(1)}, bf16[4,128,256]{2,1,0:T(8,128)(2,1)S(1)}, u32[]{:S(2)}, u32[]{:S(2)}) collective-permute-start(bf16[4,128,256]{2,1,0:T(8,128)(2,1)S(1)} %mix_features.7), channel_id=1, source_target_pairs={{2,3},{1,0},{6,7},{5,4},{10,11},{9,8},{14,15},{13,12},{18,19},{17,... | collective-permute-start | bytes 786440 | tf_op jit(solution)/shard_map/ppermute | solution.py:460
  (8 other events, 36.5 us)

commit v9 on v8

--- a/solution.py
+++ b/solution.py
@@ -405,7 +405,7 @@
     count = len(slots)
     feats = refs[count].shape[0]
 
-    @pl.loop(0, refs[0].shape[1] // 16)
+    @pl.loop(0, refs[0].shape[1] // 16, unroll=True)
     def _(index):
         rows = pl.ds(pl.multiple_of(index * 16, 16), 16)
         sums = [[None] * feats for _ in outputs]

time: 69.7 us -> 69.7 us (level)
  no operation moved by 1% of the time
where the time goes in v9:
time: 69.7 us; the launch traced here: 69.4 us
  starting transfers between devices  27.3 us (39%)
  Pallas kernels  19.9 us (29%)
  waiting for transfers between devices  19.9 us (29%)
  local copies, waits for them, and re-layouts  1.91 us (3%)
    ppermute x9, starting transfers between devices, swap(): got.append(lax.ppermute(values[rel], 'ctx', pairs))  11.8 us
    ppermute x9, waiting for transfers between devices, swap(): got.append(lax.ppermute(values[rel], 'ctx', pairs))  10.2 us
    ppermute x1, waiting for transfers between devices, line_mix(): from_far = lax.ppermute(to_far, 'tp', [(1, 3), (2, 0)])  5.13 us
    pallas_call x4, Pallas kernels, run_mix(): pl.pallas_call(functools.partial(mix_kernel, chans, slots, outputs), out_...  4.91 us
    ppermute x1, starting transfers between devices, line_mix(): far = lax.ppermute(gathered, 'tp', [(0, 2), (3, 1)])  4.51 us
    ppermute x1, starting transfers between devices, line_mix(): edge = lax.ppermute(gathered, 'tp', [(0, 1), (3, 2)])  4.33 us
    pallas_call x1, Pallas kernels, run_spectrum(): pl.pallas_call(functools.partial(spectrum_kernel, scale), out_shape=(jax....  4.32 us
    ppermute x1, waiting for transfers between devices, line_mix(): from_edge = lax.ppermute(to_edge, 'tp', [(2, 3), (1, 0)])  3.91 us
  transfers between devices with their start and end apart: 22, of which 9 were waited for; matrix products, arithmetic and copies ran while one was open for 1% of the time, Pallas kernels for 17%

profile of v9, /device:TPU:0, one launch (start us, length us, event | category | flops | bytes accessed | tf_op | source)
XLA Modules:
  0.0 69.4 jit_solution(4130697879602910102)
XLA Ops:
  0.0 2.9 %prepare_blocks.1 = (bf16[2,128,512]{2,1,0:T(8,128)(2,1)}, bf16[2,128,512]{2,1,0:T(8,128)(2,1)}, bf16[2,128,512]{2,1,0:T(8,128)(2,1)}, bf16[2,128,512]{2,1,0:T(8,128)(2,1)}) custom-call(f32[4,65536]{1,0:T(4,128)} %refs_0_.2, bf16[4,65536]{1,0:T(4,128)(2,1)} %refs_1_.2, bf16[4,65536]{1,0:T(4,128)(2,1)} %refs_2_.2), custom_call_target="tpu_custom_call" | custom-call | flops 1048576 | tf_op jit(solution)/shard_map/prepare_blocks/pallas_call | solution.py:152
  2.9 4.0 %collective-permute-start.4 = (bf16[2,128,512]{2,1,0:T(8,128)(2,1)}, bf16[2,128,512]{2,1,0:T(8,128)(2,1)S(1)}, u32[]{:S(2)}, u32[]{:S(2)}) collective-permute-start(bf16[2,128,512]{2,1,0:T(8,128)(2,1)} %get-tuple-element.51), channel_id=1, source_target_pairs={{0,24},{4,28},{8,16},{12,20},{16,8},{20,12},{24,0},{28,4},{1,25},{... | collective-permute-start | bytes 786440 | tf_op jit(solution)/shard_map/ppermute | solution.py:503
  8.8 1.3 %copy-done.2 = bf16[2,1024,1024]{2,1,0:T(8,128)(2,1)S(1)} copy-done((bf16[2,1024,1024]{2,1,0:T(8,128)(2,1)S(1)}, bf16[2,1024,1024]{2,1,0:T(8,128)(2,1)}, u32[]{:S(2)}) %copy-start.2) | copy-done | bytes 4194328
  10.1 2.1 %load_tables.1 = (bf16[1024,1024]{1,0:T(8,128)(2,1)S(1)}, bf16[512,2048]{1,0:T(8,128)(2,1)S(1)}, bf16[1024,512]{1,0:T(8,128)(2,1)S(1)}, f32[2,512,512]{2,1,0:T(8,128)S(1)}) custom-call(bf16[2,1024,1024]{2,1,0:T(8,128)(2,1)S(1)} %copy-done.2, bf16[2,512,2048]{2,1,0:T(8,128)(2,1)} %constant.23.clone.refs_1_, bf16[1024,512]{1,0:T(8,128)(2,1)S(1)} %copy-done.3, ...), custom_call_target="tpu_custom_call" | custom-call | flops 3000000000 | tf_op jit(solution)/shard_map/load_tables/pallas_call | solution.py:97
  12.2 2.0 %collective-permute-done.4.refs_1_ = bf16[2,128,512]{2,1,0:T(8,128)(2,1)S(1)} collective-permute-done((bf16[2,128,512]{2,1,0:T(8,128)(2,1)}, bf16[2,128,512]{2,1,0:T(8,128)(2,1)S(1)}, u32[]{:S(2)}, u32[]{:S(2)}) %collective-permute-start.4) | collective-permute-done | bytes 262176 | tf_op jit(solution)/shard_map/ppermute | solution.py:503
  14.3 5.0 %collective-permute-done.refs_0_ = bf16[2,128,512]{2,1,0:T(8,128)(2,1)S(1)} collective-permute-done((bf16[2,128,512]{2,1,0:T(8,128)(2,1)}, bf16[2,128,512]{2,1,0:T(8,128)(2,1)S(1)}, u32[]{:S(2)}, u32[]{:S(2)}) %collective-permute-start) | collective-permute-done | bytes 262176 | tf_op jit(solution)/shard_map/ppermute | solution.py:503
  19.8 1.6 %early_stage.1 = (f32[2,1024,512]{2,1,0:T(8,128)S(1)}, bf16[1024,512]{1,0:T(8,128)(2,1)S(1)}) custom-call(bf16[2,128,512]{2,1,0:T(8,128)(2,1)S(1)} %copy-done.1, bf16[2,128,512]{2,1,0:T(8,128)(2,1)S(1)} %collective-permute-done.4.refs_1_, bf16[2,128,512]{2,1,0:T(8,128)(2,1)S(1)} %collective-permute-done.5.refs_2_, ...), custom_call_target="tpu_custom_call" | custom-call | flops 1073741824 | tf_op jit(solution)/shard_map/early_stage/pallas_call | solution.py:231
  21.5 4.3 %spectrum_product.1 = (bf16[512,1536]{1,0:T(8,128)(2,1)S(1)}, bf16[1024,256]{1,0:T(8,128)(2,1)S(1)}) custom-call(bf16[2,128,512]{2,1,0:T(8,128)(2,1)S(1)} %collective-permute-done.refs_0_, bf16[2,128,512]{2,1,0:T(8,128)(2,1)S(1)} %collective-permute-done.1.refs_1_, bf16[2,128,512]{2,1,0:T(8,128)(2,1)S(1)} %collective-permute-done.2.refs_2_, ...), custom_call_target="tpu_custom_call" | custom-call | flops 4294967296 | tf_op jit(solution)/shard_map/spectrum_product/pallas_call | solution.py:342
  28.5 1.6 %collective-permute-start.12 = (bf16[128,256]{1,0:T(8,128)(2,1)S(1)}, bf16[128,256]{1,0:T(8,128)(2,1)S(1)}, u32[]{:S(2)}, u32[]{:S(2)}) collective-permute-start(bf16[128,256]{1,0:T(8,128)(2,1)S(1)} %get-tuple-element.70), channel_id=1, source_target_pairs={{0,8},{4,12},{8,0},{12,4},{16,24},{20,28},{24,16},{28,20},{1,9},{5... | collective-permute-start | bytes 196616 | tf_op jit(solution)/shard_map/ppermute | solution.py:503
  30.1 1.0 %collective-permute-start.13 = (bf16[128,256]{1,0:T(8,128)(2,1)S(1)}, bf16[128,256]{1,0:T(8,128)(2,1)S(1)}, u32[]{:S(2)}, u32[]{:S(2)}) collective-permute-start(bf16[128,256]{1,0:T(8,128)(2,1)S(1)} %get-tuple-element.71), channel_id=1, source_target_pairs={{0,16},{4,20},{8,24},{12,28},{16,0},{20,4},{24,8},{28,12},{1,17},{... | collective-permute-start | bytes 196616 | tf_op jit(solution)/shard_map/ppermute | solution.py:503
  32.8 2.1 %collective-permute-start.10 = (bf16[128,256]{1,0:T(8,128)(2,1)S(1)}, bf16[128,256]{1,0:T(8,128)(2,1)S(1)}, u32[]{:S(2)}, u32[]{:S(2)}) collective-permute-start(bf16[128,256]{1,0:T(8,128)(2,1)S(1)} %get-tuple-element.67), channel_id=1, source_target_pairs={{0,24},{4,28},{8,16},{12,20},{16,8},{20,12},{24,0},{28,4},{1,25},{... | collective-permute-start | bytes 196616 | tf_op jit(solution)/shard_map/ppermute | solution.py:503
  37.1 1.4 %collective-permute-done.10.refs_3_ = bf16[128,256]{1,0:T(8,128)(2,1)S(1)} collective-permute-done((bf16[128,256]{1,0:T(8,128)(2,1)S(1)}, bf16[128,256]{1,0:T(8,128)(2,1)S(1)}, u32[]{:S(2)}, u32[]{:S(2)}) %collective-permute-start.10) | collective-permute-done | bytes 65568 | tf_op jit(solution)/shard_map/ppermute | solution.py:503
  39.7 1.6 %collective-permute-start.15 = (bf16[4,128,256]{2,1,0:T(8,128)(2,1)S(1)}, bf16[4,128,256]{2,1,0:T(8,128)(2,1)S(1)}, u32[]{:S(2)}, u32[]{:S(2)}) collective-permute-start(bf16[4,128,256]{2,1,0:T(8,128)(2,1)S(1)} %gate.2.refs_0_), channel_id=1, source_target_pairs={{0,1},{1,0},{2,3},{3,2},{4,5},{5,4},{6,7},{7,6},{8,9},{9,8},{10,11... | collective-permute-start | bytes 786440 | tf_op jit(solution)/shard_map/ppermute | solution.py:452
  41.4 4.5 %collective-permute-start.18 = (bf16[4,128,256]{2,1,0:T(8,128)(2,1)S(1)}, bf16[4,128,256]{2,1,0:T(8,128)(2,1)S(1)}, u32[]{:S(2)}, u32[]{:S(2)}) collective-permute-start(bf16[4,128,256]{2,1,0:T(8,128)(2,1)S(1)} %gate.3.refs_0_), channel_id=1, source_target_pairs={{0,2},{3,1},{4,6},{7,5},{8,10},{11,9},{12,14},{15,13},{16,18},{19,... | collective-permute-start | bytes 786440 | tf_op jit(solution)/shard_map/ppermute | solution.py:450
  46.7 1.3 %mix_features.5 = (bf16[4,128,256]{2,1,0:T(8,128)(2,1)S(1)}, bf16[4,128,256]{2,1,0:T(8,128)(2,1)S(1)}) custom-call(s32[5]{0:T(128)S(1)} %stack.23.plane_ref, f32[16,16]{1,0:T(8,128)S(1)} %convert_element_type.12.weight_ref, bf16[4,128,256]{2,1,0:T(8,128)(2,1)S(1)} %gate.2.refs_0_, bf16[4,128,256]{2,1,0:T(8,128)(2,1)S(1)} %collective-permute-done.15.refs_1_), custom_call_target="tpu_custom_call" | custom-call | flops 4194304 | tf_op jit(solution)/shard_map/mix_features/pallas_call | solution.py:429
  48.0 4.3 %collective-permute-start.20 = (bf16[4,128,256]{2,1,0:T(8,128)(2,1)S(1)}, bf16[4,128,256]{2,1,0:T(8,128)(2,1)S(1)}, u32[]{:S(2)}, u32[]{:S(2)}) collective-permute-start(bf16[4,128,256]{2,1,0:T(8,128)(2,1)S(1)} %gate.3.refs_0_), channel_id=1, source_target_pairs={{0,1},{3,2},{4,5},{7,6},{8,9},{11,10},{12,13},{15,14},{16,17},{19,... | collective-permute-start | bytes 786440 | tf_op jit(solution)/shard_map/ppermute | solution.py:457
  52.4 1.3 %collective-permute-start.16 = (bf16[4,128,256]{2,1,0:T(8,128)(2,1)S(1)}, bf16[4,128,256]{2,1,0:T(8,128)(2,1)S(1)}, u32[]{:S(2)}, u32[]{:S(2)}) collective-permute-start(bf16[4,128,256]{2,1,0:T(8,128)(2,1)S(1)} %get-tuple-element.80), channel_id=1, source_target_pairs={{1,3},{2,0},{5,7},{6,4},{9,11},{10,8},{13,15},{14,12},{17,19},{18,... | collective-permute-start | bytes 786440 | tf_op jit(solution)/shard_map/ppermute | solution.py:454
  54.4 1.2 %mix_features.7 = bf16[4,128,256]{2,1,0:T(8,128)(2,1)S(1)} custom-call(s32[5]{0:T(128)S(1)} %stack.23.plane_ref, f32[16,16]{1,0:T(8,128)S(1)} %convert_element_type.12.weight_ref, bf16[4,128,256]{2,1,0:T(8,128)(2,1)S(1)} %gate.3.refs_0_, bf16[4,128,256]{2,1,0:T(8,128)(2,1)S(1)} %collective-permute-done.18.refs_1_, ...), custom_call_target="tpu_custom_call" | custom-call | flops 3145728 | tf_op jit(solution)/shard_map/mix_features/pallas_call | solution.py:429
  55.6 1.3 %collective-permute-start.21 = (bf16[4,128,256]{2,1,0:T(8,128)(2,1)S(1)}, bf16[4,128,256]{2,1,0:T(8,128)(2,1)S(1)}, u32[]{:S(2)}, u32[]{:S(2)}) collective-permute-start(bf16[4,128,256]{2,1,0:T(8,128)(2,1)S(1)} %mix_features.7), channel_id=1, source_target_pairs={{2,3},{1,0},{6,7},{5,4},{10,11},{9,8},{14,15},{13,12},{18,19},{17,... | collective-permute-start | bytes 786440 | tf_op jit(solution)/shard_map/ppermute | solution.py:460
  56.9 1.0 %mix_features.4 = f32[4,128,256]{2,1,0:T(8,128)S(1)} custom-call(s32[5]{0:T(128)S(1)} %stack.23.plane_ref, f32[16,16]{1,0:T(8,128)S(1)} %convert_element_type.12.weight_ref, bf16[4,128,256]{2,1,0:T(8,128)(2,1)S(1)} %gate.2.refs_0_, bf16[4,128,256]{2,1,0:T(8,128)(2,1)S(1)} %collective-permute-done.15.refs_1_), custom_call_target="tpu_custom_call" | custom-call | flops 2097152 | tf_op jit(solution)/shard_map/mix_features/pallas_call | solution.py:429
  57.9 1.4 %mix_features.6.acc_ref = f32[4,128,256]{2,1,0:T(8,128)S(1)} custom-call(s32[5]{0:T(128)S(1)} %stack.23.plane_ref, f32[16,16]{1,0:T(8,128)S(1)} %convert_element_type.12.weight_ref, bf16[4,128,256]{2,1,0:T(8,128)(2,1)S(1)} %gate.3.refs_0_, bf16[4,128,256]{2,1,0:T(8,128)(2,1)S(1)} %collective-permute-done.18.refs_1_, ...), custom_call_target="tpu_custom_call" | custom-call | flops 4194304 | tf_op jit(solution)/shard_map/mix_features/pallas_call | solution.py:429
  59.3 5.1 %collective-permute-done.16 = bf16[4,128,256]{2,1,0:T(8,128)(2,1)S(1)} collective-permute-done((bf16[4,128,256]{2,1,0:T(8,128)(2,1)S(1)}, bf16[4,128,256]{2,1,0:T(8,128)(2,1)S(1)}, u32[]{:S(2)}, u32[]{:S(2)}) %collective-permute-start.16) | collective-permute-done | bytes 262176 | tf_op jit(solution)/shard_map/ppermute | solution.py:454
  64.5 3.9 %collective-permute-done.21.got_ref = bf16[4,128,256]{2,1,0:T(8,128)(2,1)S(1)} collective-permute-done((bf16[4,128,256]{2,1,0:T(8,128)(2,1)S(1)}, bf16[4,128,256]{2,1,0:T(8,128)(2,1)S(1)}, u32[]{:S(2)}, u32[]{:S(2)}) %collective-permute-start.21) | collective-permute-done | bytes 262176 | tf_op jit(solution)/shard_map/ppermute | solution.py:460
  68.4 1.0 %finish.1 = bf16[4,65536]{1,0:T(4,128)(2,1)} custom-call(bf16[4,128,256]{2,1,0:T(8,128)(2,1)S(1)} %add_convert_fusion.first_ref, f32[4,128,256]{2,1,0:T(8,128)S(1)} %mix_features.6.acc_ref, bf16[4,128,256]{2,1,0:T(8,128)(2,1)S(1)} %collective-permute-done.21.got_ref), custom_call_target="tpu_custom_call" | custom-call | flops 262144 | tf_op jit(solution)/shard_map/finish/pallas_call | solution.py:190
  (60 shorter events, 11.9 us)
Async XLA Ops:
  2.9 11.4 %collective-permute-start.4 = (bf16[2,128,512]{2,1,0:T(8,128)(2,1)}, bf16[2,128,512]{2,1,0:T(8,128)(2,1)S(1)}, u32[]{:S(2)}, u32[]{:S(2)}) collective-permute-start(bf16[2,128,512]{2,1,0:T(8,128)(2,1)} %get-tuple-element.51), channel_id=1, source_target_pairs={{0,24},{4,28},{8,16},{12,20},{16,8},{20,12},{24,0},{28,4},{1,25},{... | collective-permute-start | bytes 786440 | tf_op jit(solution)/shard_map/ppermute | solution.py:503
  6.9 12.9 %collective-permute-start.5 = (bf16[2,128,512]{2,1,0:T(8,128)(2,1)}, bf16[2,128,512]{2,1,0:T(8,128)(2,1)S(1)}, u32[]{:S(2)}, u32[]{:S(2)}) collective-permute-start(bf16[2,128,512]{2,1,0:T(8,128)(2,1)} %get-tuple-element.50.refs_0_), channel_id=1, source_target_pairs={{0,4},{4,0},{8,12},{12,8},{16,20},{20,16},{24,28},{28,24},{1,5},{5... | collective-permute-start | bytes 786440 | tf_op jit(solution)/shard_map/ppermute | solution.py:512
  6.9 12.4 %collective-permute-start = (bf16[2,128,512]{2,1,0:T(8,128)(2,1)}, bf16[2,128,512]{2,1,0:T(8,128)(2,1)S(1)}, u32[]{:S(2)}, u32[]{:S(2)}) collective-permute-start(bf16[2,128,512]{2,1,0:T(8,128)(2,1)} %get-tuple-element.48), channel_id=1, source_target_pairs={{0,8},{4,12},{8,0},{12,4},{16,24},{20,28},{24,16},{28,20},{1,9},{5... | collective-permute-start | bytes 786440 | tf_op jit(solution)/shard_map/ppermute | solution.py:503
  7.4 11.9 %collective-permute-start.1 = (bf16[2,128,512]{2,1,0:T(8,128)(2,1)}, bf16[2,128,512]{2,1,0:T(8,128)(2,1)S(1)}, u32[]{:S(2)}, u32[]{:S(2)}) collective-permute-start(bf16[2,128,512]{2,1,0:T(8,128)(2,1)} %get-tuple-element.49), channel_id=1, source_target_pairs={{0,16},{4,20},{8,24},{12,28},{16,0},{20,4},{24,8},{28,12},{1,17},{... | collective-permute-start | bytes 786440 | tf_op jit(solution)/shard_map/ppermute | solution.py:503
  10.1 9.7 %copy-start.1 = (bf16[2,128,512]{2,1,0:T(8,128)(2,1)S(1)}, bf16[2,128,512]{2,1,0:T(8,128)(2,1)}, u32[]{:S(2)}) copy-start(bf16[2,128,512]{2,1,0:T(8,128)(2,1)} %get-tuple-element.50.refs_0_) | copy-start | bytes 786436
  14.3 5.6 %collective-permute-start.6 = (bf16[2,128,512]{2,1,0:T(8,128)(2,1)S(1)}, bf16[2,128,512]{2,1,0:T(8,128)(2,1)S(1)}, u32[]{:S(2)}, u32[]{:S(2)}) collective-permute-start(bf16[2,128,512]{2,1,0:T(8,128)(2,1)S(1)} %collective-permute-done.4.refs_1_), channel_id=1, source_target_pairs={{0,4},{4,0},{8,12},{12,8},{16,20},{20,16},{24,28},{28,24},{1,5},{5... | collective-permute-start | bytes 786440 | tf_op jit(solution)/shard_map/ppermute | solution.py:512
  19.3 2.2 %collective-permute-start.2 = (bf16[2,128,512]{2,1,0:T(8,128)(2,1)S(1)}, bf16[2,128,512]{2,1,0:T(8,128)(2,1)S(1)}, u32[]{:S(2)}, u32[]{:S(2)}) collective-permute-start(bf16[2,128,512]{2,1,0:T(8,128)(2,1)S(1)} %collective-permute-done.refs_0_), channel_id=1, source_target_pairs={{0,4},{4,0},{8,12},{12,8},{16,20},{20,16},{24,28},{28,24},{1,5},{5... | collective-permute-start | bytes 786440 | tf_op jit(solution)/shard_map/ppermute | solution.py:512
  19.3 2.2 %collective-permute-start.3 = (bf16[2,128,512]{2,1,0:T(8,128)(2,1)S(1)}, bf16[2,128,512]{2,1,0:T(8,128)(2,1)S(1)}, u32[]{:S(2)}, u32[]{:S(2)}) collective-permute-start(bf16[2,128,512]{2,1,0:T(8,128)(2,1)S(1)} %collective-permute-done.1.refs_1_), channel_id=1, source_target_pairs={{0,4},{4,0},{8,12},{12,8},{16,20},{20,16},{24,28},{28,24},{1,5},{5... | collective-permute-start | bytes 786440 | tf_op jit(solution)/shard_map/ppermute | solution.py:512
  25.8 2.0 %collective-permute-start.11 = (bf16[1024,256]{1,0:T(8,128)(2,1)S(1)}, bf16[1024,256]{1,0:T(8,128)(2,1)S(1)}, u32[]{:S(2)}, u32[]{:S(2)}) collective-permute-start(bf16[1024,256]{1,0:T(8,128)(2,1)S(1)} %get-tuple-element.68.refs_0_), channel_id=1, source_target_pairs={{0,4},{4,0},{8,12},{12,8},{16,20},{20,16},{24,28},{28,24},{1,5},{5... | collective-permute-start | bytes 1572872 | tf_op jit(solution)/shard_map/ppermute | solution.py:512
  26.6 5.5 %collective-permute-start.7 = (bf16[1024,256]{1,0:T(8,128)(2,1)S(1)}, bf16[1024,256]{1,0:T(8,128)(2,1)S(1)}, u32[]{:S(2)}, u32[]{:S(2)}) collective-permute-start(bf16[1024,256]{1,0:T(8,128)(2,1)S(1)} %back_columns.1.refs_0_), channel_id=1, source_target_pairs={{0,4},{4,0},{8,12},{12,8},{16,20},{20,16},{24,28},{28,24},{1,5},{5... | collective-permute-start | bytes 1572872 | tf_op jit(solution)/shard_map/ppermute | solution.py:512
  28.5 6.9 %collective-permute-start.12 = (bf16[128,256]{1,0:T(8,128)(2,1)S(1)}, bf16[128,256]{1,0:T(8,128)(2,1)S(1)}, u32[]{:S(2)}, u32[]{:S(2)}) collective-permute-start(bf16[128,256]{1,0:T(8,128)(2,1)S(1)} %get-tuple-element.70), channel_id=1, source_target_pairs={{0,8},{4,12},{8,0},{12,4},{16,24},{20,28},{24,16},{28,20},{1,9},{5... | collective-permute-start | bytes 196616 | tf_op jit(solution)/shard_map/ppermute | solution.py:503
  30.1 6.3 %collective-permute-start.13 = (bf16[128,256]{1,0:T(8,128)(2,1)S(1)}, bf16[128,256]{1,0:T(8,128)(2,1)S(1)}, u32[]{:S(2)}, u32[]{:S(2)}) collective-permute-start(bf16[128,256]{1,0:T(8,128)(2,1)S(1)} %get-tuple-element.71), channel_id=1, source_target_pairs={{0,16},{4,20},{8,24},{12,28},{16,0},{20,4},{24,8},{28,12},{1,17},{... | collective-permute-start | bytes 196616 | tf_op jit(solution)/shard_map/ppermute | solution.py:503
  31.1 5.8 %collective-permute-start.14 = (bf16[128,256]{1,0:T(8,128)(2,1)S(1)}, bf16[128,256]{1,0:T(8,128)(2,1)S(1)}, u32[]{:S(2)}, u32[]{:S(2)}) collective-permute-start(bf16[128,256]{1,0:T(8,128)(2,1)S(1)} %get-tuple-element.72), channel_id=1, source_target_pairs={{0,24},{4,28},{8,16},{12,20},{16,8},{20,12},{24,0},{28,4},{1,25},{... | collective-permute-start | bytes 196616 | tf_op jit(solution)/shard_map/ppermute | solution.py:503
  32.8 5.6 %collective-permute-start.10 = (bf16[128,256]{1,0:T(8,128)(2,1)S(1)}, bf16[128,256]{1,0:T(8,128)(2,1)S(1)}, u32[]{:S(2)}, u32[]{:S(2)}) collective-permute-start(bf16[128,256]{1,0:T(8,128)(2,1)S(1)} %get-tuple-element.67), channel_id=1, source_target_pairs={{0,24},{4,28},{8,16},{12,20},{16,8},{20,12},{24,0},{28,4},{1,25},{... | collective-permute-start | bytes 196616 | tf_op jit(solution)/shard_map/ppermute | solution.py:503
  34.9 4.3 %collective-permute-start.8 = (bf16[128,256]{1,0:T(8,128)(2,1)S(1)}, bf16[128,256]{1,0:T(8,128)(2,1)S(1)}, u32[]{:S(2)}, u32[]{:S(2)}) collective-permute-start(bf16[128,256]{1,0:T(8,128)(2,1)S(1)} %get-tuple-element.65), channel_id=1, source_target_pairs={{0,8},{4,12},{8,0},{12,4},{16,24},{20,28},{24,16},{28,20},{1,9},{5... | collective-permute-start | bytes 196616 | tf_op jit(solution)/shard_map/ppermute | solution.py:503
  35.4 4.3 %collective-permute-start.9 = (bf16[128,256]{1,0:T(8,128)(2,1)S(1)}, bf16[128,256]{1,0:T(8,128)(2,1)S(1)}, u32[]{:S(2)}, u32[]{:S(2)}) collective-permute-start(bf16[128,256]{1,0:T(8,128)(2,1)S(1)} %get-tuple-element.66), channel_id=1, source_target_pairs={{0,16},{4,20},{8,24},{12,28},{16,0},{20,4},{24,8},{28,12},{1,17},{... | collective-permute-start | bytes 196616 | tf_op jit(solution)/shard_map/ppermute | solution.py:503
  36.9 9.7 %copy-start.9 = (bf16[16,16]{1,0:T(8,128)(2,1)S(1)}, bf16[16,16]{1,0:T(8,128)(2,1)}, u32[]{:S(2)}) copy-start(bf16[16,16]{1,0:T(8,128)(2,1)} %param.16) | copy-start | bytes 1540
  39.7 7.0 %collective-permute-start.15 = (bf16[4,128,256]{2,1,0:T(8,128)(2,1)S(1)}, bf16[4,128,256]{2,1,0:T(8,128)(2,1)S(1)}, u32[]{:S(2)}, u32[]{:S(2)}) collective-permute-start(bf16[4,128,256]{2,1,0:T(8,128)(2,1)S(1)} %gate.2.refs_0_), channel_id=1, source_target_pairs={{0,1},{1,0},{2,3},{3,2},{4,5},{5,4},{6,7},{7,6},{8,9},{9,8},{10,11... | collective-permute-start | bytes 786440 | tf_op jit(solution)/shard_map/ppermute | solution.py:452
  41.4 13.0 %collective-permute-start.18 = (bf16[4,128,256]{2,1,0:T(8,128)(2,1)S(1)}, bf16[4,128,256]{2,1,0:T(8,128)(2,1)S(1)}, u32[]{:S(2)}, u32[]{:S(2)}) collective-permute-start(bf16[4,128,256]{2,1,0:T(8,128)(2,1)S(1)} %gate.3.refs_0_), channel_id=1, source_target_pairs={{0,2},{3,1},{4,6},{7,5},{8,10},{11,9},{12,14},{15,13},{16,18},{19,... | collective-permute-start | bytes 786440 | tf_op jit(solution)/shard_map/ppermute | solution.py:450
  45.9 8.5 %collective-permute-start.19 = (bf16[4,128,256]{2,1,0:T(8,128)(2,1)S(1)}, bf16[4,128,256]{2,1,0:T(8,128)(2,1)S(1)}, u32[]{:S(2)}, u32[]{:S(2)}) collective-permute-start(bf16[4,128,256]{2,1,0:T(8,128)(2,1)S(1)} %gate.3.refs_0_), channel_id=1, source_target_pairs={{1,2},{2,1},{5,6},{6,5},{9,10},{10,9},{13,14},{14,13},{17,18},{18,... | collective-permute-start | bytes 786440 | tf_op jit(solution)/shard_map/ppermute | solution.py:451
  48.0 9.9 %collective-permute-start.20 = (bf16[4,128,256]{2,1,0:T(8,128)(2,1)S(1)}, bf16[4,128,256]{2,1,0:T(8,128)(2,1)S(1)}, u32[]{:S(2)}, u32[]{:S(2)}) collective-permute-start(bf16[4,128,256]{2,1,0:T(8,128)(2,1)S(1)} %gate.3.refs_0_), channel_id=1, source_target_pairs={{0,1},{3,2},{4,5},{7,6},{8,9},{11,10},{12,13},{15,14},{16,17},{19,... | collective-permute-start | bytes 786440 | tf_op jit(solution)/shard_map/ppermute | solution.py:457
  52.4 12.1 %collective-permute-start.16 = (bf16[4,128,256]{2,1,0:T(8,128)(2,1)S(1)}, bf16[4,128,256]{2,1,0:T(8,128)(2,1)S(1)}, u32[]{:S(2)}, u32[]{:S(2)}) collective-permute-start(bf16[4,128,256]{2,1,0:T(8,128)(2,1)S(1)} %get-tuple-element.80), channel_id=1, source_target_pairs={{1,3},{2,0},{5,7},{6,4},{9,11},{10,8},{13,15},{14,12},{17,19},{18,... | collective-permute-start | bytes 786440 | tf_op jit(solution)/shard_map/ppermute | solution.py:454
  53.7 10.8 %collective-permute-start.17 = (bf16[4,128,256]{2,1,0:T(8,128)(2,1)S(1)}, bf16[4,128,256]{2,1,0:T(8,128)(2,1)S(1)}, u32[]{:S(2)}, u32[]{:S(2)}) collective-permute-start(bf16[4,128,256]{2,1,0:T(8,128)(2,1)S(1)} %get-tuple-element.81), channel_id=1, source_target_pairs={{1,2},{2,1},{5,6},{6,5},{9,10},{10,9},{13,14},{14,13},{17,18},{18,... | collective-permute-start | bytes 786440 | tf_op jit(solution)/shard_map/ppermute | solution.py:455
  55.6 12.9 %collective-permute-start.21 = (bf16[4,128,256]{2,1,0:T(8,128)(2,1)S(1)}, bf16[4,128,256]{2,1,0:T(8,128)(2,1)S(1)}, u32[]{:S(2)}, u32[]{:S(2)}) collective-permute-start(bf16[4,128,256]{2,1,0:T(8,128)(2,1)S(1)} %mix_features.7), channel_id=1, source_target_pairs={{2,3},{1,0},{6,7},{5,4},{10,11},{9,8},{14,15},{13,12},{18,19},{17,... | collective-permute-start | bytes 786440 | tf_op jit(solution)/shard_map/ppermute | solution.py:460
  (8 other events, 36.5 us)
